TPU v7x, 256 devices: a whole 4x4x8 slice. The times are simulated.
256 devices in a mesh: seq: 64 (over y, z, core), grp: 4 (over x).
Axes of the slice: x: 4, y: 4, z: 8, core: 2. Of those that a mesh axis runs over, the one named last changes fastest.
Arguments:
- queries: bfloat16 [32768, 2048], P(('grp', 'seq')), may hold values from -6 to 6
- key_row_matrix: bfloat16 [32768, 2048], P(('grp', 'seq')), may hold values from -6 to 6
- value_row_matrix: bfloat16 [32768, 2048], P(('grp', 'seq')), may hold values from -6 to 6
- output_gradient: bfloat16 [32768, 2048], P(('grp', 'seq')), may hold values from -6 to 6
Outputs:
- query_gradient: bfloat16 [32768, 2048], P(('grp', 'seq'))
- key_gradient: bfloat16 [32768, 2048], P(('grp', 'seq'))
- value_gradient: bfloat16 [32768, 2048], P(('grp', 'seq'))
All inputs are finite; a program needn't handle non-finite values.
Results may differ from a plain program's by a relative error of at most 0.005.
Values sent between devices are 32-bit elements; how exact they have to be, the bound alone decides.
No kernel may reach another device: no remote copies, remote signals or barrier semaphores. Data moves between devices by JAX's collectives and lax.ppermute only.
A program may use at most 320 MiB of HBM per device.

v0:
```python
import jax
import jax.numpy as jnp
from jax import lax
from jax.sharding import PartitionSpec as P

HEAD = 128


def carried_in(part, axis, combine, identity, reverse):
    count = lax.axis_size(axis)
    place = lax.axis_index(axis)
    ahead = count - 1 - place if reverse else place
    gathered = lax.all_gather(part, axis)
    state = jnp.zeros_like(part) + jnp.asarray(identity, part.dtype)

    def one(step, state):
        source = count - 1 - step if reverse else step
        return combine(state, lax.dynamic_index_in_dim(gathered, source, 0, False))

    return lax.fori_loop(0, ahead, one, state)


def add_states(earlier, later):
    return jax.tree.map(jnp.add, earlier, later)


def block_grads(
    query_heads,
    key_heads,
    value_heads,
    gradient_heads,
    prefix_key_value,
    suffix_query_output,
    scale_factor,
):
    count = query_heads.shape[1]
    position = jnp.arange(count)
    causal = position[:, None] >= position[None, :]
    score_dv = jnp.einsum(
        "htd,hsd->hts", gradient_heads, value_heads, preferred_element_type=jnp.float32
    )
    weight_value_gradient = jnp.where(causal[None], scale_factor * score_dv, 0.0).astype(
        jnp.bfloat16
    )
    score_qk = jnp.einsum(
        "htd,hsd->hts", query_heads, key_heads, preferred_element_type=jnp.float32
    )
    weight_query_key = jnp.where(causal[None], scale_factor * score_qk, 0.0).astype(jnp.bfloat16)
    query_gradient = scale_factor * jnp.einsum(
        "htp,hap->hta", gradient_heads, prefix_key_value, preferred_element_type=jnp.float32
    )
    query_gradient = query_gradient + jnp.einsum(
        "hts,hsd->htd", weight_value_gradient, key_heads, preferred_element_type=jnp.float32
    )
    key_gradient = scale_factor * jnp.einsum(
        "hsr,hdr->hsd", value_heads, suffix_query_output, preferred_element_type=jnp.float32
    )
    key_gradient = key_gradient + jnp.einsum(
        "hts,htd->hsd", weight_value_gradient, query_heads, preferred_element_type=jnp.float32
    )
    value_gradient = scale_factor * jnp.einsum(
        "hsa,hal->hsl", key_heads, suffix_query_output, preferred_element_type=jnp.float32
    )
    value_gradient = value_gradient + jnp.einsum(
        "hts,htd->hsd", weight_query_key, gradient_heads, preferred_element_type=jnp.float32
    )
    return (
        query_gradient.astype(jnp.bfloat16),
        key_gradient.astype(jnp.bfloat16),
        value_gradient.astype(jnp.bfloat16),
    )


def per_device(queries, key_row_matrix, value_row_matrix, output_gradient):
    row_count = queries.shape[0]
    head_count = queries.shape[1] // HEAD
    shaped = (row_count, head_count, HEAD)

    def head_major(matrix):
        return jnp.transpose(matrix.reshape(shaped), (1, 0, 2))

    query_heads = head_major(queries)
    key_heads = head_major(key_row_matrix)
    value_heads = head_major(value_row_matrix)
    gradient_heads = head_major(output_gradient)
    total_tokens = row_count * lax.axis_size("seq") * lax.axis_size("grp")
    scale_factor = float(HEAD * total_tokens) ** (-0.5)
    local_kv = jnp.einsum(
        "htd,hte->hde", key_heads, value_heads, preferred_element_type=jnp.float32
    )
    local_qo = jnp.einsum(
        "htd,hte->hde", query_heads, gradient_heads, preferred_element_type=jnp.float32
    )
    empty = jnp.zeros_like(local_kv)
    group_kv, group_qo = lax.psum((local_kv, local_qo), "seq")
    inner_kv = carried_in(local_kv, "seq", add_states, empty, False)
    inner_qo = carried_in(local_qo, "seq", add_states, empty, True)
    outer_kv = carried_in(group_kv, "grp", add_states, empty, False)
    outer_qo = carried_in(group_qo, "grp", add_states, empty, True)
    prefix_key_value = (outer_kv + inner_kv).astype(jnp.bfloat16)
    suffix_query_output = (outer_qo + inner_qo).astype(jnp.bfloat16)
    query_gradient, key_gradient, value_gradient = block_grads(
        query_heads,
        key_heads,
        value_heads,
        gradient_heads,
        prefix_key_value,
        suffix_query_output,
        scale_factor,
    )
    flat = (row_count, head_count * HEAD)

    def token_major(heads_first):
        return jnp.transpose(heads_first, (1, 0, 2)).reshape(flat)

    return (token_major(query_gradient), token_major(key_gradient), token_major(value_gradient))


def solution(mesh):
    in_specs = (
        P(("grp", "seq"), None),
        P(("grp", "seq"), None),
        P(("grp", "seq"), None),
        P(("grp", "seq"), None),
    )
    out_specs = (P(("grp", "seq"), None), P(("grp", "seq"), None), P(("grp", "seq"), None))
    return jax.shard_map(
        per_device, mesh=mesh, in_specs=in_specs, out_specs=out_specs, check_vma=False
    )
```

profile of v0, /device:TPU:1, one launch (start us, length us, event | category | flops | bytes accessed | tf_op | source)
XLA Modules:
  0.0 804.7 jit_solution(8274977044380235738)
XLA Ops:
  14.0 237.4 %all-gather.11.cloned.1.call-done = f32[1024,128,128]{2,1,0:T(8,128)} async-done(((f32[16,128,128]{2,1,0:T(8,128)}), f32[1024,128,128]{2,1,0:T(8,128)}) %all-gather.11.cloned.1.call-update) | async-done | bytes 67108880 | tf_op jit(solution)/shard_map/all_gather | solution.py:13
  251.4 236.1 %all-gather.13.cloned.1.call-done = f32[1024,128,128]{2,1,0:T(8,128)} async-done(((f32[16,128,128]{2,1,0:T(8,128)}), f32[1024,128,128]{2,1,0:T(8,128)}) %all-gather.13.cloned.1.call-update) | async-done | bytes 67108880 | tf_op jit(solution)/shard_map/all_gather | solution.py:13
  488.3 187.9 %all-reduce.3.cloned.1.call-done = (f32[1,16,128,128]{3,2,1,0:T(8,128)}, f32[1,16,128,128]{3,2,1,0:T(8,128)}) async-done(((f32[1,16,128,128]{3,2,1,0:T(8,128)}, f32[1,16,128,128]{3,2,1,0:T(8,128)}), (f32[1,16,128,128]{3,2,1,0:T(8,128)}, f32[1,16,128,128]{3,2,1,0:T(8,128)})) %all-reduce.3.cloned.1.call-update) | async-done | bytes 2097168 | tf_op jit(solution)/shard_map/psum | solution.py:95
  678.2 1.5 while.45
  679.8 94.6 %while.47 = (s32[]{:T(128)}, f32[16,128,128]{2,1,0:T(8,128)S(1)}, s32[]{:T(128)}, f32[64,16,128,128]{3,2,1,0:T(8,128)}, s32[]{:T(128)}, /*index=5*/s32[]{:T(128)}, s32[]{:T(128)}, s32[]{:T(128)}) while((s32[]{:T(128)}, f32[16,128,128]{2,1,0:T(8,128)S(1)}, s32[]{:T(128)}, f32[64,16,128,128]{3,2,1,0:T(8,128)}, s32[]{:T(128)}, ...), condition=%wide.region_9.10_spmd, body=%wide.region_8.9_spmd.sunk | while | flops 262150 | bytes 3145871 | solution.py:20
  688.9 1.6 bitcast_add_fusion.11
  690.5 1.6 bitcast_add_fusion.11
  692.2 1.6 bitcast_add_fusion.11
  698.3 1.5 bitcast_add_fusion.11
  701.4 1.5 bitcast_add_fusion.11
  704.4 1.5 bitcast_add_fusion.11
  707.4 1.5 bitcast_add_fusion.11
  715.1 1.5 bitcast_add_fusion.11
  718.1 1.5 bitcast_add_fusion.11
  742.3 1.6 bitcast_add_fusion.11
  743.9 1.6 bitcast_add_fusion.11
  745.5 1.6 bitcast_add_fusion.11
  751.6 1.5 bitcast_add_fusion.11
  754.7 1.5 bitcast_add_fusion.11
  757.7 1.5 bitcast_add_fusion.11
  762.3 1.5 bitcast_add_fusion.11
  765.3 1.5 bitcast_add_fusion.11
  768.4 1.5 bitcast_add_fusion.11
  771.4 1.5 bitcast_add_fusion.11
  775.6 8.0 while.46
  775.6 2.7 bitcast_add_fusion.10
  778.2 2.7 bitcast_add_fusion.10
  780.9 2.7 bitcast_add_fusion.10
  786.4 2.5 fusion.2
  789.3 1.7 fusion.10
  792.0 1.8 fusion.11
  794.9 2.2 fusion.12
  (80 shorter events, 82.5 us)
Async XLA Ops:
  7.2 1.3 copy-start
  7.2 244.2 %all-gather.11.cloned.1.call-start = ((), (), s32[]{:S(2)}) async-start(), calls=%async_computation.2 | async-start | bytes 68157440 | tf_op jit(solution)/shard_map/all_gather | solution.py:13
  8.4 1.4 copy-start.2
  9.8 477.7 %all-gather.13.cloned.1.call-start = ((), (), s32[]{:S(2)}) async-start(), calls=%async_computation.3 | async-start | bytes 68157440 | tf_op jit(solution)/shard_map/all_gather | solution.py:13
  12.5 665.6 %copy-start.1 = (bf16[128,2048]{0,1:T(8,128)(2,1)}, bf16[128,2048]{0,1:T(8,128)(2,1)S(1)}, u32[]{:S(2)}) copy-start(bf16[128,2048]{0,1:T(8,128)(2,1)S(1)} %copy.44) | copy-start | bytes 1572868
  487.5 188.6 %all-reduce.3.cloned.1.call-start = ((), (), s32[]{:S(2)}) async-start(), calls=%async_computation.4 | async-start | bytes 4194304 | tf_op jit(solution)/shard_map/psum | solution.py:95
  488.2 286.2 %all-gather.9.cloned.1.call-start = ((), (), s32[]{:S(2)}) async-start(), calls=%async_computation.1 | async-start | bytes 5242880 | tf_op jit(solution)/shard_map/all_gather | solution.py:13
  676.2 112.7 %all-gather.7.cloned.1.call-start = ((), (), s32[]{:S(2)}) async-start(), calls=%async_computation | async-start | bytes 5242880 | tf_op jit(solution)/shard_map/all_gather | solution.py:13
Sparse Core Ops, SparseCore 0:
  10.8 240.5 all-gather.10
  254.2 233.2 all-gather.12
  491.9 184.2 all-reduce.2
  677.8 51.1 all-gather.8
  730.7 51.1 all-gather.6
where the time goes:
time: 808 us; the launch traced here: 805 us
  waiting for transfers between devices  663 us (82%)
  other arithmetic  104 us (13%)
  matrix products  14.2 us (2%)
  between operations  13.9 us (2%)
  local copies, waits for them, and re-layouts  8.25 us (1%)
    all_gather x4, waiting for transfers between devices, carried_in(): gathered = lax.all_gather(part, axis)  474 us
    psum x1, waiting for transfers between devices, per_device(): group_kv, group_qo = lax.psum((local_kv, local_qo), 'seq')  188 us
    add x66, other arithmetic, add_states(): return jax.tree.map(jnp.add, earlier, later)  103 us
  transfers between devices with their start and end apart: 5, of which 3 were waited for; matrix products, arithmetic and copies ran while one was open for 14% of the time, Pallas kernels for 0%

commit v1 on v0

v1 whole, which is shorter than its diff:
```python
import functools

import jax
import jax.numpy as jnp
from jax import lax
from jax.experimental import pallas as pl
from jax.experimental.pallas import tpu as pltpu
from jax.sharding import Mesh
from jax.sharding import PartitionSpec as P

HEAD = 128
HEADS_PER_STEP = 4
CHIP_AXES = ("x", "y", "z")
ROWS = ("x", "y", "z", "c")
FLAG = pl.BlockSpec(memory_space=pltpu.SMEM)
VMEM_LIMIT = 24 * 1024 * 1024


def tokens_spec(count):
    return pl.BlockSpec((count, HEADS_PER_STEP * HEAD), lambda i: (0, i))


def states_spec():
    return pl.BlockSpec((HEADS_PER_STEP * HEAD, HEAD), lambda i: (i, 0))


def contract(lhs, rhs, lhs_dim, rhs_dim):
    return lax.dot_general(
        lhs, rhs, (((lhs_dim,), (rhs_dim,)), ((), ())), preferred_element_type=jnp.float32
    )


def states_kernel(core, query, key, value, gradient, keep, send):
    first = core[0] == 0
    for h in range(HEADS_PER_STEP):
        lanes = pl.ds(h * HEAD, HEAD)
        kv = contract(key[:, lanes], value[:, lanes], 0, 0)
        qo = contract(query[:, lanes], gradient[:, lanes], 0, 0)
        keep[lanes, :] = jnp.where(first, kv, qo)
        send[lanes, :] = jnp.where(first, qo, kv)


def weights_kernel(query, key, value, gradient, weight_dv, weight_qk):
    count = query.shape[0]
    causal = lax.broadcasted_iota(jnp.int32, (count, count), 0) >= lax.broadcasted_iota(
        jnp.int32, (count, count), 1
    )
    for h in range(HEADS_PER_STEP):
        lanes = pl.ds(h * HEAD, HEAD)
        dv = contract(gradient[:, lanes], value[:, lanes], 1, 1)
        qk = contract(query[:, lanes], key[:, lanes], 1, 1)
        weight_dv[:, lanes] = jnp.where(causal, dv, 0.0).astype(jnp.bfloat16)
        weight_qk[:, lanes] = jnp.where(causal, qk, 0.0).astype(jnp.bfloat16)


def scan_kernel(core, parts, out):
    count = parts.shape[0]
    reverse = core[0] == 1

    def step(i, total):
        place = jnp.where(reverse, count - 1 - i, i)
        out[place] = total
        return total + parts[place]

    lax.fori_loop(0, count, step, jnp.zeros(parts.shape[1:], jnp.float32), unroll=8)


def outputs_kernel(
    scale, core, query, key, value, gradient, weight_dv, weight_qk, own, recv, other, gq, gk, gv
):
    first = core[0] == 0
    for h in range(HEADS_PER_STEP):
        lanes = pl.ds(h * HEAD, HEAD)
        mine = own[lanes, :]
        theirs = recv[lanes, :] + other[lanes, :]
        prefix = jnp.where(first, mine, theirs).astype(jnp.bfloat16)
        suffix = jnp.where(first, theirs, mine).astype(jnp.bfloat16)
        q, k, v, g = query[:, lanes], key[:, lanes], value[:, lanes], gradient[:, lanes]
        dv, qk = weight_dv[:, lanes], weight_qk[:, lanes]
        gq[:, lanes] = (scale * (contract(g, prefix, 1, 1) + contract(dv, k, 1, 0))).astype(
            jnp.bfloat16
        )
        gk[:, lanes] = (scale * (contract(v, suffix, 1, 1) + contract(dv, q, 0, 0))).astype(
            jnp.bfloat16
        )
        gv[:, lanes] = (scale * (contract(k, suffix, 1, 0) + contract(qk, g, 0, 0))).astype(
            jnp.bfloat16
        )


def call(kernel, in_specs, out_specs, out_shape, grid, flops, moved):
    return pl.pallas_call(
        kernel,
        in_specs=in_specs,
        out_specs=out_specs,
        out_shape=out_shape,
        grid=grid,
        cost_estimate=pl.CostEstimate(flops=flops, bytes_accessed=moved, transcendentals=0),
        compiler_params=pltpu.CompilerParams(vmem_limit_bytes=VMEM_LIMIT),
    )


def per_device(chips, scale, queries, key_row_matrix, value_row_matrix, output_gradient):
    tokens, width = queries.shape
    heads = width // HEAD
    grid = (heads // HEADS_PER_STEP,)
    core = lax.axis_index("c").astype(jnp.int32).reshape(1)
    swap = [(0, 1), (1, 0)]
    product = 2 * heads * tokens * HEAD * HEAD
    token_bytes = 2 * tokens * width
    state_shape = jax.ShapeDtypeStruct((width, HEAD), jnp.float32)
    token_shape = jax.ShapeDtypeStruct((tokens, width), jnp.bfloat16)
    inputs = (queries, key_row_matrix, value_row_matrix, output_gradient)
    token = tokens_spec(tokens)
    state = states_spec()

    keep, send = call(
        states_kernel,
        [FLAG] + [token] * 4,
        [state] * 2,
        [state_shape] * 2,
        grid,
        2 * product,
        4 * token_bytes + 8 * width * HEAD,
    )(core, *inputs)
    recv = lax.ppermute(send, "c", swap)
    weight_dv, weight_qk = call(
        weights_kernel,
        [token] * 4,
        [token] * 2,
        [token_shape] * 2,
        grid,
        2 * product,
        6 * token_bytes,
    )(*inputs)
    other = lax.ppermute(keep, "c", swap)
    chip_state = (keep + recv).reshape(chips, width // chips, HEAD)
    parts = lax.all_to_all(chip_state, CHIP_AXES, 0, 0, tiled=True)
    scanned = call(
        scan_kernel,
        [FLAG, pl.BlockSpec(memory_space=pltpu.VMEM)],
        pl.BlockSpec(memory_space=pltpu.VMEM),
        jax.ShapeDtypeStruct(parts.shape, jnp.float32),
        (),
        width * HEAD,
        8 * width * HEAD,
    )(core, parts)
    own = lax.all_to_all(scanned, CHIP_AXES, 0, 0, tiled=True).reshape(width, HEAD)
    theirs = lax.ppermute(own, "c", swap)
    return call(
        functools.partial(outputs_kernel, scale),
        [FLAG] + [token] * 6 + [state] * 3,
        [token] * 3,
        [token_shape] * 3,
        grid,
        6 * product,
        9 * token_bytes + 12 * width * HEAD,
    )(core, *inputs, weight_dv, weight_qk, own, theirs, other)


def solution(mesh):
    fine = Mesh(mesh.devices.reshape(4, 8, 2, 4), ("y", "z", "c", "x"))
    chips = mesh.devices.size // 2

    def program(queries, key_row_matrix, value_row_matrix, output_gradient):
        scale = float(HEAD * queries.shape[0]) ** -0.5
        spec = P(ROWS, None)
        return jax.shard_map(
            functools.partial(per_device, chips, scale),
            mesh=fine,
            in_specs=(spec,) * 4,
            out_specs=(spec,) * 3,
            check_vma=False,
        )(queries, key_row_matrix, value_row_matrix, output_gradient)

    return program
```

time: 808 us -> 104 us (0.13)
  waiting for transfers between devices: 663 us -> 29.8 us
  other arithmetic: 104 us -> 0.11 us
  blocking collectives: 0 us -> 44.3 us
  starting transfers between devices: 0.16 us -> 15.8 us
  matrix products: 14.2 us -> 0 us
  between operations: 13.9 us -> 0.73 us
    all_gather x4 -> x0, waiting for transfers between devices: 474 us -> none  [carried_in(): gathered = lax.all_gather(part, axis)]
    psum x1 -> x0, waiting for transfers between devices: 188 us -> none  [per_device(): group_kv, group_qo = lax.psum((local_kv, local_qo), 'seq')]
    add x66 -> x1, other arithmetic: 103 us -> 0.11 us  [per_device(): chip_state = (keep + recv).reshape(chips, width // chips, HEAD)]
    all_to_all x0 -> x1, blocking collectives: none -> 44.3 us  [per_device(): parts = lax.all_to_all(chip_state, CHIP_AXES, 0, 0, tiled=True)]
    all_to_all x0 -> x1, waiting for transfers between devices: none -> 26.8 us  [per_device(): lax.all_to_all(scanned, CHIP_AXES, 0, 0, tiled=True).reshape(width, HEAD)]
    dot_general x9 -> x0, matrix products: 14.2 us -> none  [the longest x1 2.54 us: block_grads(): jnp.einsum('hsa,hal->hsl', key_heads, suffix_query_output, preferred_elem...]
    ppermute x0 -> x3, starting transfers between devices: none -> 9.42 us  [the longest x1 3.83 us: per_device(): theirs = lax.ppermute(own, 'c', swap)]
  transfers between devices with their start and end apart: 5 -> 4, of which waited for: 3 -> 3; matrix products, arithmetic and copies ran while one was open for 14% -> 0% of each run, Pallas kernels for 0% -> 1%
where the time goes in v1:
time: 104 us; the launch traced here: 103 us
  blocking collectives  44.3 us (43%)
  waiting for transfers between devices  29.8 us (29%)
  starting transfers between devices  15.8 us (15%)
  Pallas kernels  7.52 us (7%)
  local copies, waits for them, and re-layouts  5.14 us (5%)
    all_to_all x1, blocking collectives, per_device(): parts = lax.all_to_all(chip_state, CHIP_AXES, 0, 0, tiled=True)  44.3 us
    all_to_all x1, waiting for transfers between devices, per_device(): lax.all_to_all(scanned, CHIP_AXES, 0, 0, tiled=True).reshape(width, HEAD)  26.8 us
    all_to_all x1, starting transfers between devices, per_device(): lax.all_to_all(scanned, CHIP_AXES, 0, 0, tiled=True).reshape(width, HEAD)  6.33 us
    unnamed x20, local copies, waits for them, and re-layouts  5.14 us
    pallas_call x1, Pallas kernels, per_device(): call(functools.partial(outputs_kernel, scale), [FLAG] + [token] * 6 + [st...  4.47 us
    ppermute x1, starting transfers between devices, per_device(): theirs = lax.ppermute(own, 'c', swap)  3.83 us
    ppermute x1, starting transfers between devices, per_device(): recv = lax.ppermute(send, 'c', swap)  3.33 us
    ppermute x1, waiting for transfers between devices, per_device(): recv = lax.ppermute(send, 'c', swap)  2.29 us
  transfers between devices with their start and end apart: 4, of which 3 were waited for; matrix products, arithmetic and copies ran while one was open for 0% of the time, Pallas kernels for 1%

profile of v1, /device:TPU:1, one launch (start us, length us, event | category | flops | bytes accessed | tf_op | source)
XLA Modules:
  0.0 103.3 jit_solution(1138373793558079815)
XLA Ops:
  0.6 0.0 copy-start
  0.6 1.0 copy-done
  1.7 1.0 %copy-done.2 = bf16[128,2048]{1,0:T(8,128)(2,1)S(1)} copy-done((bf16[128,2048]{1,0:T(8,128)(2,1)S(1)}, bf16[128,2048]{1,0:T(8,128)(2,1)}, u32[]{:S(2)}) %copy-start.2) | copy-done | bytes 524312
  2.7 0.0 copy-start.4
  2.7 1.0 %copy-done.4 = bf16[128,2048]{1,0:T(8,128)(2,1)S(1)} copy-done((bf16[128,2048]{1,0:T(8,128)(2,1)S(1)}, bf16[128,2048]{1,0:T(8,128)(2,1)}, u32[]{:S(2)}) %copy-start.4) | copy-done | bytes 524312
  3.8 0.0 copy-start.6
  3.8 1.0 %copy-done.6 = bf16[128,2048]{1,0:T(8,128)(2,1)S(1)} copy-done((bf16[128,2048]{1,0:T(8,128)(2,1)S(1)}, bf16[128,2048]{1,0:T(8,128)(2,1)}, u32[]{:S(2)}) %copy-start.6) | copy-done | bytes 524312
  4.8 1.3 %shard_map.68 = (f32[2048,128]{1,0:T(8,128)S(1)}, f32[2048,128]{1,0:T(8,128)S(1)}) custom-call(s32[1]{0:T(128)} %bitcast.core, bf16[128,2048]{1,0:T(8,128)(2,1)S(1)} %copy-done, bf16[128,2048]{1,0:T(8,128)(2,1)S(1)} %copy-done.2, bf16[128,2048]{1,0:T(8,128)(2,1)S(1)} %copy-done.4, bf16[128,2048]{1,0:T(8,128)(2,1)S(1)} %copy-done.6), custom_call_target="tpu_custom_call" | custom-call | flops 134217728 | bytes 4194304 | tf_op jit(solution)/shard_map/pallas_call | solution.py:117
  6.1 0.0 copy-start.9
  6.1 3.3 %collective-permute-start = (f32[2048,128]{1,0:T(8,128)S(1)}, f32[2048,128]{1,0:T(8,128)S(1)}, u32[]{:S(2)}, u32[]{:S(2)}) collective-permute-start(f32[2048,128]{1,0:T(8,128)S(1)} %get-tuple-element.10), channel_id=1, source_target_pairs={{0,4},{4,0},{1,5},{5,1},{2,6},{6,2},{3,7},{7,3},{8,12},{12,8},{9,1... | collective-permute-start | bytes 3145736 | tf_op jit(solution)/shard_map/ppermute | solution.py:126
  9.4 2.3 %collective-permute-done = f32[2048,128]{1,0:T(8,128)S(1)} collective-permute-done((f32[2048,128]{1,0:T(8,128)S(1)}, f32[2048,128]{1,0:T(8,128)S(1)}, u32[]{:S(2)}, u32[]{:S(2)}) %collective-permute-start) | collective-permute-done | bytes 1048608 | tf_op jit(solution)/shard_map/ppermute | solution.py:126
  11.7 0.1 add.3
  11.8 0.0 copy-done.9
  11.8 44.3 %all_to_all.10.parts = f32[128,16,128]{2,1,0:T(8,128)S(1)} all-to-all(f32[128,16,128]{2,1,0:T(8,128)S(1)} %bitcast.5), channel_id=1, replica_groups=mesh['y'=4,'z'=8,'c'=2,'x'=4] {'x','y','z'}, dimensions={0} | all-to-all | bytes 2097152 | tf_op jit(solution)/shard_map/all_to_all | solution.py:138
  56.1 0.3 shard_map.69
  56.4 0.0 copy-start.8
  56.4 1.0 copy-done.8
  57.3 0.0 copy-start.1
  57.3 0.0 copy-start.3
  57.3 0.0 copy-start.5
  57.3 6.3 %all-to-all-start.1 = ((f32[128,16,128]{2,1,0:T(8,128)}), f32[128,16,128]{2,1,0:T(8,128)S(1)}, u32[]{:S(2)}, u32[]{:S(2)}) async-start(f32[128,16,128]{2,1,0:T(8,128)} %copy-done.8), calls=%async_computation.1 | async-start | bytes 2097152 | tf_op jit(solution)/shard_map/all_to_all | solution.py:148
  63.7 2.3 %collective-permute-start.2 = (f32[2048,128]{1,0:T(8,128)}, f32[2048,128]{1,0:T(8,128)}, u32[]{:S(2)}, u32[]{:S(2)}) collective-permute-start(f32[2048,128]{1,0:T(8,128)} %copy-done.9), channel_id=1, source_target_pairs={{0,4},{4,0},{1,5},{5,1},{2,6},{6,2},{3,7},{7,3},{8,12},{12,8},{9,1... | collective-permute-start | bytes 3145736 | tf_op jit(solution)/shard_map/ppermute | solution.py:136
  65.9 26.8 %all-to-all-done.1 = f32[128,16,128]{2,1,0:T(8,128)S(1)} async-done(((f32[128,16,128]{2,1,0:T(8,128)}), f32[128,16,128]{2,1,0:T(8,128)S(1)}, u32[]{:S(2)}, u32[]{:S(2)}) %all-to-all-start.1) | async-done | bytes 1048608 | tf_op jit(solution)/shard_map/all_to_all | solution.py:148
  92.7 3.8 %collective-permute-start.1 = (f32[2048,128]{1,0:T(8,128)S(1)}, f32[2048,128]{1,0:T(8,128)S(1)}, u32[]{:S(2)}, u32[]{:S(2)}) collective-permute-start(f32[2048,128]{1,0:T(8,128)S(1)} %bitcast.3), channel_id=1, source_target_pairs={{0,4},{4,0},{1,5},{5,1},{2,6},{6,2},{3,7},{7,3},{8,12},{12,8},{9,1... | collective-permute-start | bytes 3145736 | tf_op jit(solution)/shard_map/ppermute | solution.py:149
  96.6 0.0 copy-done.1
  96.6 0.0 copy-done.3
  96.6 0.0 copy-done.5
  96.6 0.0 copy-done.7
  96.6 1.5 %shard_map.67 = (bf16[128,2048]{1,0:T(8,128)(2,1)S(1)}, bf16[128,2048]{1,0:T(8,128)(2,1)S(1)}) custom-call(bf16[128,2048]{1,0:T(8,128)(2,1)S(1)} %copy-done.1, bf16[128,2048]{1,0:T(8,128)(2,1)S(1)} %copy-done.3, bf16[128,2048]{1,0:T(8,128)(2,1)S(1)} %copy-done.5, bf16[128,2048]{1,0:T(8,128)(2,1)S(1)} %copy-done.7), custom_call_target="tpu_custom_call" | custom-call | flops 134217728 | bytes 3145728 | tf_op jit(solution)/shard_map/pallas_call | solution.py:127
  98.1 0.0 collective-permute-done.2.other
  98.1 0.7 collective-permute-done.1.recv
  98.8 4.5 %shard_map.70 = (bf16[128,2048]{1,0:T(8,128)(2,1)}, bf16[128,2048]{1,0:T(8,128)(2,1)}, bf16[128,2048]{1,0:T(8,128)(2,1)}) custom-call(s32[1]{0:T(128)} %bitcast.core, bf16[128,2048]{1,0:T(8,128)(2,1)S(1)} %copy-done.1, bf16[128,2048]{1,0:T(8,128)(2,1)S(1)} %copy-done.3, bf16[128,2048]{1,0:T(8,128)(2,1)S(1)} %copy-done.5, bf16[128,2048]{1,0:T(8,128)(2,1)S(1)} %copy-done.7, ...), custom_call_target="tpu_custom_call" | custom-call | flops 402653184 | bytes 7864320 | tf_op jit(solution)/shard_map/pallas_call | solution.py:150
  (2 shorter events, 0.0 us)
Async XLA Ops:
  0.6 1.0 %copy-start = (bf16[128,2048]{1,0:T(8,128)(2,1)S(1)}, bf16[128,2048]{1,0:T(8,128)(2,1)}, u32[]{:S(2)}) copy-start(bf16[128,2048]{1,0:T(8,128)(2,1)} %query.5) | copy-start | bytes 1572868
  1.7 1.0 %copy-start.2 = (bf16[128,2048]{1,0:T(8,128)(2,1)S(1)}, bf16[128,2048]{1,0:T(8,128)(2,1)}, u32[]{:S(2)}) copy-start(bf16[128,2048]{1,0:T(8,128)(2,1)} %key.5) | copy-start | bytes 1572868
  2.7 1.0 %copy-start.4 = (bf16[128,2048]{1,0:T(8,128)(2,1)S(1)}, bf16[128,2048]{1,0:T(8,128)(2,1)}, u32[]{:S(2)}) copy-start(bf16[128,2048]{1,0:T(8,128)(2,1)} %value.5) | copy-start | bytes 1572868
  3.8 1.0 %copy-start.6 = (bf16[128,2048]{1,0:T(8,128)(2,1)S(1)}, bf16[128,2048]{1,0:T(8,128)(2,1)}, u32[]{:S(2)}) copy-start(bf16[128,2048]{1,0:T(8,128)(2,1)} %gradient.5) | copy-start | bytes 1572868
  6.1 5.7 %copy-start.9 = (f32[2048,128]{1,0:T(8,128)}, f32[2048,128]{1,0:T(8,128)S(1)}, u32[]{:S(2)}) copy-start(f32[2048,128]{1,0:T(8,128)S(1)} %get-tuple-element.9) | copy-start | bytes 3145732
  6.1 5.6 %collective-permute-start = (f32[2048,128]{1,0:T(8,128)S(1)}, f32[2048,128]{1,0:T(8,128)S(1)}, u32[]{:S(2)}, u32[]{:S(2)}) collective-permute-start(f32[2048,128]{1,0:T(8,128)S(1)} %get-tuple-element.10), channel_id=1, source_target_pairs={{0,4},{4,0},{1,5},{5,1},{2,6},{6,2},{3,7},{7,3},{8,12},{12,8},{9,1... | collective-permute-start | bytes 3145736 | tf_op jit(solution)/shard_map/ppermute | solution.py:126
  56.4 1.0 copy-start.8
  57.3 39.2 %copy-start.1 = (bf16[128,2048]{1,0:T(8,128)(2,1)S(1)}, bf16[128,2048]{1,0:T(8,128)(2,1)}, u32[]{:S(2)}) copy-start(bf16[128,2048]{1,0:T(8,128)(2,1)} %query.5) | copy-start | bytes 1572868
  57.3 39.2 %copy-start.3 = (bf16[128,2048]{1,0:T(8,128)(2,1)S(1)}, bf16[128,2048]{1,0:T(8,128)(2,1)}, u32[]{:S(2)}) copy-start(bf16[128,2048]{1,0:T(8,128)(2,1)} %key.5) | copy-start | bytes 1572868
  57.3 39.2 %copy-start.5 = (bf16[128,2048]{1,0:T(8,128)(2,1)S(1)}, bf16[128,2048]{1,0:T(8,128)(2,1)}, u32[]{:S(2)}) copy-start(bf16[128,2048]{1,0:T(8,128)(2,1)} %value.5) | copy-start | bytes 1572868
  57.3 39.2 %copy-start.7 = (bf16[128,2048]{1,0:T(8,128)(2,1)S(1)}, bf16[128,2048]{1,0:T(8,128)(2,1)}, u32[]{:S(2)}) copy-start(bf16[128,2048]{1,0:T(8,128)(2,1)} %gradient.5) | copy-start | bytes 1572868
  57.3 35.4 %all-to-all-start.1 = ((f32[128,16,128]{2,1,0:T(8,128)}), f32[128,16,128]{2,1,0:T(8,128)S(1)}, u32[]{:S(2)}, u32[]{:S(2)}) async-start(f32[128,16,128]{2,1,0:T(8,128)} %copy-done.8), calls=%async_computation.1 | async-start | bytes 2097152 | tf_op jit(solution)/shard_map/all_to_all | solution.py:148
  63.7 34.4 %collective-permute-start.2 = (f32[2048,128]{1,0:T(8,128)}, f32[2048,128]{1,0:T(8,128)}, u32[]{:S(2)}, u32[]{:S(2)}) collective-permute-start(f32[2048,128]{1,0:T(8,128)} %copy-done.9), channel_id=1, source_target_pairs={{0,4},{4,0},{1,5},{5,1},{2,6},{6,2},{3,7},{7,3},{8,12},{12,8},{9,1... | collective-permute-start | bytes 3145736 | tf_op jit(solution)/shard_map/ppermute | solution.py:136
  92.7 6.1 %collective-permute-start.1 = (f32[2048,128]{1,0:T(8,128)S(1)}, f32[2048,128]{1,0:T(8,128)S(1)}, u32[]{:S(2)}, u32[]{:S(2)}) collective-permute-start(f32[2048,128]{1,0:T(8,128)S(1)} %bitcast.3), channel_id=1, source_target_pairs={{0,4},{4,0},{1,5},{5,1},{2,6},{6,2},{3,7},{7,3},{8,12},{12,8},{9,1... | collective-permute-start | bytes 3145736 | tf_op jit(solution)/shard_map/ppermute | solution.py:149

commit v2 on v1

v2 whole, which is shorter than its diff:
```python
import functools

import jax
import jax.numpy as jnp
from jax import lax
from jax.experimental import pallas as pl
from jax.experimental.pallas import tpu as pltpu
from jax.sharding import Mesh
from jax.sharding import PartitionSpec as P

HEAD = 128
ROWS = ("x", "y", "z", "c")
SMEM = pl.BlockSpec(memory_space=pltpu.SMEM)
VMEM = pl.BlockSpec(memory_space=pltpu.VMEM)
HBM = pl.BlockSpec(memory_space=pltpu.HBM)
VMEM_LIMIT = 24 * 1024 * 1024
F32, BF16 = jnp.float32, jnp.bfloat16


def contract(lhs, rhs, lhs_dim, rhs_dim):
    return lax.dot_general(
        lhs, rhs, (((lhs_dim,), (rhs_dim,)), ((), ())), preferred_element_type=F32
    )


def chunk_lanes(index, width):
    return pl.ds(pl.multiple_of(index * width, width), width)


def states_kernel(places, query, key, value, gradient, keep, send, held, sems):
    first = places[0] == 0
    z = places[1]
    slots = keep.shape[0]
    width = keep.shape[1]
    copies = []
    for slot in range(slots):
        lanes = chunk_lanes(lax.rem(z + slot, slots), width)
        for n, source in enumerate((key, value, query, gradient)):
            copy = pltpu.make_async_copy(
                source.at[:, lanes], held.at[n, slot], sems.at[n, slot]
            )
            copy.start()
            copies.append(copy)
    for slot in range(slots):
        for copy in copies[4 * slot : 4 * slot + 4]:
            copy.wait()
        for h in range(width // HEAD):
            lanes = pl.ds(h * HEAD, HEAD)
            kv = contract(held[0, slot, :, lanes], held[1, slot, :, lanes], 0, 0)
            qo = contract(held[2, slot, :, lanes], held[3, slot, :, lanes], 0, 0)
            keep[slot, lanes, :] = jnp.where(first, kv, qo)
            send[slot, lanes, :] = jnp.where(first, qo, kv)


def weights_kernel(query, key, value, gradient, dv, dv_turned, qk_turned):
    count = query.shape[0]
    row = lax.broadcasted_iota(jnp.int32, (count, count), 0)
    column = lax.broadcasted_iota(jnp.int32, (count, count), 1)
    for h in range(query.shape[1] // HEAD):
        lanes = pl.ds(h * HEAD, HEAD)
        q, k, v, g = query[:, lanes], key[:, lanes], value[:, lanes], gradient[:, lanes]
        dv[:, lanes] = jnp.where(row >= column, contract(g, v, 1, 1), 0.0).astype(BF16)
        dv_turned[:, lanes] = jnp.where(row <= column, contract(v, g, 1, 1), 0.0).astype(BF16)
        qk_turned[:, lanes] = jnp.where(row <= column, contract(k, q, 1, 1), 0.0).astype(BF16)


def merge_kernel(keep, received, *outs):
    for slot, out in enumerate(outs):
        out[...] = keep[slot] + received[slot]


def scan_kernel(slots, places, *refs):
    sources, extras, outs, held = (
        refs[:slots],
        refs[slots:-slots - 1],
        refs[-slots - 1 : -1],
        refs[-1],
    )
    reverse = places[0] == 1
    z = places[1]
    for k in range(slots):
        held[lax.rem(z + slots - k, slots)] = sources[k][...]
    total = extras[0][...]
    for extra in extras[1:]:
        total = total + extra[...]
    for n in range(slots):
        place = jnp.where(reverse, slots - 1 - n, n)
        piece = held[place]
        held[place] = total
        total = total + piece
    for k in range(slots):
        outs[k][...] = held[lax.rem(z + k, slots)]


def outputs_kernel(slots, scale, places, *refs):
    query, key, value, gradient, dv, dv_turned, qk_turned, other = refs[:8]
    own = refs[8 : 8 + slots]
    received = refs[8 + slots : 8 + 2 * slots]
    outs = refs[8 + 2 * slots : 11 + 2 * slots]
    held, sems = refs[11 + 2 * slots :]
    first = places[0] == 0
    z = places[1]
    width = own[0].shape[0]
    copies = []
    for k in range(slots):
        chunk = lax.rem(z + slots - k, slots)
        for h in range(width // HEAD):
            rows = pl.ds(h * HEAD, HEAD)
            mine = own[k][rows, :]
            theirs = received[k][rows, :] + other[(slots - k) % slots, rows, :]
            prefix = jnp.where(first, mine, theirs).astype(BF16)
            suffix = jnp.where(first, theirs, mine).astype(BF16)
            lanes = chunk_lanes(chunk * (width // HEAD) + h, HEAD)
            q, kk, v, g = query[:, lanes], key[:, lanes], value[:, lanes], gradient[:, lanes]
            gq = contract(g, prefix, 1, 1) + contract(dv[:, lanes], kk, 1, 0)
            gk = contract(v, suffix, 1, 1) + contract(dv_turned[:, lanes], q, 1, 0)
            gv = contract(kk, suffix, 1, 0) + contract(qk_turned[:, lanes], g, 1, 0)
            for n, result in enumerate((gq, gk, gv)):
                held[n, k, :, rows] = (scale * result).astype(BF16)
        for n, out in enumerate(outs):
            copy = pltpu.make_async_copy(
                held.at[n, k], out.at[:, chunk_lanes(chunk, width)], sems.at[n, k]
            )
            copy.start()
            copies.append(copy)
    for copy in copies:
        copy.wait()


def call(kernel, in_specs, out_specs, out_shape, flops, moved, scratch=()):
    return pl.pallas_call(
        kernel,
        in_specs=in_specs,
        out_specs=out_specs,
        out_shape=out_shape,
        scratch_shapes=scratch,
        cost_estimate=pl.CostEstimate(flops=flops, bytes_accessed=moved, transcendentals=0),
        compiler_params=pltpu.CompilerParams(vmem_limit_bytes=VMEM_LIMIT),
    )


def turn(array, axis, count, step):
    return lax.ppermute(array, axis, [(i, (i + step) % count) for i in range(count)])


def onward(array, axis, count, step):
    pairs = [(i, i + step) for i in range(count - step)]
    pairs += [(count + i, count + i - step) for i in range(step, count)]
    return lax.ppermute(array, ("c", axis), pairs)


def issue_order(count):
    return sorted(range(1, count), key=lambda k: (-(2 * k == count), min(k, count - k)))


def per_device(sizes, scale, queries, key_row_matrix, value_row_matrix, output_gradient):
    tokens, width = queries.shape
    slots = sizes["z"]
    chunk = width // slots
    core = lax.axis_index("c").astype(jnp.int32)
    depth = lax.axis_index("z").astype(jnp.int32)
    row = lax.axis_index("y").astype(jnp.int32)
    places = jnp.stack([core, depth])
    swap = [(0, 1), (1, 0)]
    product = 2 * width * tokens * HEAD
    token_bytes = 2 * tokens * width
    state_bytes = 4 * width * HEAD
    token_shape = jax.ShapeDtypeStruct((tokens, width), BF16)
    state_shape = jax.ShapeDtypeStruct((slots, chunk, HEAD), F32)
    chunk_shape = jax.ShapeDtypeStruct((chunk, HEAD), F32)
    inputs = (queries, key_row_matrix, value_row_matrix, output_gradient)

    keep, send = call(
        states_kernel,
        [SMEM] + [HBM] * 4,
        [VMEM] * 2,
        [state_shape] * 2,
        2 * product,
        4 * token_bytes + 2 * state_bytes,
        [
            pltpu.VMEM((4, slots, tokens, chunk), BF16),
            pltpu.SemaphoreType.DMA((4, slots)),
        ],
    )(places, *(pltpu.with_memory_space_constraint(a, pltpu.HBM) for a in inputs))
    received = lax.ppermute(send, "c", swap)
    weights = call(
        weights_kernel,
        [VMEM] * 4,
        [VMEM] * 3,
        [token_shape] * 3,
        3 * product,
        7 * token_bytes,
    )(*inputs)
    pieces = call(
        merge_kernel,
        [VMEM] * 2,
        [VMEM] * slots,
        [chunk_shape] * slots,
        width * HEAD,
        3 * state_bytes,
    )(keep, received)
    other = lax.ppermute(keep, "c", swap)

    gathered = list(pieces)
    for k in issue_order(slots):
        gathered[k] = turn(pieces[k], "z", slots, k)
    gathered, weights = lax.optimization_barrier((gathered, weights))
    column = functools.reduce(jnp.add, gathered)
    rows = sizes["y"]
    around = [turn(column, "y", rows, k) for k in range(1, rows)]
    plane = functools.reduce(jnp.add, around, column)
    before = functools.reduce(
        jnp.add,
        [
            jnp.where((row >= k) == (core == 0), part, 0.0)
            for k, part in enumerate(around, 1)
        ],
    )
    planes = [onward(plane, "x", sizes["x"], k) for k in range(1, sizes["x"])]
    prefixes = call(
        functools.partial(scan_kernel, slots),
        [SMEM] + [VMEM] * (slots + 1 + len(planes)),
        [VMEM] * slots,
        [chunk_shape] * slots,
        2 * width * HEAD,
        3 * state_bytes,
        [pltpu.VMEM((slots, chunk, HEAD), F32)],
    )(places, *gathered, before, *planes)
    own = list(prefixes)
    for k in issue_order(slots):
        own[k] = turn(prefixes[k], "z", slots, k)
    theirs = [lax.ppermute(part, "c", swap) for part in own]
    return call(
        functools.partial(outputs_kernel, slots, scale),
        [SMEM] + [VMEM] * (8 + 2 * slots),
        [HBM] * 3,
        [token_shape] * 3,
        6 * product,
        10 * token_bytes + 3 * state_bytes,
        [
            pltpu.VMEM((3, slots, tokens, chunk), BF16),
            pltpu.SemaphoreType.DMA((3, slots)),
        ],
    )(places, *inputs, *weights, other, *own, *theirs)


def solution(mesh):
    sizes = {"y": 4, "z": 8, "c": 2, "x": 4}
    fine = Mesh(mesh.devices.reshape(tuple(sizes.values())), tuple(sizes))

    def program(queries, key_row_matrix, value_row_matrix, output_gradient):
        scale = float(HEAD * queries.shape[0]) ** -0.5
        spec = P(ROWS, None)
        return jax.shard_map(
            functools.partial(per_device, sizes, scale),
            mesh=fine,
            in_specs=(spec,) * 4,
            out_specs=(spec,) * 3,
            check_vma=False,
        )(queries, key_row_matrix, value_row_matrix, output_gradient)

    return program
```

time: 104 us -> 106 us (1.019)
  blocking collectives: 44.3 us -> 0 us
  starting transfers between devices: 15.8 us -> 55.3 us
  waiting for transfers between devices: 29.8 us -> 36.2 us
  local copies, waits for them, and re-layouts: 5.14 us -> 1.66 us
  Pallas kernels: 7.52 us -> 9.37 us
  other arithmetic: 0.11 us -> 1.94 us
    ppermute x2 -> x29, starting transfers between devices: 7.16 us -> 55.2 us  [the longest x17 31.4 us: turn(): lax.ppermute(array, axis, [(i, (i + step) % count) for i in range(count)])]
    all_to_all x1 -> x0, blocking collectives: 44.3 us -> none  [per_device(): parts = lax.all_to_all(chip_state, CHIP_AXES, 0, 0, tiled=True)]
    ppermute x2 -> x29, waiting for transfers between devices: 3.02 us -> 36.2 us  [the longest x17 28.2 us: turn(): lax.ppermute(array, axis, [(i, (i + step) % count) for i in range(count)])]
    all_to_all x1 -> x0, waiting for transfers between devices: 26.8 us -> none  [per_device(): lax.all_to_all(scanned, CHIP_AXES, 0, 0, tiled=True).reshape(width, HEAD)]
    all_to_all x1 -> x0, starting transfers between devices: 6.33 us -> none  [per_device(): lax.all_to_all(scanned, CHIP_AXES, 0, 0, tiled=True).reshape(width, HEAD)]
    unnamed x20 -> x40, local copies, waits for them, and re-layouts: 5.14 us -> 1.66 us
    ppermute x1, starting transfers between devices: 2.26 us -> 0.14 us  [per_device(): other = lax.ppermute(keep, 'c', swap)]
    pallas_call x4 -> x5, Pallas kernels: 7.52 us -> 9.37 us  [the longest x1 3.7 us: per_device(): call(functools.partial(outputs_kernel, slots, scale), [SMEM] + [VMEM] * (...]
  transfers between devices with their start and end apart: 4 -> 30, of which waited for: 3 -> 17; matrix products, arithmetic and copies ran while one was open for 0% -> 2% of each run, Pallas kernels for 1% -> 2%
where the time goes in v2:
time: 106 us
  starting transfers between devices  55.3 us (52%)
  waiting for transfers between devices  36.2 us (34%)
  Pallas kernels  9.37 us (9%)
  other arithmetic  1.94 us (2%)
  local copies, waits for them, and re-layouts  1.66 us (2%)
    ppermute x17, starting transfers between devices, turn(): lax.ppermute(array, axis, [(i, (i + step) % count) for i in range(count)])  31.4 us
    ppermute x17, waiting for transfers between devices, turn(): lax.ppermute(array, axis, [(i, (i + step) % count) for i in range(count)])  28.2 us
    ppermute x8, starting transfers between devices, per_device(): theirs = [lax.ppermute(part, 'c', swap) for part in own]  16.6 us
    ppermute x3, waiting for transfers between devices, onward(): return lax.ppermute(array, ('c', axis), pairs)  4.62 us
    ppermute x3, starting transfers between devices, onward(): return lax.ppermute(array, ('c', axis), pairs)  3.88 us
    pallas_call x1, Pallas kernels, per_device(): call(functools.partial(outputs_kernel, slots, scale), [SMEM] + [VMEM] * (...  3.7 us
    pallas_call x1, Pallas kernels, per_device(): call(states_kernel, [SMEM] + [HBM] * 4, [VMEM] * 2, [state_shape] * 2, 2...  3.52 us
    ppermute x1, starting transfers between devices, per_device(): received = lax.ppermute(send, 'c', swap)  3.33 us
  transfers between devices with their start and end apart: 30, of which 17 were waited for; matrix products, arithmetic and copies ran while one was open for 2% of the time, Pallas kernels for 2%

profile of v2, /device:TPU:1, one launch (start us, length us, event | category | flops | bytes accessed | tf_op | source)
XLA Modules:
  0.0 105.5 jit_solution(2256618140196060511)
XLA Ops:
  0.7 3.5 %shard_map.67 = (f32[8,256,128]{2,1,0:T(8,128)S(1)}, f32[8,256,128]{2,1,0:T(8,128)S(1)}) custom-call(s32[2]{0:T(128)S(1)} %pad_add_fusion.places, bf16[128,2048]{1,0:T(8,128)(2,1)} %refs_0_.1, bf16[128,2048]{1,0:T(8,128)(2,1)} %refs_1_.1, bf16[128,2048]{1,0:T(8,128)(2,1)} %refs_2_.1, bf16[128,2048]{1,0:T(8,128)(2,1)} %refs_3_.1), custom_call_target="tpu_custom_call" | custom-call | flops 134217728 | bytes 4194304 | tf_op jit(solution)/shard_map/pallas_call | solution.py:173
  4.2 3.3 %collective-permute-start = (f32[8,256,128]{2,1,0:T(8,128)S(1)}, f32[8,256,128]{2,1,0:T(8,128)S(1)}, u32[]{:S(2)}, u32[]{:S(2)}) collective-permute-start(f32[8,256,128]{2,1,0:T(8,128)S(1)} %get-tuple-element.36), channel_id=1, source_target_pairs={{0,4},{4,0},{1,5},{5,1},{2,6},{6,2},{3,7},{7,3},{8,12},{12,8},{9,1... | collective-permute-start | bytes 3145736 | tf_op jit(solution)/shard_map/ppermute | solution.py:185
  7.7 2.1 %collective-permute-done.received = f32[8,256,128]{2,1,0:T(8,128)S(1)} collective-permute-done((f32[8,256,128]{2,1,0:T(8,128)S(1)}, f32[8,256,128]{2,1,0:T(8,128)S(1)}, u32[]{:S(2)}, u32[]{:S(2)}) %collective-permute-start) | collective-permute-done | bytes 1048608 | tf_op jit(solution)/shard_map/ppermute | solution.py:185
  10.1 2.9 %collective-permute-start.2 = (f32[256,128]{1,0:T(8,128)S(1)}, f32[256,128]{1,0:T(8,128)S(1)}, u32[]{:S(2)}, u32[]{:S(2)}) collective-permute-start(f32[256,128]{1,0:T(8,128)S(1)} %get-tuple-element.39), channel_id=1, source_target_pairs={{0,16},{8,24},{16,32},{24,40},{32,48},{40,56},{48,0},{56,8},{1,17}... | collective-permute-start | bytes 393224 | tf_op jit(solution)/shard_map/ppermute | solution.py:143
  12.9 3.8 %collective-permute-start.3 = (f32[256,128]{1,0:T(8,128)S(1)}, f32[256,128]{1,0:T(8,128)S(1)}, u32[]{:S(2)}, u32[]{:S(2)}) collective-permute-start(f32[256,128]{1,0:T(8,128)S(1)} %get-tuple-element.40), channel_id=1, source_target_pairs={{0,24},{8,32},{16,40},{24,48},{32,56},{40,0},{48,8},{56,16},{1,25}... | collective-permute-start | bytes 393224 | tf_op jit(solution)/shard_map/ppermute | solution.py:143
  17.5 4.2 %collective-permute-start.5 = (f32[256,128]{1,0:T(8,128)S(1)}, f32[256,128]{1,0:T(8,128)S(1)}, u32[]{:S(2)}, u32[]{:S(2)}) collective-permute-start(f32[256,128]{1,0:T(8,128)S(1)} %get-tuple-element.42), channel_id=1, source_target_pairs={{0,40},{8,48},{16,56},{24,0},{32,8},{40,16},{48,24},{56,32},{1,41}... | collective-permute-start | bytes 393224 | tf_op jit(solution)/shard_map/ppermute | solution.py:143
  21.8 2.2 %collective-permute-start.6 = (f32[256,128]{1,0:T(8,128)S(1)}, f32[256,128]{1,0:T(8,128)S(1)}, u32[]{:S(2)}, u32[]{:S(2)}) collective-permute-start(f32[256,128]{1,0:T(8,128)S(1)} %get-tuple-element.43), channel_id=1, source_target_pairs={{0,48},{8,56},{16,0},{24,8},{32,16},{40,24},{48,32},{56,40},{1,49}... | collective-permute-start | bytes 393224 | tf_op jit(solution)/shard_map/ppermute | solution.py:143
  24.0 9.2 %collective-permute-done.3.refs_3_ = f32[256,128]{1,0:T(8,128)S(1)} collective-permute-done((f32[256,128]{1,0:T(8,128)S(1)}, f32[256,128]{1,0:T(8,128)S(1)}, u32[]{:S(2)}, u32[]{:S(2)}) %collective-permute-start.3) | collective-permute-done | bytes 131104 | tf_op jit(solution)/shard_map/ppermute | solution.py:143
  33.3 1.2 %shard_map.69 = (bf16[128,2048]{1,0:T(8,128)(2,1)S(1)}, bf16[128,2048]{1,0:T(8,128)(2,1)S(1)}, bf16[128,2048]{1,0:T(8,128)(2,1)S(1)}) custom-call(bf16[128,2048]{1,0:T(8,128)(2,1)S(1)} %copy-done, bf16[128,2048]{1,0:T(8,128)(2,1)S(1)} %copy-done.1, bf16[128,2048]{1,0:T(8,128)(2,1)S(1)} %copy-done.2, bf16[128,2048]{1,0:T(8,128)(2,1)S(1)} %copy-done.3), custom_call_target="tpu_custom_call" | custom-call | flops 201326592 | bytes 3670016 | tf_op jit(solution)/shard_map/pallas_call | solution.py:186
  35.3 0.8 copy-done.18
  36.1 5.6 %collective-permute-done.6.refs_6_ = f32[256,128]{1,0:T(8,128)S(1)} collective-permute-done((f32[256,128]{1,0:T(8,128)S(1)}, f32[256,128]{1,0:T(8,128)S(1)}, u32[]{:S(2)}, u32[]{:S(2)}) %collective-permute-start.6) | collective-permute-done | bytes 131104 | tf_op jit(solution)/shard_map/ppermute | solution.py:143
  42.5 2.8 %collective-permute-start.11 = (f32[256,128]{1,0:T(8,128)}, f32[256,128]{1,0:T(8,128)}, u32[]{:S(2)}, u32[]{:S(2)}) collective-permute-start(f32[256,128]{1,0:T(8,128)} %add_add_fusion.1), channel_id=1, source_target_pairs={{0,192},{64,0},{128,64},{192,128},{1,193},{65,1},{129,65},{193,129... | collective-permute-start | bytes 393224 | tf_op jit(solution)/shard_map/ppermute | solution.py:143
  46.4 1.7 %collective-permute-done.11 = f32[256,128]{1,0:T(8,128)} collective-permute-done((f32[256,128]{1,0:T(8,128)}, f32[256,128]{1,0:T(8,128)}, u32[]{:S(2)}, u32[]{:S(2)}) %collective-permute-start.11) | collective-permute-done | bytes 131104 | tf_op jit(solution)/shard_map/ppermute | solution.py:143
  48.0 3.0 %collective-permute-done.10 = f32[256,128]{1,0:T(8,128)} collective-permute-done((f32[256,128]{1,0:T(8,128)}, f32[256,128]{1,0:T(8,128)}, u32[]{:S(2)}, u32[]{:S(2)}) %collective-permute-start.10) | collective-permute-done | bytes 131104 | tf_op jit(solution)/shard_map/ppermute | solution.py:143
  51.0 3.1 %collective-permute-done.9 = f32[256,128]{1,0:T(8,128)} collective-permute-done((f32[256,128]{1,0:T(8,128)}, f32[256,128]{1,0:T(8,128)}, u32[]{:S(2)}, u32[]{:S(2)}) %collective-permute-start.9) | collective-permute-done | bytes 131104 | tf_op jit(solution)/shard_map/ppermute | solution.py:143
  54.2 1.1 %add_add_fusion = (f32[256,128]{1,0:T(8,128)S(1)}, f32[256,128]{1,0:T(8,128)S(1)}) fusion(f32[256,128]{1,0:T(8,128)} %collective-permute-done.11, f32[256,128]{1,0:T(8,128)} %collective-permute-done.10, f32[256,128]{1,0:T(8,128)} %add_add_fusion.1, f32[256,128]{1,0:T(8,128)} %collective-permute-done.9, pred[]{:T(512)S(6)} %eq.17, pred[]{:T(512)S(6)} %eq.16, ...), kind=kLoop, calls=%fused_computation | loop fusion | flops 262144 | bytes 786435 | tf_op jit(solution)/shard_map/add | solution.py:211
  55.3 1.3 %collective-permute-start.14 = (f32[256,128]{1,0:T(8,128)S(1)}, f32[256,128]{1,0:T(8,128)S(1)}, u32[]{:S(2)}, u32[]{:S(2)}) collective-permute-start(f32[256,128]{1,0:T(8,128)S(1)} %get-tuple-element.67), channel_id=1, source_target_pairs={{0,3},{7,4},{8,11},{15,12},{16,19},{23,20},{24,27},{31,28},{32,35}... | collective-permute-start | bytes 393224 | tf_op jit(solution)/shard_map/ppermute | solution.py:149
  56.6 1.3 %collective-permute-start.13 = (f32[256,128]{1,0:T(8,128)S(1)}, f32[256,128]{1,0:T(8,128)S(1)}, u32[]{:S(2)}, u32[]{:S(2)}) collective-permute-start(f32[256,128]{1,0:T(8,128)S(1)} %get-tuple-element.67), channel_id=1, source_target_pairs={{0,2},{1,3},{6,4},{7,5},{8,10},{9,11},{14,12},{15,13},{16,18},{17,... | collective-permute-start | bytes 393224 | tf_op jit(solution)/shard_map/ppermute | solution.py:149
  57.9 1.3 %collective-permute-start.12 = (f32[256,128]{1,0:T(8,128)S(1)}, f32[256,128]{1,0:T(8,128)S(1)}, u32[]{:S(2)}, u32[]{:S(2)}) collective-permute-start(f32[256,128]{1,0:T(8,128)S(1)} %get-tuple-element.67), channel_id=1, source_target_pairs={{0,1},{1,2},{2,3},{5,4},{6,5},{7,6},{8,9},{9,10},{10,11},{13,12},{... | collective-permute-start | bytes 393224 | tf_op jit(solution)/shard_map/ppermute | solution.py:149
  59.2 3.0 %collective-permute-done.14.refs_11_ = f32[256,128]{1,0:T(8,128)S(1)} collective-permute-done((f32[256,128]{1,0:T(8,128)S(1)}, f32[256,128]{1,0:T(8,128)S(1)}, u32[]{:S(2)}, u32[]{:S(2)}) %collective-permute-start.14) | collective-permute-done | bytes 131104 | tf_op jit(solution)/shard_map/ppermute | solution.py:149
  62.2 1.6 %collective-permute-done.13.refs_10_ = f32[256,128]{1,0:T(8,128)S(1)} collective-permute-done((f32[256,128]{1,0:T(8,128)S(1)}, f32[256,128]{1,0:T(8,128)S(1)}, u32[]{:S(2)}, u32[]{:S(2)}) %collective-permute-start.13) | collective-permute-done | bytes 131104 | tf_op jit(solution)/shard_map/ppermute | solution.py:149
  63.9 0.8 shard_map.70
  64.7 5.0 %collective-permute-start.15 = (f32[256,128]{1,0:T(8,128)S(1)}, f32[256,128]{1,0:T(8,128)S(1)}, u32[]{:S(2)}, u32[]{:S(2)}) collective-permute-start(f32[256,128]{1,0:T(8,128)S(1)} %get-tuple-element.60), channel_id=1, source_target_pairs={{0,8},{8,16},{16,24},{24,32},{32,40},{40,48},{48,56},{56,0},{1,9},... | collective-permute-start | bytes 393224 | tf_op jit(solution)/shard_map/ppermute | solution.py:143
  70.3 5.1 %collective-permute-start.18 = (f32[256,128]{1,0:T(8,128)S(1)}, f32[256,128]{1,0:T(8,128)S(1)}, u32[]{:S(2)}, u32[]{:S(2)}) collective-permute-start(f32[256,128]{1,0:T(8,128)S(1)} %get-tuple-element.63), channel_id=1, source_target_pairs={{0,32},{8,40},{16,48},{24,56},{32,0},{40,8},{48,16},{56,24},{1,33}... | collective-permute-start | bytes 393224 | tf_op jit(solution)/shard_map/ppermute | solution.py:143
  75.9 2.1 %collective-permute-start.20 = (f32[256,128]{1,0:T(8,128)S(1)}, f32[256,128]{1,0:T(8,128)S(1)}, u32[]{:S(2)}, u32[]{:S(2)}) collective-permute-start(f32[256,128]{1,0:T(8,128)S(1)} %get-tuple-element.65), channel_id=1, source_target_pairs={{0,48},{8,56},{16,0},{24,8},{32,16},{40,24},{48,32},{56,40},{1,49}... | collective-permute-start | bytes 393224 | tf_op jit(solution)/shard_map/ppermute | solution.py:143
  79.4 2.8 %collective-permute-done.17.refs_11_ = f32[256,128]{1,0:T(8,128)S(1)} collective-permute-done((f32[256,128]{1,0:T(8,128)S(1)}, f32[256,128]{1,0:T(8,128)S(1)}, u32[]{:S(2)}, u32[]{:S(2)}) %collective-permute-start.17) | collective-permute-done | bytes 131104 | tf_op jit(solution)/shard_map/ppermute | solution.py:143
  82.2 9.9 %collective-permute-start.22 = (f32[256,128]{1,0:T(8,128)S(1)}, f32[256,128]{1,0:T(8,128)S(1)}, u32[]{:S(2)}, u32[]{:S(2)}) collective-permute-start(f32[256,128]{1,0:T(8,128)S(1)} %get-tuple-element.59.refs_8_), channel_id=1, source_target_pairs={{0,4},{4,0},{1,5},{5,1},{2,6},{6,2},{3,7},{7,3},{8,12},{12,8},{9,1... | collective-permute-start | bytes 393224 | tf_op jit(solution)/shard_map/ppermute | solution.py:232
  92.1 0.9 collective-permute-start.24
  92.9 1.6 %collective-permute-done.20.refs_14_ = f32[256,128]{1,0:T(8,128)S(1)} collective-permute-done((f32[256,128]{1,0:T(8,128)S(1)}, f32[256,128]{1,0:T(8,128)S(1)}, u32[]{:S(2)}, u32[]{:S(2)}) %collective-permute-start.20) | collective-permute-done | bytes 131104 | tf_op jit(solution)/shard_map/ppermute | solution.py:143
  94.5 4.0 %collective-permute-start.25 = (f32[256,128]{1,0:T(8,128)S(1)}, f32[256,128]{1,0:T(8,128)S(1)}, u32[]{:S(2)}, u32[]{:S(2)}) collective-permute-start(f32[256,128]{1,0:T(8,128)S(1)} %collective-permute-done.17.refs_11_), channel_id=1, source_target_pairs={{0,4},{4,0},{1,5},{5,1},{2,6},{6,2},{3,7},{7,3},{8,12},{12,8},{9,1... | collective-permute-start | bytes 393224 | tf_op jit(solution)/shard_map/ppermute | solution.py:232
  98.6 1.2 %collective-permute-start.26 = (f32[256,128]{1,0:T(8,128)S(1)}, f32[256,128]{1,0:T(8,128)S(1)}, u32[]{:S(2)}, u32[]{:S(2)}) collective-permute-start(f32[256,128]{1,0:T(8,128)S(1)} %collective-permute-done.18.refs_12_), channel_id=1, source_target_pairs={{0,4},{4,0},{1,5},{5,1},{2,6},{6,2},{3,7},{7,3},{8,12},{12,8},{9,1... | collective-permute-start | bytes 393224 | tf_op jit(solution)/shard_map/ppermute | solution.py:232
  101.7 3.7 %shard_map.71 = (bf16[128,2048]{1,0:T(8,128)(2,1)}, bf16[128,2048]{1,0:T(8,128)(2,1)}, bf16[128,2048]{1,0:T(8,128)(2,1)}) custom-call(s32[2]{0:T(128)S(1)} %pad_add_fusion.places, bf16[128,2048]{1,0:T(8,128)(2,1)S(1)} %copy-done, bf16[128,2048]{1,0:T(8,128)(2,1)S(1)} %copy-done.1, bf16[128,2048]{1,0:T(8,128)(2,1)S(1)} %copy-done.2, ...), custom_call_target="tpu_custom_call" | custom-call | flops 402653184 | bytes 8388608 | tf_op jit(solution)/shard_map/pallas_call | solution.py:233
  (76 shorter events, 8.3 us)
Async XLA Ops:
  4.2 5.6 %collective-permute-start = (f32[8,256,128]{2,1,0:T(8,128)S(1)}, f32[8,256,128]{2,1,0:T(8,128)S(1)}, u32[]{:S(2)}, u32[]{:S(2)}) collective-permute-start(f32[8,256,128]{2,1,0:T(8,128)S(1)} %get-tuple-element.36), channel_id=1, source_target_pairs={{0,4},{4,0},{1,5},{5,1},{2,6},{6,2},{3,7},{7,3},{8,12},{12,8},{9,1... | collective-permute-start | bytes 3145736 | tf_op jit(solution)/shard_map/ppermute | solution.py:185
  7.6 67.8 %collective-permute-start.8 = (f32[8,256,128]{2,1,0:T(8,128)S(1)}, f32[8,256,128]{2,1,0:T(8,128)}, u32[]{:S(2)}, u32[]{:S(2)}) collective-permute-start(f32[8,256,128]{2,1,0:T(8,128)S(1)} %get-tuple-element.35.keep), channel_id=1, source_target_pairs={{0,4},{4,0},{1,5},{5,1},{2,6},{6,2},{3,7},{7,3},{8,12},{12,8},{9,1... | collective-permute-start | bytes 3145736 | tf_op jit(solution)/shard_map/ppermute | solution.py:202
  10.0 7.5 %collective-permute-start.1 = (f32[256,128]{1,0:T(8,128)S(1)}, f32[256,128]{1,0:T(8,128)S(1)}, u32[]{:S(2)}, u32[]{:S(2)}) collective-permute-start(f32[256,128]{1,0:T(8,128)S(1)} %get-tuple-element.38), channel_id=1, source_target_pairs={{0,8},{8,16},{16,24},{24,32},{32,40},{40,48},{48,56},{56,0},{1,9},... | collective-permute-start | bytes 393224 | tf_op jit(solution)/shard_map/ppermute | solution.py:143
  10.1 11.7 %collective-permute-start.2 = (f32[256,128]{1,0:T(8,128)S(1)}, f32[256,128]{1,0:T(8,128)S(1)}, u32[]{:S(2)}, u32[]{:S(2)}) collective-permute-start(f32[256,128]{1,0:T(8,128)S(1)} %get-tuple-element.39), channel_id=1, source_target_pairs={{0,16},{8,24},{16,32},{24,40},{32,48},{40,56},{48,0},{56,8},{1,17}... | collective-permute-start | bytes 393224 | tf_op jit(solution)/shard_map/ppermute | solution.py:143
  12.9 20.3 %collective-permute-start.3 = (f32[256,128]{1,0:T(8,128)S(1)}, f32[256,128]{1,0:T(8,128)S(1)}, u32[]{:S(2)}, u32[]{:S(2)}) collective-permute-start(f32[256,128]{1,0:T(8,128)S(1)} %get-tuple-element.40), channel_id=1, source_target_pairs={{0,24},{8,32},{16,40},{24,48},{32,56},{40,0},{48,8},{56,16},{1,25}... | collective-permute-start | bytes 393224 | tf_op jit(solution)/shard_map/ppermute | solution.py:143
  16.7 19.4 %collective-permute-start.4 = (f32[256,128]{1,0:T(8,128)S(1)}, f32[256,128]{1,0:T(8,128)S(1)}, u32[]{:S(2)}, u32[]{:S(2)}) collective-permute-start(f32[256,128]{1,0:T(8,128)S(1)} %get-tuple-element.41), channel_id=1, source_target_pairs={{0,32},{8,40},{16,48},{24,56},{32,0},{40,8},{48,16},{56,24},{1,33}... | collective-permute-start | bytes 393224 | tf_op jit(solution)/shard_map/ppermute | solution.py:143
  17.5 18.6 %collective-permute-start.5 = (f32[256,128]{1,0:T(8,128)S(1)}, f32[256,128]{1,0:T(8,128)S(1)}, u32[]{:S(2)}, u32[]{:S(2)}) collective-permute-start(f32[256,128]{1,0:T(8,128)S(1)} %get-tuple-element.42), channel_id=1, source_target_pairs={{0,40},{8,48},{16,56},{24,0},{32,8},{40,16},{48,24},{56,32},{1,41}... | collective-permute-start | bytes 393224 | tf_op jit(solution)/shard_map/ppermute | solution.py:143
  21.8 19.9 %collective-permute-start.6 = (f32[256,128]{1,0:T(8,128)S(1)}, f32[256,128]{1,0:T(8,128)S(1)}, u32[]{:S(2)}, u32[]{:S(2)}) collective-permute-start(f32[256,128]{1,0:T(8,128)S(1)} %get-tuple-element.43), channel_id=1, source_target_pairs={{0,48},{8,56},{16,0},{24,8},{32,16},{40,24},{48,32},{56,40},{1,49}... | collective-permute-start | bytes 393224 | tf_op jit(solution)/shard_map/ppermute | solution.py:143
  33.2 8.5 %collective-permute-start.7 = (f32[256,128]{1,0:T(8,128)S(1)}, f32[256,128]{1,0:T(8,128)S(1)}, u32[]{:S(2)}, u32[]{:S(2)}) collective-permute-start(f32[256,128]{1,0:T(8,128)S(1)} %get-tuple-element.44), channel_id=1, source_target_pairs={{0,56},{8,0},{16,8},{24,16},{32,24},{40,32},{48,40},{56,48},{1,57}... | collective-permute-start | bytes 393224 | tf_op jit(solution)/shard_map/ppermute | solution.py:143
  42.5 5.5 %collective-permute-start.11 = (f32[256,128]{1,0:T(8,128)}, f32[256,128]{1,0:T(8,128)}, u32[]{:S(2)}, u32[]{:S(2)}) collective-permute-start(f32[256,128]{1,0:T(8,128)} %add_add_fusion.1), channel_id=1, source_target_pairs={{0,192},{64,0},{128,64},{192,128},{1,193},{65,1},{129,65},{193,129... | collective-permute-start | bytes 393224 | tf_op jit(solution)/shard_map/ppermute | solution.py:143
  45.3 5.7 %collective-permute-start.10 = (f32[256,128]{1,0:T(8,128)}, f32[256,128]{1,0:T(8,128)}, u32[]{:S(2)}, u32[]{:S(2)}) collective-permute-start(f32[256,128]{1,0:T(8,128)} %add_add_fusion.1), channel_id=1, source_target_pairs={{0,128},{64,192},{128,0},{192,64},{1,129},{65,193},{129,1},{193,65... | collective-permute-start | bytes 393224 | tf_op jit(solution)/shard_map/ppermute | solution.py:143
  45.7 8.5 %collective-permute-start.9 = (f32[256,128]{1,0:T(8,128)}, f32[256,128]{1,0:T(8,128)}, u32[]{:S(2)}, u32[]{:S(2)}) collective-permute-start(f32[256,128]{1,0:T(8,128)} %add_add_fusion.1), channel_id=1, source_target_pairs={{0,64},{64,128},{128,192},{192,0},{1,65},{65,129},{129,193},{193,1... | collective-permute-start | bytes 393224 | tf_op jit(solution)/shard_map/ppermute | solution.py:143
  55.3 6.9 %collective-permute-start.14 = (f32[256,128]{1,0:T(8,128)S(1)}, f32[256,128]{1,0:T(8,128)S(1)}, u32[]{:S(2)}, u32[]{:S(2)}) collective-permute-start(f32[256,128]{1,0:T(8,128)S(1)} %get-tuple-element.67), channel_id=1, source_target_pairs={{0,3},{7,4},{8,11},{15,12},{16,19},{23,20},{24,27},{31,28},{32,35}... | collective-permute-start | bytes 393224 | tf_op jit(solution)/shard_map/ppermute | solution.py:149
  56.6 7.2 %collective-permute-start.13 = (f32[256,128]{1,0:T(8,128)S(1)}, f32[256,128]{1,0:T(8,128)S(1)}, u32[]{:S(2)}, u32[]{:S(2)}) collective-permute-start(f32[256,128]{1,0:T(8,128)S(1)} %get-tuple-element.67), channel_id=1, source_target_pairs={{0,2},{1,3},{6,4},{7,5},{8,10},{9,11},{14,12},{15,13},{16,18},{17,... | collective-permute-start | bytes 393224 | tf_op jit(solution)/shard_map/ppermute | solution.py:149
  57.9 5.9 %collective-permute-start.12 = (f32[256,128]{1,0:T(8,128)S(1)}, f32[256,128]{1,0:T(8,128)S(1)}, u32[]{:S(2)}, u32[]{:S(2)}) collective-permute-start(f32[256,128]{1,0:T(8,128)S(1)} %get-tuple-element.67), channel_id=1, source_target_pairs={{0,1},{1,2},{2,3},{5,4},{6,5},{7,6},{8,9},{9,10},{10,11},{13,12},{... | collective-permute-start | bytes 393224 | tf_op jit(solution)/shard_map/ppermute | solution.py:149
  63.8 37.8 %copy-start.15 = (bf16[128,2048]{1,0:T(8,128)(2,1)S(1)}, bf16[128,2048]{1,0:T(8,128)(2,1)}, u32[]{:S(2)}) copy-start(bf16[128,2048]{1,0:T(8,128)(2,1)} %copy-done.14) | copy-start | bytes 1572868
  63.9 37.8 %copy-start.17 = (bf16[128,2048]{1,0:T(8,128)(2,1)S(1)}, bf16[128,2048]{1,0:T(8,128)(2,1)}, u32[]{:S(2)}) copy-start(bf16[128,2048]{1,0:T(8,128)(2,1)} %copy-done.16) | copy-start | bytes 1572868
  64.7 11.1 %collective-permute-start.15 = (f32[256,128]{1,0:T(8,128)S(1)}, f32[256,128]{1,0:T(8,128)S(1)}, u32[]{:S(2)}, u32[]{:S(2)}) collective-permute-start(f32[256,128]{1,0:T(8,128)S(1)} %get-tuple-element.60), channel_id=1, source_target_pairs={{0,8},{8,16},{16,24},{24,32},{32,40},{40,48},{48,56},{56,0},{1,9},... | collective-permute-start | bytes 393224 | tf_op jit(solution)/shard_map/ppermute | solution.py:143
  69.8 9.0 %collective-permute-start.16 = (f32[256,128]{1,0:T(8,128)S(1)}, f32[256,128]{1,0:T(8,128)S(1)}, u32[]{:S(2)}, u32[]{:S(2)}) collective-permute-start(f32[256,128]{1,0:T(8,128)S(1)} %get-tuple-element.61), channel_id=1, source_target_pairs={{0,16},{8,24},{16,32},{24,40},{32,48},{40,56},{48,0},{56,8},{1,17}... | collective-permute-start | bytes 393224 | tf_op jit(solution)/shard_map/ppermute | solution.py:143
  70.2 12.0 %collective-permute-start.17 = (f32[256,128]{1,0:T(8,128)S(1)}, f32[256,128]{1,0:T(8,128)S(1)}, u32[]{:S(2)}, u32[]{:S(2)}) collective-permute-start(f32[256,128]{1,0:T(8,128)S(1)} %get-tuple-element.62), channel_id=1, source_target_pairs={{0,24},{8,32},{16,40},{24,48},{32,56},{40,0},{48,8},{56,16},{1,25}... | collective-permute-start | bytes 393224 | tf_op jit(solution)/shard_map/ppermute | solution.py:143
  70.3 21.8 %collective-permute-start.18 = (f32[256,128]{1,0:T(8,128)S(1)}, f32[256,128]{1,0:T(8,128)S(1)}, u32[]{:S(2)}, u32[]{:S(2)}) collective-permute-start(f32[256,128]{1,0:T(8,128)S(1)} %get-tuple-element.63), channel_id=1, source_target_pairs={{0,32},{8,40},{16,48},{24,56},{32,0},{40,8},{48,16},{56,24},{1,33}... | collective-permute-start | bytes 393224 | tf_op jit(solution)/shard_map/ppermute | solution.py:143
  75.4 16.7 %collective-permute-start.19 = (f32[256,128]{1,0:T(8,128)S(1)}, f32[256,128]{1,0:T(8,128)S(1)}, u32[]{:S(2)}, u32[]{:S(2)}) collective-permute-start(f32[256,128]{1,0:T(8,128)S(1)} %get-tuple-element.64), channel_id=1, source_target_pairs={{0,40},{8,48},{16,56},{24,0},{32,8},{40,16},{48,24},{56,32},{1,41}... | collective-permute-start | bytes 393224 | tf_op jit(solution)/shard_map/ppermute | solution.py:143
  75.9 18.7 %collective-permute-start.20 = (f32[256,128]{1,0:T(8,128)S(1)}, f32[256,128]{1,0:T(8,128)S(1)}, u32[]{:S(2)}, u32[]{:S(2)}) collective-permute-start(f32[256,128]{1,0:T(8,128)S(1)} %get-tuple-element.65), channel_id=1, source_target_pairs={{0,48},{8,56},{16,0},{24,8},{32,16},{40,24},{48,32},{56,40},{1,49}... | collective-permute-start | bytes 393224 | tf_op jit(solution)/shard_map/ppermute | solution.py:143
  78.8 19.8 %collective-permute-start.21 = (f32[256,128]{1,0:T(8,128)S(1)}, f32[256,128]{1,0:T(8,128)S(1)}, u32[]{:S(2)}, u32[]{:S(2)}) collective-permute-start(f32[256,128]{1,0:T(8,128)S(1)} %get-tuple-element.66), channel_id=1, source_target_pairs={{0,56},{8,0},{16,8},{24,16},{32,24},{40,32},{48,40},{56,48},{1,57}... | collective-permute-start | bytes 393224 | tf_op jit(solution)/shard_map/ppermute | solution.py:143
  82.2 17.6 %collective-permute-start.22 = (f32[256,128]{1,0:T(8,128)S(1)}, f32[256,128]{1,0:T(8,128)S(1)}, u32[]{:S(2)}, u32[]{:S(2)}) collective-permute-start(f32[256,128]{1,0:T(8,128)S(1)} %get-tuple-element.59.refs_8_), channel_id=1, source_target_pairs={{0,4},{4,0},{1,5},{5,1},{2,6},{6,2},{3,7},{7,3},{8,12},{12,8},{9,1... | collective-permute-start | bytes 393224 | tf_op jit(solution)/shard_map/ppermute | solution.py:232
  92.1 7.7 %collective-permute-start.23 = (f32[256,128]{1,0:T(8,128)S(1)}, f32[256,128]{1,0:T(8,128)S(1)}, u32[]{:S(2)}, u32[]{:S(2)}) collective-permute-start(f32[256,128]{1,0:T(8,128)S(1)} %collective-permute-done.15.refs_9_), channel_id=1, source_target_pairs={{0,4},{4,0},{1,5},{5,1},{2,6},{6,2},{3,7},{7,3},{8,12},{12,8},{9,1... | collective-permute-start | bytes 393224 | tf_op jit(solution)/shard_map/ppermute | solution.py:232
  92.1 8.2 %collective-permute-start.24 = (f32[256,128]{1,0:T(8,128)S(1)}, f32[256,128]{1,0:T(8,128)S(1)}, u32[]{:S(2)}, u32[]{:S(2)}) collective-permute-start(f32[256,128]{1,0:T(8,128)S(1)} %collective-permute-done.16.refs_10_), channel_id=1, source_target_pairs={{0,4},{4,0},{1,5},{5,1},{2,6},{6,2},{3,7},{7,3},{8,12},{12,8},{9,1... | collective-permute-start | bytes 393224 | tf_op jit(solution)/shard_map/ppermute | solution.py:232
  94.5 5.9 %collective-permute-start.25 = (f32[256,128]{1,0:T(8,128)S(1)}, f32[256,128]{1,0:T(8,128)S(1)}, u32[]{:S(2)}, u32[]{:S(2)}) collective-permute-start(f32[256,128]{1,0:T(8,128)S(1)} %collective-permute-done.17.refs_11_), channel_id=1, source_target_pairs={{0,4},{4,0},{1,5},{5,1},{2,6},{6,2},{3,7},{7,3},{8,12},{12,8},{9,1... | collective-permute-start | bytes 393224 | tf_op jit(solution)/shard_map/ppermute | solution.py:232
  98.6 2.2 %collective-permute-start.26 = (f32[256,128]{1,0:T(8,128)S(1)}, f32[256,128]{1,0:T(8,128)S(1)}, u32[]{:S(2)}, u32[]{:S(2)}) collective-permute-start(f32[256,128]{1,0:T(8,128)S(1)} %collective-permute-done.18.refs_12_), channel_id=1, source_target_pairs={{0,4},{4,0},{1,5},{5,1},{2,6},{6,2},{3,7},{7,3},{8,12},{12,8},{9,1... | collective-permute-start | bytes 393224 | tf_op jit(solution)/shard_map/ppermute | solution.py:232
  99.8 1.3 %collective-permute-start.27 = (f32[256,128]{1,0:T(8,128)S(1)}, f32[256,128]{1,0:T(8,128)S(1)}, u32[]{:S(2)}, u32[]{:S(2)}) collective-permute-start(f32[256,128]{1,0:T(8,128)S(1)} %collective-permute-done.19.refs_13_), channel_id=1, source_target_pairs={{0,4},{4,0},{1,5},{5,1},{2,6},{6,2},{3,7},{7,3},{8,12},{12,8},{9,1... | collective-permute-start | bytes 393224 | tf_op jit(solution)/shard_map/ppermute | solution.py:232
  99.8 1.5 %collective-permute-start.28 = (f32[256,128]{1,0:T(8,128)S(1)}, f32[256,128]{1,0:T(8,128)S(1)}, u32[]{:S(2)}, u32[]{:S(2)}) collective-permute-start(f32[256,128]{1,0:T(8,128)S(1)} %collective-permute-done.20.refs_14_), channel_id=1, source_target_pairs={{0,4},{4,0},{1,5},{5,1},{2,6},{6,2},{3,7},{7,3},{8,12},{12,8},{9,1... | collective-permute-start | bytes 393224 | tf_op jit(solution)/shard_map/ppermute | solution.py:232
  100.3 1.3 %collective-permute-start.29 = (f32[256,128]{1,0:T(8,128)S(1)}, f32[256,128]{1,0:T(8,128)S(1)}, u32[]{:S(2)}, u32[]{:S(2)}) collective-permute-start(f32[256,128]{1,0:T(8,128)S(1)} %collective-permute-done.21.refs_15_), channel_id=1, source_target_pairs={{0,4},{4,0},{1,5},{5,1},{2,6},{6,2},{3,7},{7,3},{8,12},{12,8},{9,1... | collective-permute-start | bytes 393224 | tf_op jit(solution)/shard_map/ppermute | solution.py:232
  (18 other events, 258.6 us)

commit v3 on v2

v3 whole, which is shorter than its diff:
```python
import functools

import jax
import jax.numpy as jnp
from jax import lax
from jax.experimental import pallas as pl
from jax.experimental.pallas import tpu as pltpu
from jax.sharding import Mesh
from jax.sharding import PartitionSpec as P

HEAD = 128
LOADS = 4
ROWS = ("x", "y", "z", "c")
SMEM = pl.BlockSpec(memory_space=pltpu.SMEM)
VMEM = pl.BlockSpec(memory_space=pltpu.VMEM)
HBM = pl.BlockSpec(memory_space=pltpu.HBM)
VMEM_LIMIT = 24 * 1024 * 1024
F32, BF16 = jnp.float32, jnp.bfloat16


def contract(lhs, rhs, lhs_dim, rhs_dim):
    return lax.dot_general(
        lhs, rhs, (((lhs_dim,), (rhs_dim,)), ((), ())), preferred_element_type=F32
    )


def chunk_lanes(index, width):
    return pl.ds(pl.multiple_of(index * width, width), width)


def states_kernel(places, query, key, value, gradient, keep, send, held, sems):
    first = places[0] == 0
    z = places[1]
    slots = keep.shape[0]
    width = keep.shape[1]
    part = held.shape[3]
    copies = []
    for n in range(held.shape[1]):
        for source, tensor in enumerate((key, value, query, gradient)):
            copy = pltpu.make_async_copy(
                tensor.at[:, pl.ds(n * part, part)], held.at[source, n], sems.at[source, n]
            )
            copy.start()
            copies.append(copy)
    for n in range(held.shape[1]):
        for copy in copies[4 * n : 4 * n + 4]:
            copy.wait()
        for h in range(part // HEAD):
            lanes = pl.ds(h * HEAD, HEAD)
            chunk, row = divmod(n * part + h * HEAD, width)
            slot = lax.rem(chunk + slots - z, slots)
            kv = contract(held[0, n, :, lanes], held[1, n, :, lanes], 0, 0)
            qo = contract(held[2, n, :, lanes], held[3, n, :, lanes], 0, 0)
            keep[slot, pl.ds(row, HEAD), :] = jnp.where(first, kv, qo)
            send[slot, pl.ds(row, HEAD), :] = jnp.where(first, qo, kv)


def inner_kernel(query, key, value, gradient, gq, gk, gv):
    count = query.shape[0]
    causal = lax.broadcasted_iota(jnp.int32, (count, count), 0) >= lax.broadcasted_iota(
        jnp.int32, (count, count), 1
    )
    for h in range(query.shape[1] // HEAD):
        lanes = pl.ds(h * HEAD, HEAD)
        q, k, v, g = query[:, lanes], key[:, lanes], value[:, lanes], gradient[:, lanes]
        dv = jnp.where(causal, contract(g, v, 1, 1), 0.0).astype(BF16)
        qk = jnp.where(causal, contract(q, k, 1, 1), 0.0).astype(BF16)
        gq[:, lanes] = contract(dv, k, 1, 0)
        gk[:, lanes] = contract(dv, q, 0, 0)
        gv[:, lanes] = contract(qk, g, 0, 0)


def merge_kernel(order, keep, received, *outs):
    for offset, out in zip(order, outs, strict=True):
        out[...] = keep[offset] + received[offset]


def sum_kernel(*refs):
    total = refs[0][...]
    for ref in refs[1:-1]:
        total = total + ref[...]
    refs[-1][...] = total


def scan_kernel(order, rows, places, *refs):
    slots = len(order)
    sources = refs[:slots]
    around = refs[slots : slots + rows - 1]
    planes = refs[slots + rows - 1 : -slots - 1]
    outs = refs[-slots - 1 : -1]
    held = refs[-1]
    first = places[0] == 0
    z = places[1]
    row = places[2]
    total = planes[0][...]
    for plane in planes[1:]:
        total = total + plane[...]
    for step, part in enumerate(around, 1):
        total = total + jnp.where((row >= step) == first, part[...], 0.0)
    for offset, source in zip(order, sources, strict=True):
        held[lax.rem(z + slots - offset, slots)] = source[...]
    for n in range(slots):
        place = jnp.where(first, n, slots - 1 - n)
        piece = held[place]
        held[place] = total
        total = total + piece
    for offset, out in zip(order, outs, strict=True):
        out[...] = held[lax.rem(z + offset, slots)]


def outputs_kernel(order, scale, places, *refs):
    slots = len(order)
    query, key, value, gradient = refs[:4]
    inner = refs[4:7]
    other = refs[7]
    own = refs[8 : 8 + slots]
    received = refs[8 + slots : 8 + 2 * slots]
    outs = refs[8 + 2 * slots : 11 + 2 * slots]
    held, sems = refs[11 + 2 * slots :]
    first = places[0] == 0
    z = places[1]
    width = own[0].shape[0]
    copies = []
    for n, offset in enumerate(order):
        chunk = lax.rem(z + slots - offset, slots)
        for h in range(width // HEAD):
            rows = pl.ds(h * HEAD, HEAD)
            mine = own[n][rows, :]
            theirs = received[n][rows, :] + other[(slots - offset) % slots, rows, :]
            prefix = jnp.where(first, mine, theirs).astype(BF16)
            suffix = jnp.where(first, theirs, mine).astype(BF16)
            lanes = chunk_lanes(chunk * (width // HEAD) + h, HEAD)
            gq = contract(gradient[:, lanes], prefix, 1, 1)
            gk = contract(value[:, lanes], suffix, 1, 1)
            gv = contract(key[:, lanes], suffix, 1, 0)
            for t, result in enumerate((gq, gk, gv)):
                held[t, n, :, rows] = (scale * (result + inner[t][:, lanes])).astype(BF16)
        for t, out in enumerate(outs):
            copy = pltpu.make_async_copy(
                held.at[t, n], out.at[:, chunk_lanes(chunk, width)], sems.at[t, n]
            )
            copy.start()
            copies.append(copy)
    for copy in copies:
        copy.wait()


def call(kernel, in_specs, out_specs, out_shape, flops, moved, scratch=()):
    return pl.pallas_call(
        kernel,
        in_specs=in_specs,
        out_specs=out_specs,
        out_shape=out_shape,
        scratch_shapes=scratch,
        cost_estimate=pl.CostEstimate(flops=flops, bytes_accessed=moved, transcendentals=0),
        compiler_params=pltpu.CompilerParams(vmem_limit_bytes=VMEM_LIMIT),
    )


def turn(array, axis, count, step):
    return lax.ppermute(array, axis, [(i, (i + step) % count) for i in range(count)])


def onward(array, axis, count, step):
    pairs = [(i, i + step) for i in range(count - step)]
    pairs += [(count + i, count + i - step) for i in range(step, count)]
    return lax.ppermute(array, ("c", axis), pairs)


def issue_order(count):
    return sorted(range(count), key=lambda k: (k > 0, 2 * k != count, min(k, count - k), k))


def per_device(sizes, scale, queries, key_row_matrix, value_row_matrix, output_gradient):
    tokens, width = queries.shape
    slots = sizes["z"]
    rows = sizes["y"]
    order = issue_order(slots)
    chunk = width // slots
    core = lax.axis_index("c").astype(jnp.int32)
    depth = lax.axis_index("z").astype(jnp.int32)
    row = lax.axis_index("y").astype(jnp.int32)
    places = jnp.stack([core, depth, row])
    swap = [(0, 1), (1, 0)]
    product = 2 * width * tokens * HEAD
    token_bytes = 2 * tokens * width
    state_bytes = 4 * width * HEAD
    token_shape = jax.ShapeDtypeStruct((tokens, width), BF16)
    inner_shape = jax.ShapeDtypeStruct((tokens, width), F32)
    state_shape = jax.ShapeDtypeStruct((slots, chunk, HEAD), F32)
    chunk_shape = jax.ShapeDtypeStruct((chunk, HEAD), F32)
    inputs = (queries, key_row_matrix, value_row_matrix, output_gradient)

    keep, send = call(
        states_kernel,
        [SMEM] + [HBM] * 4,
        [VMEM] * 2,
        [state_shape] * 2,
        2 * product,
        4 * token_bytes + 2 * state_bytes,
        [
            pltpu.VMEM((4, LOADS, tokens, width // LOADS), BF16),
            pltpu.SemaphoreType.DMA((4, LOADS)),
        ],
    )(places, *(pltpu.with_memory_space_constraint(a, pltpu.HBM) for a in inputs))
    received = lax.ppermute(send, "c", swap)
    inner = call(
        inner_kernel,
        [VMEM] * 4,
        [VMEM] * 3,
        [inner_shape] * 3,
        5 * product,
        10 * token_bytes,
    )(*inputs)
    pieces = call(
        functools.partial(merge_kernel, order),
        [VMEM] * 2,
        [VMEM] * slots,
        [chunk_shape] * slots,
        width * HEAD,
        3 * state_bytes,
    )(keep, received)
    def total(*parts):
        return call(
            sum_kernel,
            [VMEM] * len(parts),
            VMEM,
            chunk_shape,
            len(parts) * chunk * HEAD,
            (len(parts) + 1) * 4 * chunk * HEAD,
        )(*parts)

    gathered = [p if k == 0 else turn(p, "z", slots, k) for k, p in zip(order, pieces, strict=True)]
    gathered, inner = lax.optimization_barrier((gathered, inner))
    column, keep = lax.optimization_barrier((total(*gathered), keep))
    other = lax.ppermute(keep, "c", swap)
    around = [turn(column, "y", rows, k) for k in range(1, rows)]
    around, other = lax.optimization_barrier((around, other))
    plane = total(column, *around)
    planes = [onward(plane, "x", sizes["x"], k) for k in range(1, sizes["x"])]
    prefixes = call(
        functools.partial(scan_kernel, order, rows),
        [SMEM] + [VMEM] * (slots + len(around) + len(planes)),
        [VMEM] * slots,
        [chunk_shape] * slots,
        2 * width * HEAD,
        3 * state_bytes,
        [pltpu.VMEM((slots, chunk, HEAD), F32)],
    )(places, *gathered, *around, *planes)
    own = [p if k == 0 else turn(p, "z", slots, k) for k, p in zip(order, prefixes, strict=True)]
    theirs = [lax.ppermute(part, "c", swap) for part in own]
    return call(
        functools.partial(outputs_kernel, order, scale),
        [SMEM] + [VMEM] * (8 + 2 * slots),
        [HBM] * 3,
        [token_shape] * 3,
        3 * product,
        13 * token_bytes + 3 * state_bytes,
        [
            pltpu.VMEM((3, slots, tokens, chunk), BF16),
            pltpu.SemaphoreType.DMA((3, slots)),
        ],
    )(places, *inputs, *inner, other, *own, *theirs)


def solution(mesh):
    sizes = {"y": 4, "z": 8, "c": 2, "x": 4}
    fine = Mesh(mesh.devices.reshape(tuple(sizes.values())), tuple(sizes))

    def program(queries, key_row_matrix, value_row_matrix, output_gradient):
        scale = float(HEAD * queries.shape[0]) ** -0.5
        spec = P(ROWS, None)
        return jax.shard_map(
            functools.partial(per_device, sizes, scale),
            mesh=fine,
            in_specs=(spec,) * 4,
            out_specs=(spec,) * 3,
            check_vma=False,
        )(queries, key_row_matrix, value_row_matrix, output_gradient)

    return program
```

time: 106 us -> 96.2 us (0.908)
  waiting for transfers between devices: 36.2 us -> 30.3 us
  other arithmetic: 1.94 us -> 0.08 us
  local copies, waits for them, and re-layouts: 1.66 us -> 0.01 us
  starting transfers between devices: 55.3 us -> 53.8 us
    ppermute x17, waiting for transfers between devices: 28.2 us -> 22.3 us  [turn(): lax.ppermute(array, axis, [(i, (i + step) % count) for i in range(count)])]
    ppermute x8, starting transfers between devices: 16.6 us -> 13.5 us  [per_device(): theirs = [lax.ppermute(part, 'c', swap) for part in own]]
    add x2 -> x0, other arithmetic: 1.87 us -> none  [the longest x1 1.13 us: per_device(): plane = functools.reduce(jnp.add, around, column)]
    unnamed x40 -> x8, local copies, waits for them, and re-layouts: 1.66 us -> 0.01 us
    pallas_call x4 -> x6, Pallas kernels: 5.85 us -> 7.19 us  [the longest x1 3.62 us: per_device(): call(inner_kernel, [VMEM] * 4, [VMEM] * 3, [inner_shape] * 3, 5 * product...]
    ppermute x17, starting transfers between devices: 31.4 us -> 32.5 us  [turn(): lax.ppermute(array, axis, [(i, (i + step) % count) for i in range(count)])]
  transfers between devices with their start and end apart: 30 -> 30, of which waited for: 17 -> 15; matrix products, arithmetic and copies ran while one was open for 2% -> 0% of each run, Pallas kernels for 2% -> 4%
where the time goes in v3:
time: 96.2 us; the launch traced here: 95.1 us
  starting transfers between devices  53.8 us (56%)
  waiting for transfers between devices  30.3 us (31%)
  Pallas kernels  10 us (10%)
    ppermute x17, starting transfers between devices, turn(): lax.ppermute(array, axis, [(i, (i + step) % count) for i in range(count)])  32.5 us
    ppermute x17, waiting for transfers between devices, turn(): lax.ppermute(array, axis, [(i, (i + step) % count) for i in range(count)])  22.3 us
    ppermute x8, starting transfers between devices, per_device(): theirs = [lax.ppermute(part, 'c', swap) for part in own]  13.5 us
    ppermute x3, waiting for transfers between devices, onward(): return lax.ppermute(array, ('c', axis), pairs)  4.62 us
    ppermute x3, starting transfers between devices, onward(): return lax.ppermute(array, ('c', axis), pairs)  3.88 us
    pallas_call x1, Pallas kernels, per_device(): call(inner_kernel, [VMEM] * 4, [VMEM] * 3, [inner_shape] * 3, 5 * product...  3.62 us
    ppermute x1, starting transfers between devices, per_device(): received = lax.ppermute(send, 'c', swap)  3.33 us
    pallas_call x1, Pallas kernels, per_device(): call(states_kernel, [SMEM] + [HBM] * 4, [VMEM] * 2, [state_shape] * 2, 2...  2.85 us
  transfers between devices with their start and end apart: 30, of which 15 were waited for; matrix products, arithmetic and copies ran while one was open for 0% of the time, Pallas kernels for 4%

profile of v3, /device:TPU:1, one launch (start us, length us, event | category | flops | bytes accessed | tf_op | source)
XLA Modules:
  0.0 95.1 jit_solution(4228563242737603081)
XLA Ops:
  0.7 2.8 %shard_map.67 = (f32[8,256,128]{2,1,0:T(8,128)S(1)}, f32[8,256,128]{2,1,0:T(8,128)S(1)}) custom-call(s32[3]{0:T(128)S(1)} %pad_add_fusion.places, bf16[128,2048]{1,0:T(8,128)(2,1)} %refs_0_.1, bf16[128,2048]{1,0:T(8,128)(2,1)} %refs_1_.1, bf16[128,2048]{1,0:T(8,128)(2,1)} %refs_2_.1, bf16[128,2048]{1,0:T(8,128)(2,1)} %refs_3_.1), custom_call_target="tpu_custom_call" | custom-call | flops 134217728 | bytes 4194304 | tf_op jit(solution)/shard_map/pallas_call | solution.py:194
  3.6 3.3 %collective-permute-start = (f32[8,256,128]{2,1,0:T(8,128)S(1)}, f32[8,256,128]{2,1,0:T(8,128)S(1)}, u32[]{:S(2)}, u32[]{:S(2)}) collective-permute-start(f32[8,256,128]{2,1,0:T(8,128)S(1)} %get-tuple-element.42), channel_id=1, source_target_pairs={{0,4},{4,0},{1,5},{5,1},{2,6},{6,2},{3,7},{7,3},{8,12},{12,8},{9,1... | collective-permute-start | bytes 3145736 | tf_op jit(solution)/shard_map/ppermute | solution.py:206
  6.9 2.3 %collective-permute-done.received = f32[8,256,128]{2,1,0:T(8,128)S(1)} collective-permute-done((f32[8,256,128]{2,1,0:T(8,128)S(1)}, f32[8,256,128]{2,1,0:T(8,128)S(1)}, u32[]{:S(2)}, u32[]{:S(2)}) %collective-permute-start) | collective-permute-done | bytes 1048608 | tf_op jit(solution)/shard_map/ppermute | solution.py:206
  9.3 5.3 %collective-permute-start.1 = (f32[256,128]{1,0:T(8,128)S(1)}, f32[256,128]{1,0:T(8,128)S(1)}, u32[]{:S(2)}, u32[]{:S(2)}) collective-permute-start(f32[256,128]{1,0:T(8,128)S(1)} %get-tuple-element.44), channel_id=1, source_target_pairs={{0,32},{8,40},{16,48},{24,56},{32,0},{40,8},{48,16},{56,24},{1,33}... | collective-permute-start | bytes 393224 | tf_op jit(solution)/shard_map/ppermute | solution.py:161
  15.3 1.9 %collective-permute-start.3 = (f32[256,128]{1,0:T(8,128)S(1)}, f32[256,128]{1,0:T(8,128)S(1)}, u32[]{:S(2)}, u32[]{:S(2)}) collective-permute-start(f32[256,128]{1,0:T(8,128)S(1)} %get-tuple-element.46), channel_id=1, source_target_pairs={{0,56},{8,0},{16,8},{24,16},{32,24},{40,32},{48,40},{56,48},{1,57}... | collective-permute-start | bytes 393224 | tf_op jit(solution)/shard_map/ppermute | solution.py:161
  17.2 3.6 %collective-permute-start.5 = (f32[256,128]{1,0:T(8,128)S(1)}, f32[256,128]{1,0:T(8,128)S(1)}, u32[]{:S(2)}, u32[]{:S(2)}) collective-permute-start(f32[256,128]{1,0:T(8,128)S(1)} %get-tuple-element.48), channel_id=1, source_target_pairs={{0,48},{8,56},{16,0},{24,8},{32,16},{40,24},{48,32},{56,40},{1,49}... | collective-permute-start | bytes 393224 | tf_op jit(solution)/shard_map/ppermute | solution.py:161
  20.8 3.3 %collective-permute-done.2.refs_2_ = f32[256,128]{1,0:T(8,128)S(1)} collective-permute-done((f32[256,128]{1,0:T(8,128)S(1)}, f32[256,128]{1,0:T(8,128)S(1)}, u32[]{:S(2)}, u32[]{:S(2)}) %collective-permute-start.2) | collective-permute-done | bytes 131104 | tf_op jit(solution)/shard_map/ppermute | solution.py:161
  24.2 1.1 %collective-permute-start.7 = (f32[256,128]{1,0:T(8,128)S(1)}, f32[256,128]{1,0:T(8,128)S(1)}, u32[]{:S(2)}, u32[]{:S(2)}) collective-permute-start(f32[256,128]{1,0:T(8,128)S(1)} %get-tuple-element.50), channel_id=1, source_target_pairs={{0,40},{8,48},{16,56},{24,0},{32,8},{40,16},{48,24},{56,32},{1,41}... | collective-permute-start | bytes 393224 | tf_op jit(solution)/shard_map/ppermute | solution.py:161
  25.3 3.6 %shard_map.69 = (f32[128,2048]{1,0:T(8,128)S(1)}, f32[128,2048]{1,0:T(8,128)S(1)}, f32[128,2048]{1,0:T(8,128)S(1)}) custom-call(bf16[128,2048]{1,0:T(8,128)(2,1)S(1)} %copy-done, bf16[128,2048]{1,0:T(8,128)(2,1)S(1)} %copy-done.1, bf16[128,2048]{1,0:T(8,128)(2,1)S(1)} %copy-done.2, bf16[128,2048]{1,0:T(8,128)(2,1)S(1)} %copy-done.3), custom_call_target="tpu_custom_call" | custom-call | flops 335544320 | bytes 5242880 | tf_op jit(solution)/shard_map/pallas_call | solution.py:207
  29.0 1.3 %collective-permute-done.5.refs_5_ = f32[256,128]{1,0:T(8,128)S(1)} collective-permute-done((f32[256,128]{1,0:T(8,128)S(1)}, f32[256,128]{1,0:T(8,128)S(1)}, u32[]{:S(2)}, u32[]{:S(2)}) %collective-permute-start.5) | collective-permute-done | bytes 131104 | tf_op jit(solution)/shard_map/ppermute | solution.py:161
  30.3 6.4 %collective-permute-done.6.refs_6_ = f32[256,128]{1,0:T(8,128)S(1)} collective-permute-done((f32[256,128]{1,0:T(8,128)S(1)}, f32[256,128]{1,0:T(8,128)S(1)}, u32[]{:S(2)}, u32[]{:S(2)}) %collective-permute-start.6) | collective-permute-done | bytes 131104 | tf_op jit(solution)/shard_map/ppermute | solution.py:161
  37.3 2.4 %collective-permute-start.10 = (f32[256,128]{1,0:T(8,128)S(1)}, f32[256,128]{1,0:T(8,128)S(1)}, u32[]{:S(2)}, u32[]{:S(2)}) collective-permute-start(f32[256,128]{1,0:T(8,128)S(1)} %shard_map.70.refs_0_), channel_id=1, source_target_pairs={{0,192},{64,0},{128,64},{192,128},{1,193},{65,1},{129,65},{193,129... | collective-permute-start | bytes 393224 | tf_op jit(solution)/shard_map/ppermute | solution.py:161
  40.8 4.5 %collective-permute-done.10.refs_3_.refs_10_ = f32[256,128]{1,0:T(8,128)S(1)} collective-permute-done((f32[256,128]{1,0:T(8,128)S(1)}, f32[256,128]{1,0:T(8,128)S(1)}, u32[]{:S(2)}, u32[]{:S(2)}) %collective-permute-start.10) | collective-permute-done | bytes 131104 | tf_op jit(solution)/shard_map/ppermute | solution.py:161
  45.3 0.8 collective-permute-done.9.refs_2_.refs_9_
  46.0 3.5 %collective-permute-done.8.refs_1_.refs_8_ = f32[256,128]{1,0:T(8,128)S(1)} collective-permute-done((f32[256,128]{1,0:T(8,128)S(1)}, f32[256,128]{1,0:T(8,128)S(1)}, u32[]{:S(2)}, u32[]{:S(2)}) %collective-permute-start.8) | collective-permute-done | bytes 131104 | tf_op jit(solution)/shard_map/ppermute | solution.py:161
  49.5 1.3 %collective-permute-start.14 = (f32[256,128]{1,0:T(8,128)S(1)}, f32[256,128]{1,0:T(8,128)S(1)}, u32[]{:S(2)}, u32[]{:S(2)}) collective-permute-start(f32[256,128]{1,0:T(8,128)S(1)} %shard_map.71), channel_id=1, source_target_pairs={{0,3},{7,4},{8,11},{15,12},{16,19},{23,20},{24,27},{31,28},{32,35}... | collective-permute-start | bytes 393224 | tf_op jit(solution)/shard_map/ppermute | solution.py:167
  50.8 1.3 %collective-permute-start.13 = (f32[256,128]{1,0:T(8,128)S(1)}, f32[256,128]{1,0:T(8,128)S(1)}, u32[]{:S(2)}, u32[]{:S(2)}) collective-permute-start(f32[256,128]{1,0:T(8,128)S(1)} %shard_map.71), channel_id=1, source_target_pairs={{0,2},{1,3},{6,4},{7,5},{8,10},{9,11},{14,12},{15,13},{16,18},{17,... | collective-permute-start | bytes 393224 | tf_op jit(solution)/shard_map/ppermute | solution.py:167
  52.1 1.3 %collective-permute-start.12 = (f32[256,128]{1,0:T(8,128)S(1)}, f32[256,128]{1,0:T(8,128)S(1)}, u32[]{:S(2)}, u32[]{:S(2)}) collective-permute-start(f32[256,128]{1,0:T(8,128)S(1)} %shard_map.71), channel_id=1, source_target_pairs={{0,1},{1,2},{2,3},{5,4},{6,5},{7,6},{8,9},{9,10},{10,11},{13,12},{... | collective-permute-start | bytes 393224 | tf_op jit(solution)/shard_map/ppermute | solution.py:167
  53.4 3.0 %collective-permute-done.14.refs_13_ = f32[256,128]{1,0:T(8,128)S(1)} collective-permute-done((f32[256,128]{1,0:T(8,128)S(1)}, f32[256,128]{1,0:T(8,128)S(1)}, u32[]{:S(2)}, u32[]{:S(2)}) %collective-permute-start.14) | collective-permute-done | bytes 131104 | tf_op jit(solution)/shard_map/ppermute | solution.py:167
  56.4 1.6 %collective-permute-done.13.refs_12_ = f32[256,128]{1,0:T(8,128)S(1)} collective-permute-done((f32[256,128]{1,0:T(8,128)S(1)}, f32[256,128]{1,0:T(8,128)S(1)}, u32[]{:S(2)}, u32[]{:S(2)}) %collective-permute-start.13) | collective-permute-done | bytes 131104 | tf_op jit(solution)/shard_map/ppermute | solution.py:167
  58.0 0.8 shard_map.72
  58.9 6.5 %collective-permute-start.15 = (f32[256,128]{1,0:T(8,128)S(1)}, f32[256,128]{1,0:T(8,128)S(1)}, u32[]{:S(2)}, u32[]{:S(2)}) collective-permute-start(f32[256,128]{1,0:T(8,128)S(1)} %get-tuple-element.72), channel_id=1, source_target_pairs={{0,32},{8,40},{16,48},{24,56},{32,0},{40,8},{48,16},{56,24},{1,33}... | collective-permute-start | bytes 393224 | tf_op jit(solution)/shard_map/ppermute | solution.py:161
  65.3 2.7 %collective-permute-start.17 = (f32[256,128]{1,0:T(8,128)S(1)}, f32[256,128]{1,0:T(8,128)S(1)}, u32[]{:S(2)}, u32[]{:S(2)}) collective-permute-start(f32[256,128]{1,0:T(8,128)S(1)} %get-tuple-element.74), channel_id=1, source_target_pairs={{0,56},{8,0},{16,8},{24,16},{32,24},{40,32},{48,40},{56,48},{1,57}... | collective-permute-start | bytes 393224 | tf_op jit(solution)/shard_map/ppermute | solution.py:161
  68.5 3.1 %collective-permute-start.19 = (f32[256,128]{1,0:T(8,128)S(1)}, f32[256,128]{1,0:T(8,128)S(1)}, u32[]{:S(2)}, u32[]{:S(2)}) collective-permute-start(f32[256,128]{1,0:T(8,128)S(1)} %get-tuple-element.76), channel_id=1, source_target_pairs={{0,48},{8,56},{16,0},{24,8},{32,16},{40,24},{48,32},{56,40},{1,49}... | collective-permute-start | bytes 393224 | tf_op jit(solution)/shard_map/ppermute | solution.py:161
  71.6 1.5 %collective-permute-start.20 = (f32[256,128]{1,0:T(8,128)S(1)}, f32[256,128]{1,0:T(8,128)S(1)}, u32[]{:S(2)}, u32[]{:S(2)}) collective-permute-start(f32[256,128]{1,0:T(8,128)S(1)} %get-tuple-element.77), channel_id=1, source_target_pairs={{0,24},{8,32},{16,40},{24,48},{32,56},{40,0},{48,8},{56,16},{1,25}... | collective-permute-start | bytes 393224 | tf_op jit(solution)/shard_map/ppermute | solution.py:161
  73.1 0.8 collective-permute-done.16.refs_10_
  73.9 2.1 %collective-permute-start.21 = (f32[256,128]{1,0:T(8,128)S(1)}, f32[256,128]{1,0:T(8,128)S(1)}, u32[]{:S(2)}, u32[]{:S(2)}) collective-permute-start(f32[256,128]{1,0:T(8,128)S(1)} %get-tuple-element.78), channel_id=1, source_target_pairs={{0,40},{8,48},{16,56},{24,0},{32,8},{40,16},{48,24},{56,32},{1,41}... | collective-permute-start | bytes 393224 | tf_op jit(solution)/shard_map/ppermute | solution.py:161
  76.1 5.2 %collective-permute-start.22 = (f32[256,128]{1,0:T(8,128)S(1)}, f32[256,128]{1,0:T(8,128)S(1)}, u32[]{:S(2)}, u32[]{:S(2)}) collective-permute-start(f32[256,128]{1,0:T(8,128)S(1)} %get-tuple-element.71.refs_8_), channel_id=1, source_target_pairs={{0,4},{4,0},{1,5},{5,1},{2,6},{6,2},{3,7},{7,3},{8,12},{12,8},{9,1... | collective-permute-start | bytes 393224 | tf_op jit(solution)/shard_map/ppermute | solution.py:251
  81.3 5.2 %collective-permute-start.23 = (f32[256,128]{1,0:T(8,128)S(1)}, f32[256,128]{1,0:T(8,128)S(1)}, u32[]{:S(2)}, u32[]{:S(2)}) collective-permute-start(f32[256,128]{1,0:T(8,128)S(1)} %collective-permute-done.15.refs_9_), channel_id=1, source_target_pairs={{0,4},{4,0},{1,5},{5,1},{2,6},{6,2},{3,7},{7,3},{8,12},{12,8},{9,1... | collective-permute-start | bytes 393224 | tf_op jit(solution)/shard_map/ppermute | solution.py:251
  86.5 1.8 %collective-permute-done.20.refs_14_ = f32[256,128]{1,0:T(8,128)S(1)} collective-permute-done((f32[256,128]{1,0:T(8,128)S(1)}, f32[256,128]{1,0:T(8,128)S(1)}, u32[]{:S(2)}, u32[]{:S(2)}) %collective-permute-start.20) | collective-permute-done | bytes 131104 | tf_op jit(solution)/shard_map/ppermute | solution.py:161
  88.3 2.1 %collective-permute-start.25 = (f32[256,128]{1,0:T(8,128)S(1)}, f32[256,128]{1,0:T(8,128)S(1)}, u32[]{:S(2)}, u32[]{:S(2)}) collective-permute-start(f32[256,128]{1,0:T(8,128)S(1)} %collective-permute-done.17.refs_11_), channel_id=1, source_target_pairs={{0,4},{4,0},{1,5},{5,1},{2,6},{6,2},{3,7},{7,3},{8,12},{12,8},{9,1... | collective-permute-start | bytes 393224 | tf_op jit(solution)/shard_map/ppermute | solution.py:251
  92.4 2.5 %shard_map.73 = (bf16[128,2048]{1,0:T(8,128)(2,1)}, bf16[128,2048]{1,0:T(8,128)(2,1)}, bf16[128,2048]{1,0:T(8,128)(2,1)}) custom-call(s32[3]{0:T(128)S(1)} %pad_add_fusion.places, bf16[128,2048]{1,0:T(8,128)(2,1)S(1)} %copy-done, bf16[128,2048]{1,0:T(8,128)(2,1)S(1)} %copy-done.1, bf16[128,2048]{1,0:T(8,128)(2,1)S(1)} %copy-done.2, ...), custom_call_target="tpu_custom_call" | custom-call | flops 201326592 | bytes 9961472 | tf_op jit(solution)/shard_map/pallas_call | solution.py:252
  (44 shorter events, 5.2 us)
Async XLA Ops:
  3.6 5.6 %collective-permute-start = (f32[8,256,128]{2,1,0:T(8,128)S(1)}, f32[8,256,128]{2,1,0:T(8,128)S(1)}, u32[]{:S(2)}, u32[]{:S(2)}) collective-permute-start(f32[8,256,128]{2,1,0:T(8,128)S(1)} %get-tuple-element.42), channel_id=1, source_target_pairs={{0,4},{4,0},{1,5},{5,1},{2,6},{6,2},{3,7},{7,3},{8,12},{12,8},{9,1... | collective-permute-start | bytes 3145736 | tf_op jit(solution)/shard_map/ppermute | solution.py:206
  9.2 16.1 %copy-start.2 = (bf16[128,2048]{1,0:T(8,128)(2,1)S(1)}, bf16[128,2048]{1,0:T(8,128)(2,1)}, u32[]{:S(2)}) copy-start(bf16[128,2048]{1,0:T(8,128)(2,1)} %refs_2_.1) | copy-start | bytes 1572868
  9.2 16.1 %copy-start.3 = (bf16[128,2048]{1,0:T(8,128)(2,1)S(1)}, bf16[128,2048]{1,0:T(8,128)(2,1)}, u32[]{:S(2)}) copy-start(bf16[128,2048]{1,0:T(8,128)(2,1)} %refs_3_.1) | copy-start | bytes 1572868
  9.3 11.5 %collective-permute-start.1 = (f32[256,128]{1,0:T(8,128)S(1)}, f32[256,128]{1,0:T(8,128)S(1)}, u32[]{:S(2)}, u32[]{:S(2)}) collective-permute-start(f32[256,128]{1,0:T(8,128)S(1)} %get-tuple-element.44), channel_id=1, source_target_pairs={{0,32},{8,40},{16,48},{24,56},{32,0},{40,8},{48,16},{56,24},{1,33}... | collective-permute-start | bytes 393224 | tf_op jit(solution)/shard_map/ppermute | solution.py:161
  14.6 9.6 %collective-permute-start.2 = (f32[256,128]{1,0:T(8,128)S(1)}, f32[256,128]{1,0:T(8,128)S(1)}, u32[]{:S(2)}, u32[]{:S(2)}) collective-permute-start(f32[256,128]{1,0:T(8,128)S(1)} %get-tuple-element.45), channel_id=1, source_target_pairs={{0,8},{8,16},{16,24},{24,32},{32,40},{40,48},{48,56},{56,0},{1,9},... | collective-permute-start | bytes 393224 | tf_op jit(solution)/shard_map/ppermute | solution.py:161
  15.3 13.6 %collective-permute-start.3 = (f32[256,128]{1,0:T(8,128)S(1)}, f32[256,128]{1,0:T(8,128)S(1)}, u32[]{:S(2)}, u32[]{:S(2)}) collective-permute-start(f32[256,128]{1,0:T(8,128)S(1)} %get-tuple-element.46), channel_id=1, source_target_pairs={{0,56},{8,0},{16,8},{24,16},{32,24},{40,32},{48,40},{56,48},{1,57}... | collective-permute-start | bytes 393224 | tf_op jit(solution)/shard_map/ppermute | solution.py:161
  17.2 11.7 %collective-permute-start.4 = (f32[256,128]{1,0:T(8,128)S(1)}, f32[256,128]{1,0:T(8,128)S(1)}, u32[]{:S(2)}, u32[]{:S(2)}) collective-permute-start(f32[256,128]{1,0:T(8,128)S(1)} %get-tuple-element.47), channel_id=1, source_target_pairs={{0,16},{8,24},{16,32},{24,40},{32,48},{40,56},{48,0},{56,8},{1,17}... | collective-permute-start | bytes 393224 | tf_op jit(solution)/shard_map/ppermute | solution.py:161
  17.2 13.0 %collective-permute-start.5 = (f32[256,128]{1,0:T(8,128)S(1)}, f32[256,128]{1,0:T(8,128)S(1)}, u32[]{:S(2)}, u32[]{:S(2)}) collective-permute-start(f32[256,128]{1,0:T(8,128)S(1)} %get-tuple-element.48), channel_id=1, source_target_pairs={{0,48},{8,56},{16,0},{24,8},{32,16},{40,24},{48,32},{56,40},{1,49}... | collective-permute-start | bytes 393224 | tf_op jit(solution)/shard_map/ppermute | solution.py:161
  20.8 15.8 %collective-permute-start.6 = (f32[256,128]{1,0:T(8,128)S(1)}, f32[256,128]{1,0:T(8,128)S(1)}, u32[]{:S(2)}, u32[]{:S(2)}) collective-permute-start(f32[256,128]{1,0:T(8,128)S(1)} %get-tuple-element.49), channel_id=1, source_target_pairs={{0,24},{8,32},{16,40},{24,48},{32,56},{40,0},{48,8},{56,16},{1,25}... | collective-permute-start | bytes 393224 | tf_op jit(solution)/shard_map/ppermute | solution.py:161
  24.2 12.5 %collective-permute-start.7 = (f32[256,128]{1,0:T(8,128)S(1)}, f32[256,128]{1,0:T(8,128)S(1)}, u32[]{:S(2)}, u32[]{:S(2)}) collective-permute-start(f32[256,128]{1,0:T(8,128)S(1)} %get-tuple-element.50), channel_id=1, source_target_pairs={{0,40},{8,48},{16,56},{24,0},{32,8},{40,16},{48,24},{56,32},{1,41}... | collective-permute-start | bytes 393224 | tf_op jit(solution)/shard_map/ppermute | solution.py:161
  36.7 12.7 %collective-permute-start.11 = (f32[8,256,128]{2,1,0:T(8,128)S(1)}, f32[8,256,128]{2,1,0:T(8,128)S(1)}, u32[]{:S(2)}, u32[]{:S(2)}) collective-permute-start(f32[8,256,128]{2,1,0:T(8,128)S(1)} %get-tuple-element.66.keep), channel_id=1, source_target_pairs={{0,4},{4,0},{1,5},{5,1},{2,6},{6,2},{3,7},{7,3},{8,12},{12,8},{9,1... | collective-permute-start | bytes 3145736 | tf_op jit(solution)/shard_map/ppermute | solution.py:236
  37.3 7.9 %collective-permute-start.10 = (f32[256,128]{1,0:T(8,128)S(1)}, f32[256,128]{1,0:T(8,128)S(1)}, u32[]{:S(2)}, u32[]{:S(2)}) collective-permute-start(f32[256,128]{1,0:T(8,128)S(1)} %shard_map.70.refs_0_), channel_id=1, source_target_pairs={{0,192},{64,0},{128,64},{192,128},{1,193},{65,1},{129,65},{193,129... | collective-permute-start | bytes 393224 | tf_op jit(solution)/shard_map/ppermute | solution.py:161
  39.8 6.3 %collective-permute-start.9 = (f32[256,128]{1,0:T(8,128)S(1)}, f32[256,128]{1,0:T(8,128)S(1)}, u32[]{:S(2)}, u32[]{:S(2)}) collective-permute-start(f32[256,128]{1,0:T(8,128)S(1)} %shard_map.70.refs_0_), channel_id=1, source_target_pairs={{0,128},{64,192},{128,0},{192,64},{1,129},{65,193},{129,1},{193,65... | collective-permute-start | bytes 393224 | tf_op jit(solution)/shard_map/ppermute | solution.py:161
  40.1 9.4 %collective-permute-start.8 = (f32[256,128]{1,0:T(8,128)S(1)}, f32[256,128]{1,0:T(8,128)S(1)}, u32[]{:S(2)}, u32[]{:S(2)}) collective-permute-start(f32[256,128]{1,0:T(8,128)S(1)} %shard_map.70.refs_0_), channel_id=1, source_target_pairs={{0,64},{64,128},{128,192},{192,0},{1,65},{65,129},{129,193},{193,1... | collective-permute-start | bytes 393224 | tf_op jit(solution)/shard_map/ppermute | solution.py:161
  49.5 6.9 %collective-permute-start.14 = (f32[256,128]{1,0:T(8,128)S(1)}, f32[256,128]{1,0:T(8,128)S(1)}, u32[]{:S(2)}, u32[]{:S(2)}) collective-permute-start(f32[256,128]{1,0:T(8,128)S(1)} %shard_map.71), channel_id=1, source_target_pairs={{0,3},{7,4},{8,11},{15,12},{16,19},{23,20},{24,27},{31,28},{32,35}... | collective-permute-start | bytes 393224 | tf_op jit(solution)/shard_map/ppermute | solution.py:167
  50.8 7.2 %collective-permute-start.13 = (f32[256,128]{1,0:T(8,128)S(1)}, f32[256,128]{1,0:T(8,128)S(1)}, u32[]{:S(2)}, u32[]{:S(2)}) collective-permute-start(f32[256,128]{1,0:T(8,128)S(1)} %shard_map.71), channel_id=1, source_target_pairs={{0,2},{1,3},{6,4},{7,5},{8,10},{9,11},{14,12},{15,13},{16,18},{17,... | collective-permute-start | bytes 393224 | tf_op jit(solution)/shard_map/ppermute | solution.py:167
  52.1 5.9 %collective-permute-start.12 = (f32[256,128]{1,0:T(8,128)S(1)}, f32[256,128]{1,0:T(8,128)S(1)}, u32[]{:S(2)}, u32[]{:S(2)}) collective-permute-start(f32[256,128]{1,0:T(8,128)S(1)} %shard_map.71), channel_id=1, source_target_pairs={{0,1},{1,2},{2,3},{5,4},{6,5},{7,6},{8,9},{9,10},{10,11},{13,12},{... | collective-permute-start | bytes 393224 | tf_op jit(solution)/shard_map/ppermute | solution.py:167
  58.9 12.7 %collective-permute-start.15 = (f32[256,128]{1,0:T(8,128)S(1)}, f32[256,128]{1,0:T(8,128)S(1)}, u32[]{:S(2)}, u32[]{:S(2)}) collective-permute-start(f32[256,128]{1,0:T(8,128)S(1)} %get-tuple-element.72), channel_id=1, source_target_pairs={{0,32},{8,40},{16,48},{24,56},{32,0},{40,8},{48,16},{56,24},{1,33}... | collective-permute-start | bytes 393224 | tf_op jit(solution)/shard_map/ppermute | solution.py:161
  65.3 8.6 %collective-permute-start.16 = (f32[256,128]{1,0:T(8,128)S(1)}, f32[256,128]{1,0:T(8,128)S(1)}, u32[]{:S(2)}, u32[]{:S(2)}) collective-permute-start(f32[256,128]{1,0:T(8,128)S(1)} %get-tuple-element.73), channel_id=1, source_target_pairs={{0,8},{8,16},{16,24},{24,32},{32,40},{40,48},{48,56},{56,0},{1,9},... | collective-permute-start | bytes 393224 | tf_op jit(solution)/shard_map/ppermute | solution.py:161
  65.3 10.7 %collective-permute-start.17 = (f32[256,128]{1,0:T(8,128)S(1)}, f32[256,128]{1,0:T(8,128)S(1)}, u32[]{:S(2)}, u32[]{:S(2)}) collective-permute-start(f32[256,128]{1,0:T(8,128)S(1)} %get-tuple-element.74), channel_id=1, source_target_pairs={{0,56},{8,0},{16,8},{24,16},{32,24},{40,32},{48,40},{56,48},{1,57}... | collective-permute-start | bytes 393224 | tf_op jit(solution)/shard_map/ppermute | solution.py:161
  68.0 13.2 %collective-permute-start.18 = (f32[256,128]{1,0:T(8,128)S(1)}, f32[256,128]{1,0:T(8,128)S(1)}, u32[]{:S(2)}, u32[]{:S(2)}) collective-permute-start(f32[256,128]{1,0:T(8,128)S(1)} %get-tuple-element.75), channel_id=1, source_target_pairs={{0,16},{8,24},{16,32},{24,40},{32,48},{40,56},{48,0},{56,8},{1,17}... | collective-permute-start | bytes 393224 | tf_op jit(solution)/shard_map/ppermute | solution.py:161
  68.5 18.0 %collective-permute-start.19 = (f32[256,128]{1,0:T(8,128)S(1)}, f32[256,128]{1,0:T(8,128)S(1)}, u32[]{:S(2)}, u32[]{:S(2)}) collective-permute-start(f32[256,128]{1,0:T(8,128)S(1)} %get-tuple-element.76), channel_id=1, source_target_pairs={{0,48},{8,56},{16,0},{24,8},{32,16},{40,24},{48,32},{56,40},{1,49}... | collective-permute-start | bytes 393224 | tf_op jit(solution)/shard_map/ppermute | solution.py:161
  71.6 16.6 %collective-permute-start.20 = (f32[256,128]{1,0:T(8,128)S(1)}, f32[256,128]{1,0:T(8,128)S(1)}, u32[]{:S(2)}, u32[]{:S(2)}) collective-permute-start(f32[256,128]{1,0:T(8,128)S(1)} %get-tuple-element.77), channel_id=1, source_target_pairs={{0,24},{8,32},{16,40},{24,48},{32,56},{40,0},{48,8},{56,16},{1,25}... | collective-permute-start | bytes 393224 | tf_op jit(solution)/shard_map/ppermute | solution.py:161
  73.9 16.4 %collective-permute-start.21 = (f32[256,128]{1,0:T(8,128)S(1)}, f32[256,128]{1,0:T(8,128)S(1)}, u32[]{:S(2)}, u32[]{:S(2)}) collective-permute-start(f32[256,128]{1,0:T(8,128)S(1)} %get-tuple-element.78), channel_id=1, source_target_pairs={{0,40},{8,48},{16,56},{24,0},{32,8},{40,16},{48,24},{56,32},{1,41}... | collective-permute-start | bytes 393224 | tf_op jit(solution)/shard_map/ppermute | solution.py:161
  76.1 14.3 %collective-permute-start.22 = (f32[256,128]{1,0:T(8,128)S(1)}, f32[256,128]{1,0:T(8,128)S(1)}, u32[]{:S(2)}, u32[]{:S(2)}) collective-permute-start(f32[256,128]{1,0:T(8,128)S(1)} %get-tuple-element.71.refs_8_), channel_id=1, source_target_pairs={{0,4},{4,0},{1,5},{5,1},{2,6},{6,2},{3,7},{7,3},{8,12},{12,8},{9,1... | collective-permute-start | bytes 393224 | tf_op jit(solution)/shard_map/ppermute | solution.py:251
  81.3 9.6 %collective-permute-start.23 = (f32[256,128]{1,0:T(8,128)S(1)}, f32[256,128]{1,0:T(8,128)S(1)}, u32[]{:S(2)}, u32[]{:S(2)}) collective-permute-start(f32[256,128]{1,0:T(8,128)S(1)} %collective-permute-done.15.refs_9_), channel_id=1, source_target_pairs={{0,4},{4,0},{1,5},{5,1},{2,6},{6,2},{3,7},{7,3},{8,12},{12,8},{9,1... | collective-permute-start | bytes 393224 | tf_op jit(solution)/shard_map/ppermute | solution.py:251
  86.5 4.5 %collective-permute-start.24 = (f32[256,128]{1,0:T(8,128)S(1)}, f32[256,128]{1,0:T(8,128)S(1)}, u32[]{:S(2)}, u32[]{:S(2)}) collective-permute-start(f32[256,128]{1,0:T(8,128)S(1)} %collective-permute-done.16.refs_10_), channel_id=1, source_target_pairs={{0,4},{4,0},{1,5},{5,1},{2,6},{6,2},{3,7},{7,3},{8,12},{12,8},{9,1... | collective-permute-start | bytes 393224 | tf_op jit(solution)/shard_map/ppermute | solution.py:251
  88.3 3.2 %collective-permute-start.25 = (f32[256,128]{1,0:T(8,128)S(1)}, f32[256,128]{1,0:T(8,128)S(1)}, u32[]{:S(2)}, u32[]{:S(2)}) collective-permute-start(f32[256,128]{1,0:T(8,128)S(1)} %collective-permute-done.17.refs_11_), channel_id=1, source_target_pairs={{0,4},{4,0},{1,5},{5,1},{2,6},{6,2},{3,7},{7,3},{8,12},{12,8},{9,1... | collective-permute-start | bytes 393224 | tf_op jit(solution)/shard_map/ppermute | solution.py:251
  90.4 1.3 %collective-permute-start.26 = (f32[256,128]{1,0:T(8,128)S(1)}, f32[256,128]{1,0:T(8,128)S(1)}, u32[]{:S(2)}, u32[]{:S(2)}) collective-permute-start(f32[256,128]{1,0:T(8,128)S(1)} %collective-permute-done.18.refs_12_), channel_id=1, source_target_pairs={{0,4},{4,0},{1,5},{5,1},{2,6},{6,2},{3,7},{7,3},{8,12},{12,8},{9,1... | collective-permute-start | bytes 393224 | tf_op jit(solution)/shard_map/ppermute | solution.py:251
  90.4 1.5 %collective-permute-start.27 = (f32[256,128]{1,0:T(8,128)S(1)}, f32[256,128]{1,0:T(8,128)S(1)}, u32[]{:S(2)}, u32[]{:S(2)}) collective-permute-start(f32[256,128]{1,0:T(8,128)S(1)} %collective-permute-done.19.refs_13_), channel_id=1, source_target_pairs={{0,4},{4,0},{1,5},{5,1},{2,6},{6,2},{3,7},{7,3},{8,12},{12,8},{9,1... | collective-permute-start | bytes 393224 | tf_op jit(solution)/shard_map/ppermute | solution.py:251
  90.9 1.3 %collective-permute-start.28 = (f32[256,128]{1,0:T(8,128)S(1)}, f32[256,128]{1,0:T(8,128)S(1)}, u32[]{:S(2)}, u32[]{:S(2)}) collective-permute-start(f32[256,128]{1,0:T(8,128)S(1)} %collective-permute-done.20.refs_14_), channel_id=1, source_target_pairs={{0,4},{4,0},{1,5},{5,1},{2,6},{6,2},{3,7},{7,3},{8,12},{12,8},{9,1... | collective-permute-start | bytes 393224 | tf_op jit(solution)/shard_map/ppermute | solution.py:251
  91.0 1.4 %collective-permute-start.29 = (f32[256,128]{1,0:T(8,128)S(1)}, f32[256,128]{1,0:T(8,128)S(1)}, u32[]{:S(2)}, u32[]{:S(2)}) collective-permute-start(f32[256,128]{1,0:T(8,128)S(1)} %collective-permute-done.21.refs_15_), channel_id=1, source_target_pairs={{0,4},{4,0},{1,5},{5,1},{2,6},{6,2},{3,7},{7,3},{8,12},{12,8},{9,1... | collective-permute-start | bytes 393224 | tf_op jit(solution)/shard_map/ppermute | solution.py:251
  (2 other events, 32.2 us)

commit v4 on v3

--- a/solution.py
+++ b/solution.py
@@ -26,6 +26,10 @@
 
 def chunk_lanes(index, width):
     return pl.ds(pl.multiple_of(index * width, width), width)
+
+
+def moved(forward, place, step, count):
+    return jnp.where(forward, lax.rem(place + step, count), lax.rem(place + count - step, count))
 
 
 def states_kernel(places, query, key, value, gradient, keep, send, held, sems):
@@ -48,11 +52,14 @@
         for h in range(part // HEAD):
             lanes = pl.ds(h * HEAD, HEAD)
             chunk, row = divmod(n * part + h * HEAD, width)
-            slot = lax.rem(chunk + slots - z, slots)
+            ahead = lax.rem(chunk + slots - z, slots)
+            behind = lax.rem(z + slots - chunk, slots)
+            mine = jnp.where(first, ahead, behind)
+            theirs = jnp.where(first, behind, ahead)
             kv = contract(held[0, n, :, lanes], held[1, n, :, lanes], 0, 0)
             qo = contract(held[2, n, :, lanes], held[3, n, :, lanes], 0, 0)
-            keep[slot, pl.ds(row, HEAD), :] = jnp.where(first, kv, qo)
-            send[slot, pl.ds(row, HEAD), :] = jnp.where(first, qo, kv)
+            keep[mine, pl.ds(row, HEAD), :] = jnp.where(first, kv, qo)
+            send[theirs, pl.ds(row, HEAD), :] = jnp.where(first, qo, kv)
 
 
 def inner_kernel(query, key, value, gradient, gq, gk, gv):
@@ -91,21 +98,21 @@
     held = refs[-1]
     first = places[0] == 0
     z = places[1]
-    row = places[2]
+    row = jnp.where(first, places[2], rows - 1 - places[2])
     total = planes[0][...]
     for plane in planes[1:]:
         total = total + plane[...]
     for step, part in enumerate(around, 1):
-        total = total + jnp.where((row >= step) == first, part[...], 0.0)
+        total = total + jnp.where(row >= step, part[...], 0.0)
     for offset, source in zip(order, sources, strict=True):
-        held[lax.rem(z + slots - offset, slots)] = source[...]
+        held[moved(first, z, slots - offset, slots)] = source[...]
     for n in range(slots):
         place = jnp.where(first, n, slots - 1 - n)
         piece = held[place]
         held[place] = total
         total = total + piece
     for offset, out in zip(order, outs, strict=True):
-        out[...] = held[lax.rem(z + offset, slots)]
+        out[...] = held[moved(first, z, offset, slots)]
 
 
 def outputs_kernel(order, scale, places, *refs):
@@ -122,11 +129,12 @@
     width = own[0].shape[0]
     copies = []
     for n, offset in enumerate(order):
-        chunk = lax.rem(z + slots - offset, slots)
+        chunk = moved(first, z, slots - offset, slots)
+        mirror = order.index((slots - offset) % slots)
         for h in range(width // HEAD):
             rows = pl.ds(h * HEAD, HEAD)
             mine = own[n][rows, :]
-            theirs = received[n][rows, :] + other[(slots - offset) % slots, rows, :]
+            theirs = received[mirror][rows, :] + other[offset, rows, :]
             prefix = jnp.where(first, mine, theirs).astype(BF16)
             suffix = jnp.where(first, theirs, mine).astype(BF16)
             lanes = chunk_lanes(chunk * (width // HEAD) + h, HEAD)
@@ -158,7 +166,11 @@
 
 
 def turn(array, axis, count, step):
-    return lax.ppermute(array, axis, [(i, (i + step) % count) for i in range(count)])
+    steps = (step, count - step)
+    pairs = [
+        (2 * i + c, 2 * ((i + steps[c]) % count) + c) for i in range(count) for c in range(2)
+    ]
+    return lax.ppermute(array, (axis, "c"), pairs)
 
 
 def onward(array, axis, count, step):

time: 96.2 us -> 93.4 us (0.971)
  waiting for transfers between devices: 30.3 us -> 21.7 us
  starting transfers between devices: 53.8 us -> 60.2 us
    ppermute x17, waiting for transfers between devices: 22.3 us -> 13.8 us  [turn(): return lax.ppermute(array, (axis, 'c'), pairs)]
    ppermute x8, starting transfers between devices: 13.5 us -> 19.3 us  [per_device(): theirs = [lax.ppermute(part, 'c', swap) for part in own]]
  transfers between devices with their start and end apart: 30 -> 30, of which waited for: 15 -> 12; matrix products, arithmetic and copies ran while one was open for 0% -> 0% of each run, Pallas kernels for 4% -> 4%
where the time goes in v4:
time: 93.4 us; the launch traced here: 93 us
  starting transfers between devices  60.2 us (64%)
  waiting for transfers between devices  21.7 us (23%)
  Pallas kernels  10 us (11%)
    ppermute x17, starting transfers between devices, turn(): return lax.ppermute(array, (axis, 'c'), pairs)  33 us
    ppermute x8, starting transfers between devices, per_device(): theirs = [lax.ppermute(part, 'c', swap) for part in own]  19.3 us
    ppermute x17, waiting for transfers between devices, turn(): return lax.ppermute(array, (axis, 'c'), pairs)  13.8 us
    ppermute x3, waiting for transfers between devices, onward(): return lax.ppermute(array, ('c', axis), pairs)  4.62 us
    ppermute x3, starting transfers between devices, onward(): return lax.ppermute(array, ('c', axis), pairs)  3.88 us
    pallas_call x1, Pallas kernels, per_device(): call(inner_kernel, [VMEM] * 4, [VMEM] * 3, [inner_shape] * 3, 5 * product...  3.62 us
    ppermute x1, starting transfers between devices, per_device(): received = lax.ppermute(send, 'c', swap)  3.33 us
    pallas_call x1, Pallas kernels, per_device(): call(states_kernel, [SMEM] + [HBM] * 4, [VMEM] * 2, [state_shape] * 2, 2...  2.85 us
  transfers between devices with their start and end apart: 30, of which 12 were waited for; matrix products, arithmetic and copies ran while one was open for 0% of the time, Pallas kernels for 4%

profile of v4, /device:TPU:1, one launch (start us, length us, event | category | flops | bytes accessed | tf_op | source)
XLA Modules:
  0.0 93.0 jit_solution(17544745130278296397)
XLA Ops:
  0.7 2.8 %shard_map.67 = (f32[8,256,128]{2,1,0:T(8,128)S(1)}, f32[8,256,128]{2,1,0:T(8,128)S(1)}) custom-call(s32[3]{0:T(128)S(1)} %pad_add_fusion.places, bf16[128,2048]{1,0:T(8,128)(2,1)} %refs_0_.1, bf16[128,2048]{1,0:T(8,128)(2,1)} %refs_1_.1, bf16[128,2048]{1,0:T(8,128)(2,1)} %refs_2_.1, bf16[128,2048]{1,0:T(8,128)(2,1)} %refs_3_.1), custom_call_target="tpu_custom_call" | custom-call | flops 134217728 | bytes 4194304 | tf_op jit(solution)/shard_map/pallas_call | solution.py:206
  3.6 3.3 %collective-permute-start = (f32[8,256,128]{2,1,0:T(8,128)S(1)}, f32[8,256,128]{2,1,0:T(8,128)S(1)}, u32[]{:S(2)}, u32[]{:S(2)}) collective-permute-start(f32[8,256,128]{2,1,0:T(8,128)S(1)} %get-tuple-element.42), channel_id=1, source_target_pairs={{0,4},{4,0},{1,5},{5,1},{2,6},{6,2},{3,7},{7,3},{8,12},{12,8},{9,1... | collective-permute-start | bytes 3145736 | tf_op jit(solution)/shard_map/ppermute | solution.py:218
  6.9 2.3 %collective-permute-done.received = f32[8,256,128]{2,1,0:T(8,128)S(1)} collective-permute-done((f32[8,256,128]{2,1,0:T(8,128)S(1)}, f32[8,256,128]{2,1,0:T(8,128)S(1)}, u32[]{:S(2)}, u32[]{:S(2)}) %collective-permute-start) | collective-permute-done | bytes 1048608 | tf_op jit(solution)/shard_map/ppermute | solution.py:218
  9.3 5.3 %collective-permute-start.1 = (f32[256,128]{1,0:T(8,128)S(1)}, f32[256,128]{1,0:T(8,128)S(1)}, u32[]{:S(2)}, u32[]{:S(2)}) collective-permute-start(f32[256,128]{1,0:T(8,128)S(1)} %get-tuple-element.44), channel_id=1, source_target_pairs={{0,32},{4,36},{8,40},{12,44},{16,48},{20,52},{24,56},{28,60},{32,0... | collective-permute-start | bytes 393224 | tf_op jit(solution)/shard_map/ppermute | solution.py:173
  14.6 1.5 %collective-permute-start.3 = (f32[256,128]{1,0:T(8,128)S(1)}, f32[256,128]{1,0:T(8,128)S(1)}, u32[]{:S(2)}, u32[]{:S(2)}) collective-permute-start(f32[256,128]{1,0:T(8,128)S(1)} %get-tuple-element.46), channel_id=1, source_target_pairs={{0,56},{4,12},{8,0},{12,20},{16,8},{20,28},{24,16},{28,36},{32,24}... | collective-permute-start | bytes 393224 | tf_op jit(solution)/shard_map/ppermute | solution.py:173
  16.0 2.4 %collective-permute-start.5 = (f32[256,128]{1,0:T(8,128)S(1)}, f32[256,128]{1,0:T(8,128)S(1)}, u32[]{:S(2)}, u32[]{:S(2)}) collective-permute-start(f32[256,128]{1,0:T(8,128)S(1)} %get-tuple-element.48), channel_id=1, source_target_pairs={{0,48},{4,20},{8,56},{12,28},{16,0},{20,36},{24,8},{28,44},{32,16}... | collective-permute-start | bytes 393224 | tf_op jit(solution)/shard_map/ppermute | solution.py:173
  18.4 6.5 %collective-permute-start.6 = (f32[256,128]{1,0:T(8,128)S(1)}, f32[256,128]{1,0:T(8,128)S(1)}, u32[]{:S(2)}, u32[]{:S(2)}) collective-permute-start(f32[256,128]{1,0:T(8,128)S(1)} %get-tuple-element.49), channel_id=1, source_target_pairs={{0,24},{4,44},{8,32},{12,52},{16,40},{20,60},{24,48},{28,4},{32,56... | collective-permute-start | bytes 393224 | tf_op jit(solution)/shard_map/ppermute | solution.py:173
  25.0 3.6 %shard_map.69 = (f32[128,2048]{1,0:T(8,128)S(1)}, f32[128,2048]{1,0:T(8,128)S(1)}, f32[128,2048]{1,0:T(8,128)S(1)}) custom-call(bf16[128,2048]{1,0:T(8,128)(2,1)S(1)} %copy-done, bf16[128,2048]{1,0:T(8,128)(2,1)S(1)} %copy-done.1, bf16[128,2048]{1,0:T(8,128)(2,1)S(1)} %copy-done.2, bf16[128,2048]{1,0:T(8,128)(2,1)S(1)} %copy-done.3), custom_call_target="tpu_custom_call" | custom-call | flops 335544320 | bytes 5242880 | tf_op jit(solution)/shard_map/pallas_call | solution.py:219
  28.6 1.5 %collective-permute-done.4.refs_4_ = f32[256,128]{1,0:T(8,128)S(1)} collective-permute-done((f32[256,128]{1,0:T(8,128)S(1)}, f32[256,128]{1,0:T(8,128)S(1)}, u32[]{:S(2)}, u32[]{:S(2)}) %collective-permute-start.4) | collective-permute-done | bytes 131104 | tf_op jit(solution)/shard_map/ppermute | solution.py:173
  30.2 7.8 %collective-permute-done.6.refs_6_ = f32[256,128]{1,0:T(8,128)S(1)} collective-permute-done((f32[256,128]{1,0:T(8,128)S(1)}, f32[256,128]{1,0:T(8,128)S(1)}, u32[]{:S(2)}, u32[]{:S(2)}) %collective-permute-start.6) | collective-permute-done | bytes 131104 | tf_op jit(solution)/shard_map/ppermute | solution.py:173
  38.1 0.7 collective-permute-start.11
  38.8 1.3 %collective-permute-start.10 = (f32[256,128]{1,0:T(8,128)S(1)}, f32[256,128]{1,0:T(8,128)S(1)}, u32[]{:S(2)}, u32[]{:S(2)}) collective-permute-start(f32[256,128]{1,0:T(8,128)S(1)} %shard_map.70.refs_0_), channel_id=1, source_target_pairs={{0,192},{4,68},{64,0},{68,132},{128,64},{132,196},{192,128},{196,4... | collective-permute-start | bytes 393224 | tf_op jit(solution)/shard_map/ppermute | solution.py:173
  40.1 2.6 %collective-permute-start.9 = (f32[256,128]{1,0:T(8,128)S(1)}, f32[256,128]{1,0:T(8,128)S(1)}, u32[]{:S(2)}, u32[]{:S(2)}) collective-permute-start(f32[256,128]{1,0:T(8,128)S(1)} %shard_map.70.refs_0_), channel_id=1, source_target_pairs={{0,128},{4,132},{64,192},{68,196},{128,0},{132,4},{192,64},{196,68... | collective-permute-start | bytes 393224 | tf_op jit(solution)/shard_map/ppermute | solution.py:173
  42.7 1.1 %collective-permute-start.8 = (f32[256,128]{1,0:T(8,128)S(1)}, f32[256,128]{1,0:T(8,128)S(1)}, u32[]{:S(2)}, u32[]{:S(2)}) collective-permute-start(f32[256,128]{1,0:T(8,128)S(1)} %shard_map.70.refs_0_), channel_id=1, source_target_pairs={{0,64},{4,196},{64,128},{68,4},{128,192},{132,68},{192,0},{196,132... | collective-permute-start | bytes 393224 | tf_op jit(solution)/shard_map/ppermute | solution.py:173
  43.9 3.0 %collective-permute-done.9.refs_2_.refs_9_ = f32[256,128]{1,0:T(8,128)S(1)} collective-permute-done((f32[256,128]{1,0:T(8,128)S(1)}, f32[256,128]{1,0:T(8,128)S(1)}, u32[]{:S(2)}, u32[]{:S(2)}) %collective-permute-start.9) | collective-permute-done | bytes 131104 | tf_op jit(solution)/shard_map/ppermute | solution.py:173
  46.9 1.3 %collective-permute-done.8.refs_1_.refs_8_ = f32[256,128]{1,0:T(8,128)S(1)} collective-permute-done((f32[256,128]{1,0:T(8,128)S(1)}, f32[256,128]{1,0:T(8,128)S(1)}, u32[]{:S(2)}, u32[]{:S(2)}) %collective-permute-start.8) | collective-permute-done | bytes 131104 | tf_op jit(solution)/shard_map/ppermute | solution.py:173
  48.2 1.3 %collective-permute-start.14 = (f32[256,128]{1,0:T(8,128)S(1)}, f32[256,128]{1,0:T(8,128)S(1)}, u32[]{:S(2)}, u32[]{:S(2)}) collective-permute-start(f32[256,128]{1,0:T(8,128)S(1)} %shard_map.71), channel_id=1, source_target_pairs={{0,3},{7,4},{8,11},{15,12},{16,19},{23,20},{24,27},{31,28},{32,35}... | collective-permute-start | bytes 393224 | tf_op jit(solution)/shard_map/ppermute | solution.py:179
  49.5 1.3 %collective-permute-start.13 = (f32[256,128]{1,0:T(8,128)S(1)}, f32[256,128]{1,0:T(8,128)S(1)}, u32[]{:S(2)}, u32[]{:S(2)}) collective-permute-start(f32[256,128]{1,0:T(8,128)S(1)} %shard_map.71), channel_id=1, source_target_pairs={{0,2},{1,3},{6,4},{7,5},{8,10},{9,11},{14,12},{15,13},{16,18},{17,... | collective-permute-start | bytes 393224 | tf_op jit(solution)/shard_map/ppermute | solution.py:179
  50.8 1.3 %collective-permute-start.12 = (f32[256,128]{1,0:T(8,128)S(1)}, f32[256,128]{1,0:T(8,128)S(1)}, u32[]{:S(2)}, u32[]{:S(2)}) collective-permute-start(f32[256,128]{1,0:T(8,128)S(1)} %shard_map.71), channel_id=1, source_target_pairs={{0,1},{1,2},{2,3},{5,4},{6,5},{7,6},{8,9},{9,10},{10,11},{13,12},{... | collective-permute-start | bytes 393224 | tf_op jit(solution)/shard_map/ppermute | solution.py:179
  52.1 3.0 %collective-permute-done.14.refs_13_ = f32[256,128]{1,0:T(8,128)S(1)} collective-permute-done((f32[256,128]{1,0:T(8,128)S(1)}, f32[256,128]{1,0:T(8,128)S(1)}, u32[]{:S(2)}, u32[]{:S(2)}) %collective-permute-start.14) | collective-permute-done | bytes 131104 | tf_op jit(solution)/shard_map/ppermute | solution.py:179
  55.1 1.6 %collective-permute-done.13.refs_12_ = f32[256,128]{1,0:T(8,128)S(1)} collective-permute-done((f32[256,128]{1,0:T(8,128)S(1)}, f32[256,128]{1,0:T(8,128)S(1)}, u32[]{:S(2)}, u32[]{:S(2)}) %collective-permute-start.13) | collective-permute-done | bytes 131104 | tf_op jit(solution)/shard_map/ppermute | solution.py:179
  56.7 0.8 shard_map.72
  57.6 4.7 %collective-permute-start.15 = (f32[256,128]{1,0:T(8,128)S(1)}, f32[256,128]{1,0:T(8,128)S(1)}, u32[]{:S(2)}, u32[]{:S(2)}) collective-permute-start(f32[256,128]{1,0:T(8,128)S(1)} %get-tuple-element.72), channel_id=1, source_target_pairs={{0,32},{4,36},{8,40},{12,44},{16,48},{20,52},{24,56},{28,60},{32,0... | collective-permute-start | bytes 393224 | tf_op jit(solution)/shard_map/ppermute | solution.py:173
  62.6 1.1 %collective-permute-start.17 = (f32[256,128]{1,0:T(8,128)S(1)}, f32[256,128]{1,0:T(8,128)S(1)}, u32[]{:S(2)}, u32[]{:S(2)}) collective-permute-start(f32[256,128]{1,0:T(8,128)S(1)} %get-tuple-element.74), channel_id=1, source_target_pairs={{0,56},{4,12},{8,0},{12,20},{16,8},{20,28},{24,16},{28,36},{32,24}... | collective-permute-start | bytes 393224 | tf_op jit(solution)/shard_map/ppermute | solution.py:173
  63.8 2.2 %collective-permute-start.19 = (f32[256,128]{1,0:T(8,128)S(1)}, f32[256,128]{1,0:T(8,128)S(1)}, u32[]{:S(2)}, u32[]{:S(2)}) collective-permute-start(f32[256,128]{1,0:T(8,128)S(1)} %get-tuple-element.76), channel_id=1, source_target_pairs={{0,48},{4,20},{8,56},{12,28},{16,0},{20,36},{24,8},{28,44},{32,16}... | collective-permute-start | bytes 393224 | tf_op jit(solution)/shard_map/ppermute | solution.py:173
  66.0 2.8 %collective-permute-start.20 = (f32[256,128]{1,0:T(8,128)S(1)}, f32[256,128]{1,0:T(8,128)S(1)}, u32[]{:S(2)}, u32[]{:S(2)}) collective-permute-start(f32[256,128]{1,0:T(8,128)S(1)} %get-tuple-element.77), channel_id=1, source_target_pairs={{0,24},{4,44},{8,32},{12,52},{16,40},{20,60},{24,48},{28,4},{32,56... | collective-permute-start | bytes 393224 | tf_op jit(solution)/shard_map/ppermute | solution.py:173
  68.8 1.1 %collective-permute-start.21 = (f32[256,128]{1,0:T(8,128)S(1)}, f32[256,128]{1,0:T(8,128)S(1)}, u32[]{:S(2)}, u32[]{:S(2)}) collective-permute-start(f32[256,128]{1,0:T(8,128)S(1)} %get-tuple-element.78), channel_id=1, source_target_pairs={{0,40},{4,28},{8,48},{12,36},{16,56},{20,44},{24,0},{28,52},{32,8}... | collective-permute-start | bytes 393224 | tf_op jit(solution)/shard_map/ppermute | solution.py:173
  70.0 9.5 %collective-permute-start.22 = (f32[256,128]{1,0:T(8,128)S(1)}, f32[256,128]{1,0:T(8,128)S(1)}, u32[]{:S(2)}, u32[]{:S(2)}) collective-permute-start(f32[256,128]{1,0:T(8,128)S(1)} %get-tuple-element.71.refs_8_), channel_id=1, source_target_pairs={{0,4},{4,0},{1,5},{5,1},{2,6},{6,2},{3,7},{7,3},{8,12},{12,8},{9,1... | collective-permute-start | bytes 393224 | tf_op jit(solution)/shard_map/ppermute | solution.py:263
  79.7 3.5 %collective-permute-start.24 = (f32[256,128]{1,0:T(8,128)S(1)}, f32[256,128]{1,0:T(8,128)S(1)}, u32[]{:S(2)}, u32[]{:S(2)}) collective-permute-start(f32[256,128]{1,0:T(8,128)S(1)} %collective-permute-done.16.refs_10_), channel_id=1, source_target_pairs={{0,4},{4,0},{1,5},{5,1},{2,6},{6,2},{3,7},{7,3},{8,12},{12,8},{9,1... | collective-permute-start | bytes 393224 | tf_op jit(solution)/shard_map/ppermute | solution.py:263
  83.2 5.0 %collective-permute-start.25 = (f32[256,128]{1,0:T(8,128)S(1)}, f32[256,128]{1,0:T(8,128)S(1)}, u32[]{:S(2)}, u32[]{:S(2)}) collective-permute-start(f32[256,128]{1,0:T(8,128)S(1)} %collective-permute-done.17.refs_11_), channel_id=1, source_target_pairs={{0,4},{4,0},{1,5},{5,1},{2,6},{6,2},{3,7},{7,3},{8,12},{12,8},{9,1... | collective-permute-start | bytes 393224 | tf_op jit(solution)/shard_map/ppermute | solution.py:263
  88.3 0.4 collective-permute-start.27
  90.3 2.5 %shard_map.73 = (bf16[128,2048]{1,0:T(8,128)(2,1)}, bf16[128,2048]{1,0:T(8,128)(2,1)}, bf16[128,2048]{1,0:T(8,128)(2,1)}) custom-call(s32[3]{0:T(128)S(1)} %pad_add_fusion.places, bf16[128,2048]{1,0:T(8,128)(2,1)S(1)} %copy-done, bf16[128,2048]{1,0:T(8,128)(2,1)S(1)} %copy-done.1, bf16[128,2048]{1,0:T(8,128)(2,1)S(1)} %copy-done.2, ...), custom_call_target="tpu_custom_call" | custom-call | flops 201326592 | bytes 9961472 | tf_op jit(solution)/shard_map/pallas_call | solution.py:264
  (44 shorter events, 2.9 us)
Async XLA Ops:
  3.6 5.6 %collective-permute-start = (f32[8,256,128]{2,1,0:T(8,128)S(1)}, f32[8,256,128]{2,1,0:T(8,128)S(1)}, u32[]{:S(2)}, u32[]{:S(2)}) collective-permute-start(f32[8,256,128]{2,1,0:T(8,128)S(1)} %get-tuple-element.42), channel_id=1, source_target_pairs={{0,4},{4,0},{1,5},{5,1},{2,6},{6,2},{3,7},{7,3},{8,12},{12,8},{9,1... | collective-permute-start | bytes 3145736 | tf_op jit(solution)/shard_map/ppermute | solution.py:218
  9.2 15.8 %copy-start.2 = (bf16[128,2048]{1,0:T(8,128)(2,1)S(1)}, bf16[128,2048]{1,0:T(8,128)(2,1)}, u32[]{:S(2)}) copy-start(bf16[128,2048]{1,0:T(8,128)(2,1)} %refs_2_.1) | copy-start | bytes 1572868
  9.2 15.8 %copy-start.3 = (bf16[128,2048]{1,0:T(8,128)(2,1)S(1)}, bf16[128,2048]{1,0:T(8,128)(2,1)}, u32[]{:S(2)}) copy-start(bf16[128,2048]{1,0:T(8,128)(2,1)} %refs_3_.1) | copy-start | bytes 1572868
  9.3 9.1 %collective-permute-start.1 = (f32[256,128]{1,0:T(8,128)S(1)}, f32[256,128]{1,0:T(8,128)S(1)}, u32[]{:S(2)}, u32[]{:S(2)}) collective-permute-start(f32[256,128]{1,0:T(8,128)S(1)} %get-tuple-element.44), channel_id=1, source_target_pairs={{0,32},{4,36},{8,40},{12,44},{16,48},{20,52},{24,56},{28,60},{32,0... | collective-permute-start | bytes 393224 | tf_op jit(solution)/shard_map/ppermute | solution.py:173
  14.6 10.3 %collective-permute-start.2 = (f32[256,128]{1,0:T(8,128)S(1)}, f32[256,128]{1,0:T(8,128)S(1)}, u32[]{:S(2)}, u32[]{:S(2)}) collective-permute-start(f32[256,128]{1,0:T(8,128)S(1)} %get-tuple-element.45), channel_id=1, source_target_pairs={{0,8},{4,60},{8,16},{12,4},{16,24},{20,12},{24,32},{28,20},{32,40}... | collective-permute-start | bytes 393224 | tf_op jit(solution)/shard_map/ppermute | solution.py:173
  14.6 14.1 %collective-permute-start.3 = (f32[256,128]{1,0:T(8,128)S(1)}, f32[256,128]{1,0:T(8,128)S(1)}, u32[]{:S(2)}, u32[]{:S(2)}) collective-permute-start(f32[256,128]{1,0:T(8,128)S(1)} %get-tuple-element.46), channel_id=1, source_target_pairs={{0,56},{4,12},{8,0},{12,20},{16,8},{20,28},{24,16},{28,36},{32,24}... | collective-permute-start | bytes 393224 | tf_op jit(solution)/shard_map/ppermute | solution.py:173
  16.0 14.2 %collective-permute-start.4 = (f32[256,128]{1,0:T(8,128)S(1)}, f32[256,128]{1,0:T(8,128)S(1)}, u32[]{:S(2)}, u32[]{:S(2)}) collective-permute-start(f32[256,128]{1,0:T(8,128)S(1)} %get-tuple-element.47), channel_id=1, source_target_pairs={{0,16},{4,52},{8,24},{12,60},{16,32},{20,4},{24,40},{28,12},{32,48... | collective-permute-start | bytes 393224 | tf_op jit(solution)/shard_map/ppermute | solution.py:173
  16.0 14.2 %collective-permute-start.5 = (f32[256,128]{1,0:T(8,128)S(1)}, f32[256,128]{1,0:T(8,128)S(1)}, u32[]{:S(2)}, u32[]{:S(2)}) collective-permute-start(f32[256,128]{1,0:T(8,128)S(1)} %get-tuple-element.48), channel_id=1, source_target_pairs={{0,48},{4,20},{8,56},{12,28},{16,0},{20,36},{24,8},{28,44},{32,16}... | collective-permute-start | bytes 393224 | tf_op jit(solution)/shard_map/ppermute | solution.py:173
  18.4 19.6 %collective-permute-start.6 = (f32[256,128]{1,0:T(8,128)S(1)}, f32[256,128]{1,0:T(8,128)S(1)}, u32[]{:S(2)}, u32[]{:S(2)}) collective-permute-start(f32[256,128]{1,0:T(8,128)S(1)} %get-tuple-element.49), channel_id=1, source_target_pairs={{0,24},{4,44},{8,32},{12,52},{16,40},{20,60},{24,48},{28,4},{32,56... | collective-permute-start | bytes 393224 | tf_op jit(solution)/shard_map/ppermute | solution.py:173
  24.9 13.2 %collective-permute-start.7 = (f32[256,128]{1,0:T(8,128)S(1)}, f32[256,128]{1,0:T(8,128)S(1)}, u32[]{:S(2)}, u32[]{:S(2)}) collective-permute-start(f32[256,128]{1,0:T(8,128)S(1)} %get-tuple-element.50), channel_id=1, source_target_pairs={{0,40},{4,28},{8,48},{12,36},{16,56},{20,44},{24,0},{28,52},{32,8}... | collective-permute-start | bytes 393224 | tf_op jit(solution)/shard_map/ppermute | solution.py:173
  38.1 10.1 %collective-permute-start.11 = (f32[8,256,128]{2,1,0:T(8,128)S(1)}, f32[8,256,128]{2,1,0:T(8,128)S(1)}, u32[]{:S(2)}, u32[]{:S(2)}) collective-permute-start(f32[8,256,128]{2,1,0:T(8,128)S(1)} %get-tuple-element.66.keep), channel_id=1, source_target_pairs={{0,4},{4,0},{1,5},{5,1},{2,6},{6,2},{3,7},{7,3},{8,12},{12,8},{9,1... | collective-permute-start | bytes 3145736 | tf_op jit(solution)/shard_map/ppermute | solution.py:248
  38.8 5.1 %collective-permute-start.10 = (f32[256,128]{1,0:T(8,128)S(1)}, f32[256,128]{1,0:T(8,128)S(1)}, u32[]{:S(2)}, u32[]{:S(2)}) collective-permute-start(f32[256,128]{1,0:T(8,128)S(1)} %shard_map.70.refs_0_), channel_id=1, source_target_pairs={{0,192},{4,68},{64,0},{68,132},{128,64},{132,196},{192,128},{196,4... | collective-permute-start | bytes 393224 | tf_op jit(solution)/shard_map/ppermute | solution.py:173
  40.1 6.8 %collective-permute-start.9 = (f32[256,128]{1,0:T(8,128)S(1)}, f32[256,128]{1,0:T(8,128)S(1)}, u32[]{:S(2)}, u32[]{:S(2)}) collective-permute-start(f32[256,128]{1,0:T(8,128)S(1)} %shard_map.70.refs_0_), channel_id=1, source_target_pairs={{0,128},{4,132},{64,192},{68,196},{128,0},{132,4},{192,64},{196,68... | collective-permute-start | bytes 393224 | tf_op jit(solution)/shard_map/ppermute | solution.py:173
  42.7 5.5 %collective-permute-start.8 = (f32[256,128]{1,0:T(8,128)S(1)}, f32[256,128]{1,0:T(8,128)S(1)}, u32[]{:S(2)}, u32[]{:S(2)}) collective-permute-start(f32[256,128]{1,0:T(8,128)S(1)} %shard_map.70.refs_0_), channel_id=1, source_target_pairs={{0,64},{4,196},{64,128},{68,4},{128,192},{132,68},{192,0},{196,132... | collective-permute-start | bytes 393224 | tf_op jit(solution)/shard_map/ppermute | solution.py:173
  48.2 6.9 %collective-permute-start.14 = (f32[256,128]{1,0:T(8,128)S(1)}, f32[256,128]{1,0:T(8,128)S(1)}, u32[]{:S(2)}, u32[]{:S(2)}) collective-permute-start(f32[256,128]{1,0:T(8,128)S(1)} %shard_map.71), channel_id=1, source_target_pairs={{0,3},{7,4},{8,11},{15,12},{16,19},{23,20},{24,27},{31,28},{32,35}... | collective-permute-start | bytes 393224 | tf_op jit(solution)/shard_map/ppermute | solution.py:179
  49.5 7.2 %collective-permute-start.13 = (f32[256,128]{1,0:T(8,128)S(1)}, f32[256,128]{1,0:T(8,128)S(1)}, u32[]{:S(2)}, u32[]{:S(2)}) collective-permute-start(f32[256,128]{1,0:T(8,128)S(1)} %shard_map.71), channel_id=1, source_target_pairs={{0,2},{1,3},{6,4},{7,5},{8,10},{9,11},{14,12},{15,13},{16,18},{17,... | collective-permute-start | bytes 393224 | tf_op jit(solution)/shard_map/ppermute | solution.py:179
  50.8 5.9 %collective-permute-start.12 = (f32[256,128]{1,0:T(8,128)S(1)}, f32[256,128]{1,0:T(8,128)S(1)}, u32[]{:S(2)}, u32[]{:S(2)}) collective-permute-start(f32[256,128]{1,0:T(8,128)S(1)} %shard_map.71), channel_id=1, source_target_pairs={{0,1},{1,2},{2,3},{5,4},{6,5},{7,6},{8,9},{9,10},{10,11},{13,12},{... | collective-permute-start | bytes 393224 | tf_op jit(solution)/shard_map/ppermute | solution.py:179
  57.6 8.5 %collective-permute-start.15 = (f32[256,128]{1,0:T(8,128)S(1)}, f32[256,128]{1,0:T(8,128)S(1)}, u32[]{:S(2)}, u32[]{:S(2)}) collective-permute-start(f32[256,128]{1,0:T(8,128)S(1)} %get-tuple-element.72), channel_id=1, source_target_pairs={{0,32},{4,36},{8,40},{12,44},{16,48},{20,52},{24,56},{28,60},{32,0... | collective-permute-start | bytes 393224 | tf_op jit(solution)/shard_map/ppermute | solution.py:173
  62.2 6.6 %collective-permute-start.16 = (f32[256,128]{1,0:T(8,128)S(1)}, f32[256,128]{1,0:T(8,128)S(1)}, u32[]{:S(2)}, u32[]{:S(2)}) collective-permute-start(f32[256,128]{1,0:T(8,128)S(1)} %get-tuple-element.73), channel_id=1, source_target_pairs={{0,8},{4,60},{8,16},{12,4},{16,24},{20,12},{24,32},{28,20},{32,40}... | collective-permute-start | bytes 393224 | tf_op jit(solution)/shard_map/ppermute | solution.py:173
  62.6 7.3 %collective-permute-start.17 = (f32[256,128]{1,0:T(8,128)S(1)}, f32[256,128]{1,0:T(8,128)S(1)}, u32[]{:S(2)}, u32[]{:S(2)}) collective-permute-start(f32[256,128]{1,0:T(8,128)S(1)} %get-tuple-element.74), channel_id=1, source_target_pairs={{0,56},{4,12},{8,0},{12,20},{16,8},{20,28},{24,16},{28,36},{32,24}... | collective-permute-start | bytes 393224 | tf_op jit(solution)/shard_map/ppermute | solution.py:173
  63.7 15.8 %collective-permute-start.18 = (f32[256,128]{1,0:T(8,128)S(1)}, f32[256,128]{1,0:T(8,128)S(1)}, u32[]{:S(2)}, u32[]{:S(2)}) collective-permute-start(f32[256,128]{1,0:T(8,128)S(1)} %get-tuple-element.75), channel_id=1, source_target_pairs={{0,16},{4,52},{8,24},{12,60},{16,32},{20,4},{24,40},{28,12},{32,48... | collective-permute-start | bytes 393224 | tf_op jit(solution)/shard_map/ppermute | solution.py:173
  63.8 15.9 %collective-permute-start.19 = (f32[256,128]{1,0:T(8,128)S(1)}, f32[256,128]{1,0:T(8,128)S(1)}, u32[]{:S(2)}, u32[]{:S(2)}) collective-permute-start(f32[256,128]{1,0:T(8,128)S(1)} %get-tuple-element.76), channel_id=1, source_target_pairs={{0,48},{4,20},{8,56},{12,28},{16,0},{20,36},{24,8},{28,44},{32,16}... | collective-permute-start | bytes 393224 | tf_op jit(solution)/shard_map/ppermute | solution.py:173
  66.0 17.2 %collective-permute-start.20 = (f32[256,128]{1,0:T(8,128)S(1)}, f32[256,128]{1,0:T(8,128)S(1)}, u32[]{:S(2)}, u32[]{:S(2)}) collective-permute-start(f32[256,128]{1,0:T(8,128)S(1)} %get-tuple-element.77), channel_id=1, source_target_pairs={{0,24},{4,44},{8,32},{12,52},{16,40},{20,60},{24,48},{28,4},{32,56... | collective-permute-start | bytes 393224 | tf_op jit(solution)/shard_map/ppermute | solution.py:173
  68.8 19.4 %collective-permute-start.21 = (f32[256,128]{1,0:T(8,128)S(1)}, f32[256,128]{1,0:T(8,128)S(1)}, u32[]{:S(2)}, u32[]{:S(2)}) collective-permute-start(f32[256,128]{1,0:T(8,128)S(1)} %get-tuple-element.78), channel_id=1, source_target_pairs={{0,40},{4,28},{8,48},{12,36},{16,56},{20,44},{24,0},{28,52},{32,8}... | collective-permute-start | bytes 393224 | tf_op jit(solution)/shard_map/ppermute | solution.py:173
  70.0 18.4 %collective-permute-start.22 = (f32[256,128]{1,0:T(8,128)S(1)}, f32[256,128]{1,0:T(8,128)S(1)}, u32[]{:S(2)}, u32[]{:S(2)}) collective-permute-start(f32[256,128]{1,0:T(8,128)S(1)} %get-tuple-element.71.refs_8_), channel_id=1, source_target_pairs={{0,4},{4,0},{1,5},{5,1},{2,6},{6,2},{3,7},{7,3},{8,12},{12,8},{9,1... | collective-permute-start | bytes 393224 | tf_op jit(solution)/shard_map/ppermute | solution.py:263
  79.5 9.3 %collective-permute-start.23 = (f32[256,128]{1,0:T(8,128)S(1)}, f32[256,128]{1,0:T(8,128)S(1)}, u32[]{:S(2)}, u32[]{:S(2)}) collective-permute-start(f32[256,128]{1,0:T(8,128)S(1)} %collective-permute-done.15.refs_9_), channel_id=1, source_target_pairs={{0,4},{4,0},{1,5},{5,1},{2,6},{6,2},{3,7},{7,3},{8,12},{12,8},{9,1... | collective-permute-start | bytes 393224 | tf_op jit(solution)/shard_map/ppermute | solution.py:263
  79.7 9.2 %collective-permute-start.24 = (f32[256,128]{1,0:T(8,128)S(1)}, f32[256,128]{1,0:T(8,128)S(1)}, u32[]{:S(2)}, u32[]{:S(2)}) collective-permute-start(f32[256,128]{1,0:T(8,128)S(1)} %collective-permute-done.16.refs_10_), channel_id=1, source_target_pairs={{0,4},{4,0},{1,5},{5,1},{2,6},{6,2},{3,7},{7,3},{8,12},{12,8},{9,1... | collective-permute-start | bytes 393224 | tf_op jit(solution)/shard_map/ppermute | solution.py:263
  83.2 6.1 %collective-permute-start.25 = (f32[256,128]{1,0:T(8,128)S(1)}, f32[256,128]{1,0:T(8,128)S(1)}, u32[]{:S(2)}, u32[]{:S(2)}) collective-permute-start(f32[256,128]{1,0:T(8,128)S(1)} %collective-permute-done.17.refs_11_), channel_id=1, source_target_pairs={{0,4},{4,0},{1,5},{5,1},{2,6},{6,2},{3,7},{7,3},{8,12},{12,8},{9,1... | collective-permute-start | bytes 393224 | tf_op jit(solution)/shard_map/ppermute | solution.py:263
  88.2 1.3 %collective-permute-start.26 = (f32[256,128]{1,0:T(8,128)S(1)}, f32[256,128]{1,0:T(8,128)S(1)}, u32[]{:S(2)}, u32[]{:S(2)}) collective-permute-start(f32[256,128]{1,0:T(8,128)S(1)} %collective-permute-done.18.refs_12_), channel_id=1, source_target_pairs={{0,4},{4,0},{1,5},{5,1},{2,6},{6,2},{3,7},{7,3},{8,12},{12,8},{9,1... | collective-permute-start | bytes 393224 | tf_op jit(solution)/shard_map/ppermute | solution.py:263
  88.3 1.5 %collective-permute-start.27 = (f32[256,128]{1,0:T(8,128)S(1)}, f32[256,128]{1,0:T(8,128)S(1)}, u32[]{:S(2)}, u32[]{:S(2)}) collective-permute-start(f32[256,128]{1,0:T(8,128)S(1)} %collective-permute-done.19.refs_13_), channel_id=1, source_target_pairs={{0,4},{4,0},{1,5},{5,1},{2,6},{6,2},{3,7},{7,3},{8,12},{12,8},{9,1... | collective-permute-start | bytes 393224 | tf_op jit(solution)/shard_map/ppermute | solution.py:263
  88.8 1.3 %collective-permute-start.28 = (f32[256,128]{1,0:T(8,128)S(1)}, f32[256,128]{1,0:T(8,128)S(1)}, u32[]{:S(2)}, u32[]{:S(2)}) collective-permute-start(f32[256,128]{1,0:T(8,128)S(1)} %collective-permute-done.20.refs_14_), channel_id=1, source_target_pairs={{0,4},{4,0},{1,5},{5,1},{2,6},{6,2},{3,7},{7,3},{8,12},{12,8},{9,1... | collective-permute-start | bytes 393224 | tf_op jit(solution)/shard_map/ppermute | solution.py:263
  88.9 1.4 %collective-permute-start.29 = (f32[256,128]{1,0:T(8,128)S(1)}, f32[256,128]{1,0:T(8,128)S(1)}, u32[]{:S(2)}, u32[]{:S(2)}) collective-permute-start(f32[256,128]{1,0:T(8,128)S(1)} %collective-permute-done.21.refs_15_), channel_id=1, source_target_pairs={{0,4},{4,0},{1,5},{5,1},{2,6},{6,2},{3,7},{7,3},{8,12},{12,8},{9,1... | collective-permute-start | bytes 393224 | tf_op jit(solution)/shard_map/ppermute | solution.py:263
  (2 other events, 31.6 us)

commit v5 on v3

v5 whole, which is shorter than its diff:
```python
import functools

import jax
import jax.numpy as jnp
from jax import lax
from jax.experimental import pallas as pl
from jax.experimental.pallas import tpu as pltpu
from jax.sharding import Mesh
from jax.sharding import PartitionSpec as P

HEAD = 128
LOADS = 4
ROWS = ("x", "y", "z", "c")
SMEM = pl.BlockSpec(memory_space=pltpu.SMEM)
VMEM = pl.BlockSpec(memory_space=pltpu.VMEM)
HBM = pl.BlockSpec(memory_space=pltpu.HBM)
VMEM_LIMIT = 24 * 1024 * 1024
F32, BF16 = jnp.float32, jnp.bfloat16


def contract(lhs, rhs, lhs_dim, rhs_dim):
    return lax.dot_general(
        lhs, rhs, (((lhs_dim,), (rhs_dim,)), ((), ())), preferred_element_type=F32
    )


def states_kernel(places, query, key, value, gradient, keep, send, held, sems):
    first = places[0] == 0
    part = held.shape[3]
    copies = []
    for n in range(held.shape[1]):
        for source, tensor in enumerate((key, value, query, gradient)):
            copy = pltpu.make_async_copy(
                tensor.at[:, pl.ds(n * part, part)], held.at[source, n], sems.at[source, n]
            )
            copy.start()
            copies.append(copy)
    for n in range(held.shape[1]):
        for copy in copies[4 * n : 4 * n + 4]:
            copy.wait()
        for h in range(part // HEAD):
            lanes = pl.ds(h * HEAD, HEAD)
            rows = pl.ds(n * part + h * HEAD, HEAD)
            kv = contract(held[0, n, :, lanes], held[1, n, :, lanes], 0, 0)
            qo = contract(held[2, n, :, lanes], held[3, n, :, lanes], 0, 0)
            keep[rows, :] = jnp.where(first, kv, qo)
            send[rows, :] = jnp.where(first, qo, kv)


def inner_kernel(query, key, value, gradient, gq, gk, gv):
    count = query.shape[0]
    causal = lax.broadcasted_iota(jnp.int32, (count, count), 0) >= lax.broadcasted_iota(
        jnp.int32, (count, count), 1
    )
    for h in range(query.shape[1] // HEAD):
        lanes = pl.ds(h * HEAD, HEAD)
        q, k, v, g = query[:, lanes], key[:, lanes], value[:, lanes], gradient[:, lanes]
        dv = jnp.where(causal, contract(g, v, 1, 1), 0.0).astype(BF16)
        qk = jnp.where(causal, contract(q, k, 1, 1), 0.0).astype(BF16)
        gq[:, lanes] = contract(dv, k, 1, 0)
        gk[:, lanes] = contract(dv, q, 0, 0)
        gv[:, lanes] = contract(qk, g, 0, 0)


def merge_kernel(keep, received, out):
    out[...] = keep[...] + received[...]


def total_kernel(parts, out):
    total = parts[0]
    for n in range(1, parts.shape[0]):
        total = total + parts[n]
    out[...] = total


def scan_kernel(places, parts, *refs):
    first = places[0] == 0
    count = parts.shape[0]
    out = refs[-1]
    total = refs[0][...]
    for plane in refs[1:-1]:
        total = total + plane[...]
    for n in range(count):
        place = jnp.where(first, n, count - 1 - n)
        out[place] = total
        total = total + parts[place]


def outputs_kernel(scale, places, query, key, value, gradient, *refs):
    inner = refs[:3]
    other, own, received = refs[3:6]
    outs = refs[6:9]
    held, sems = refs[9:]
    first = places[0] == 0
    part = held.shape[3]
    copies = []
    for n in range(held.shape[1]):
        for h in range(part // HEAD):
            rows = pl.ds(n * part + h * HEAD, HEAD)
            mine = own[rows, :]
            theirs = received[rows, :] + other[rows, :]
            prefix = jnp.where(first, mine, theirs).astype(BF16)
            suffix = jnp.where(first, theirs, mine).astype(BF16)
            gq = contract(gradient[:, rows], prefix, 1, 1)
            gk = contract(value[:, rows], suffix, 1, 1)
            gv = contract(key[:, rows], suffix, 1, 0)
            for t, result in enumerate((gq, gk, gv)):
                held[t, n, :, pl.ds(h * HEAD, HEAD)] = (
                    scale * (result + inner[t][:, rows])
                ).astype(BF16)
        for t, out in enumerate(outs):
            copy = pltpu.make_async_copy(
                held.at[t, n], out.at[:, pl.ds(n * part, part)], sems.at[t, n]
            )
            copy.start()
            copies.append(copy)
    for copy in copies:
        copy.wait()


def call(kernel, in_specs, out_specs, out_shape, flops, moved, scratch=()):
    return pl.pallas_call(
        kernel,
        in_specs=in_specs,
        out_specs=out_specs,
        out_shape=out_shape,
        scratch_shapes=scratch,
        cost_estimate=pl.CostEstimate(flops=flops, bytes_accessed=moved, transcendentals=0),
        compiler_params=pltpu.CompilerParams(vmem_limit_bytes=VMEM_LIMIT),
    )


def onward(array, axis, count, step):
    pairs = [(i, i + step) for i in range(count - step)]
    pairs += [(count + i, count + i - step) for i in range(step, count)]
    return lax.ppermute(array, ("c", axis), pairs)


def per_device(sizes, scale, queries, key_row_matrix, value_row_matrix, output_gradient):
    tokens, width = queries.shape
    members = sizes["y"] * sizes["z"]
    places = lax.axis_index("c").astype(jnp.int32).reshape(1)
    swap = [(0, 1), (1, 0)]
    product = 2 * width * tokens * HEAD
    token_bytes = 2 * tokens * width
    state_bytes = 4 * width * HEAD
    token_shape = jax.ShapeDtypeStruct((tokens, width), BF16)
    inner_shape = jax.ShapeDtypeStruct((tokens, width), F32)
    state_shape = jax.ShapeDtypeStruct((width, HEAD), F32)
    parts_shape = jax.ShapeDtypeStruct((members, width // members, HEAD), F32)
    inputs = (queries, key_row_matrix, value_row_matrix, output_gradient)

    keep, send = call(
        states_kernel,
        [SMEM] + [HBM] * 4,
        [VMEM] * 2,
        [state_shape] * 2,
        2 * product,
        4 * token_bytes + 2 * state_bytes,
        [
            pltpu.VMEM((4, LOADS, tokens, width // LOADS), BF16),
            pltpu.SemaphoreType.DMA((4, LOADS)),
        ],
    )(places, *(pltpu.with_memory_space_constraint(a, pltpu.HBM) for a in inputs))
    received = lax.ppermute(send, "c", swap)
    chip = call(
        merge_kernel, [VMEM] * 2, VMEM, state_shape, width * HEAD, 3 * state_bytes
    )(keep, received)
    parts = lax.all_to_all(chip.reshape(parts_shape.shape), ("y", "z"), 0, 0, tiled=True)
    parts, keep, inputs = lax.optimization_barrier((parts, keep, inputs))
    plane = call(
        total_kernel,
        [VMEM],
        VMEM,
        jax.ShapeDtypeStruct(parts_shape.shape[1:], F32),
        width * HEAD,
        state_bytes,
    )(parts)
    planes = [onward(plane, "x", sizes["x"], k) for k in range(1, sizes["x"])]
    other = lax.ppermute(keep, "c", swap)
    inner = call(
        inner_kernel,
        [VMEM] * 4,
        [VMEM] * 3,
        [inner_shape] * 3,
        5 * product,
        10 * token_bytes,
    )(*inputs)
    planes, other, inner = lax.optimization_barrier((planes, other, inner))
    prefixes = call(
        scan_kernel,
        [SMEM] + [VMEM] * (1 + len(planes)),
        VMEM,
        parts_shape,
        width * HEAD,
        2 * state_bytes,
    )(places, parts, *planes)
    own = lax.all_to_all(prefixes, ("y", "z"), 0, 0, tiled=True).reshape(width, HEAD)
    theirs = lax.ppermute(own, "c", swap)
    return call(
        functools.partial(outputs_kernel, scale),
        [SMEM] + [VMEM] * 10,
        [HBM] * 3,
        [token_shape] * 3,
        3 * product,
        13 * token_bytes + 3 * state_bytes,
        [
            pltpu.VMEM((3, LOADS, tokens, width // LOADS), BF16),
            pltpu.SemaphoreType.DMA((3, LOADS)),
        ],
    )(places, *inputs, *inner, other, own, theirs)


def solution(mesh):
    sizes = {"y": 4, "z": 8, "c": 2, "x": 4}
    fine = Mesh(mesh.devices.reshape(tuple(sizes.values())), tuple(sizes))

    def program(queries, key_row_matrix, value_row_matrix, output_gradient):
        scale = float(HEAD * queries.shape[0]) ** -0.5
        spec = P(ROWS, None)
        return jax.shard_map(
            functools.partial(per_device, sizes, scale),
            mesh=fine,
            in_specs=(spec,) * 4,
            out_specs=(spec,) * 3,
            check_vma=False,
        )(queries, key_row_matrix, value_row_matrix, output_gradient)

    return program
```

time: 96.2 us -> 94.6 us (0.983)
  blocking collectives: 0 us -> 58.5 us
  starting transfers between devices: 53.8 us -> 21.8 us
  waiting for transfers between devices: 30.3 us -> 4.58 us
  Pallas kernels: 10 us -> 7.97 us
    all_to_all x0 -> x2, blocking collectives: none -> 58.5 us  [the longest x1 34.6 us: per_device(): lax.all_to_all(chip.reshape(parts_shape.shape), ('y', 'z'), 0, 0, tiled=T...]
    ppermute x25 -> x1, starting transfers between devices: 46 us -> 10.2 us  [per_device(): theirs = lax.ppermute(own, 'c', swap)]
    ppermute x25 -> x1, waiting for transfers between devices: 23.4 us -> 2.29 us  [per_device(): theirs = lax.ppermute(own, 'c', swap)]
    ppermute x3, waiting for transfers between devices: 4.62 us -> 0.01 us  [onward(): return lax.ppermute(array, ('c', axis), pairs)]
    ppermute x1, starting transfers between devices: 0.58 us -> 4.35 us  [per_device(): other = lax.ppermute(keep, 'c', swap)]
    pallas_call x5 -> x4, Pallas kernels: 3.57 us -> 2.04 us  [the longest x1 1.78 us: per_device(): call(functools.partial(outputs_kernel, scale), [SMEM] + [VMEM] * 10, [HBM...]
  transfers between devices with their start and end apart: 30 -> 6, of which waited for: 15 -> 2; matrix products, arithmetic and copies ran while one was open for 0% -> 0% of each run, Pallas kernels for 4% -> 4%
where the time goes in v5:
time: 94.6 us; the launch traced here: 93.6 us
  blocking collectives  58.5 us (62%)
  starting transfers between devices  21.8 us (23%)
  Pallas kernels  7.97 us (8%)
  waiting for transfers between devices  4.58 us (5%)
    all_to_all x1, blocking collectives, per_device(): lax.all_to_all(chip.reshape(parts_shape.shape), ('y', 'z'), 0, 0, tiled=T...  34.6 us
    all_to_all x1, blocking collectives, per_device(): lax.all_to_all(prefixes, ('y', 'z'), 0, 0, tiled=True).reshape(width, HEAD)  23.9 us
    ppermute x1, starting transfers between devices, per_device(): theirs = lax.ppermute(own, 'c', swap)  10.2 us
    ppermute x1, starting transfers between devices, per_device(): other = lax.ppermute(keep, 'c', swap)  4.35 us
    ppermute x3, starting transfers between devices, onward(): return lax.ppermute(array, ('c', axis), pairs)  3.88 us
    pallas_call x1, Pallas kernels, per_device(): call(inner_kernel, [VMEM] * 4, [VMEM] * 3, [inner_shape] * 3, 5 * product...  3.62 us
    ppermute x1, starting transfers between devices, per_device(): received = lax.ppermute(send, 'c', swap)  3.33 us
    pallas_call x1, Pallas kernels, per_device(): call(states_kernel, [SMEM] + [HBM] * 4, [VMEM] * 2, [state_shape] * 2, 2...  2.31 us
  transfers between devices with their start and end apart: 6, of which 2 were waited for; matrix products, arithmetic and copies ran while one was open for 0% of the time, Pallas kernels for 4%

profile of v5, /device:TPU:1, one launch (start us, length us, event | category | flops | bytes accessed | tf_op | source)
XLA Modules:
  0.0 93.6 jit_solution(17682986544294933957)
XLA Ops:
  0.6 2.3 %shard_map.67 = (f32[2048,128]{1,0:T(8,128)S(1)}, f32[2048,128]{1,0:T(8,128)S(1)}) custom-call(s32[1]{0:T(128)} %bitcast.places, bf16[128,2048]{1,0:T(8,128)(2,1)} %query.3, bf16[128,2048]{1,0:T(8,128)(2,1)} %key.3, bf16[128,2048]{1,0:T(8,128)(2,1)} %value.3, bf16[128,2048]{1,0:T(8,128)(2,1)} %gradient.3), custom_call_target="tpu_custom_call" | custom-call | flops 134217728 | bytes 4194304 | tf_op jit(solution)/shard_map/pallas_call | solution.py:153
  2.9 3.3 %collective-permute-start = (f32[2048,128]{1,0:T(8,128)S(1)}, f32[2048,128]{1,0:T(8,128)S(1)}, u32[]{:S(2)}, u32[]{:S(2)}) collective-permute-start(f32[2048,128]{1,0:T(8,128)S(1)} %get-tuple-element.22), channel_id=1, source_target_pairs={{0,4},{4,0},{1,5},{5,1},{2,6},{6,2},{3,7},{7,3},{8,12},{12,8},{9,1... | collective-permute-start | bytes 3145736 | tf_op jit(solution)/shard_map/ppermute | solution.py:165
  6.3 2.3 %collective-permute-done.received = f32[2048,128]{1,0:T(8,128)S(1)} collective-permute-done((f32[2048,128]{1,0:T(8,128)S(1)}, f32[2048,128]{1,0:T(8,128)S(1)}, u32[]{:S(2)}, u32[]{:S(2)}) %collective-permute-start) | collective-permute-done | bytes 1048608 | tf_op jit(solution)/shard_map/ppermute | solution.py:165
  8.6 0.1 shard_map.68
  8.7 0.0 copy-start.2
  8.7 0.0 copy-start.3
  8.7 34.6 %all_to_all.10.parts = f32[32,64,128]{2,1,0:T(8,128)S(1)} all-to-all(f32[32,64,128]{2,1,0:T(8,128)S(1)} %bitcast.5), channel_id=1, replica_groups=mesh['y'=4,'z'=8,'c'=2,'x'=4] {'y','z'}, dimensions={0} | all-to-all | bytes 2097152 | tf_op jit(solution)/shard_map/all_to_all | solution.py:169
  43.3 0.0 copy-start
  43.3 0.0 copy-start.1
  43.3 4.4 %collective-permute-start.4 = (f32[2048,128]{1,0:T(8,128)S(1)}, f32[2048,128]{1,0:T(8,128)S(1)}, u32[]{:S(2)}, u32[]{:S(2)}) collective-permute-start(f32[2048,128]{1,0:T(8,128)S(1)} %get-tuple-element.28.keep), channel_id=1, source_target_pairs={{0,4},{4,0},{1,5},{5,1},{2,6},{6,2},{3,7},{7,3},{8,12},{12,8},{9,1... | collective-permute-start | bytes 3145736 | tf_op jit(solution)/shard_map/ppermute | solution.py:180
  47.7 0.1 shard_map.69
  47.7 1.3 %collective-permute-start.3 = (f32[64,128]{1,0:T(8,128)S(1)}, f32[64,128]{1,0:T(8,128)S(1)}, u32[]{:S(2)}, u32[]{:S(2)}) collective-permute-start(f32[64,128]{1,0:T(8,128)S(1)} %shard_map.69), channel_id=1, source_target_pairs={{0,3},{7,4},{8,11},{15,12},{16,19},{23,20},{24,27},{31,28},{32,35}... | collective-permute-start | bytes 98312 | tf_op jit(solution)/shard_map/ppermute | solution.py:136
  49.0 1.3 %collective-permute-start.2 = (f32[64,128]{1,0:T(8,128)S(1)}, f32[64,128]{1,0:T(8,128)S(1)}, u32[]{:S(2)}, u32[]{:S(2)}) collective-permute-start(f32[64,128]{1,0:T(8,128)S(1)} %shard_map.69), channel_id=1, source_target_pairs={{0,2},{1,3},{6,4},{7,5},{8,10},{9,11},{14,12},{15,13},{16,18},{17,... | collective-permute-start | bytes 98312 | tf_op jit(solution)/shard_map/ppermute | solution.py:136
  50.3 1.3 %collective-permute-start.1 = (f32[64,128]{1,0:T(8,128)S(1)}, f32[64,128]{1,0:T(8,128)S(1)}, u32[]{:S(2)}, u32[]{:S(2)}) collective-permute-start(f32[64,128]{1,0:T(8,128)S(1)} %shard_map.69), channel_id=1, source_target_pairs={{0,1},{1,2},{2,3},{5,4},{6,5},{7,6},{8,9},{9,10},{10,11},{13,12},{... | collective-permute-start | bytes 98312 | tf_op jit(solution)/shard_map/ppermute | solution.py:136
  51.6 0.0 copy-done.2
  51.6 0.0 copy-done.3
  51.7 0.0 copy-done
  51.7 0.0 copy-done.1
  51.7 3.6 %shard_map.70 = (f32[128,2048]{1,0:T(8,128)S(1)}, f32[128,2048]{1,0:T(8,128)S(1)}, f32[128,2048]{1,0:T(8,128)S(1)}) custom-call(bf16[128,2048]{1,0:T(8,128)(2,1)S(1)} %copy-done, bf16[128,2048]{1,0:T(8,128)(2,1)S(1)} %copy-done.1, bf16[128,2048]{1,0:T(8,128)(2,1)S(1)} %copy-done.2, bf16[128,2048]{1,0:T(8,128)(2,1)S(1)} %copy-done.3), custom_call_target="tpu_custom_call" | custom-call | flops 335544320 | bytes 5242880 | tf_op jit(solution)/shard_map/pallas_call | solution.py:181
  55.3 0.0 collective-permute-done.3.refs_2_
  55.3 0.0 collective-permute-done.2.refs_1_
  55.3 0.0 collective-permute-done.1.refs_0_
  55.3 0.0 collective-permute-done.4.refs_3_
  55.3 0.1 shard_map.71
  55.4 23.9 %all_to_all.11 = f32[32,64,128]{2,1,0:T(8,128)S(1)} all-to-all(f32[32,64,128]{2,1,0:T(8,128)S(1)} %shard_map.71), channel_id=1, replica_groups=mesh['y'=4,'z'=8,'c'=2,'x'=4] {'y','z'}, dimensions={0} | all-to-all | bytes 2097152 | tf_op jit(solution)/shard_map/all_to_all | solution.py:198
  79.3 10.2 %collective-permute-start.5 = (f32[2048,128]{1,0:T(8,128)S(1)}, f32[2048,128]{1,0:T(8,128)S(1)}, u32[]{:S(2)}, u32[]{:S(2)}) collective-permute-start(f32[2048,128]{1,0:T(8,128)S(1)} %bitcast.3), channel_id=1, source_target_pairs={{0,4},{4,0},{1,5},{5,1},{2,6},{6,2},{3,7},{7,3},{8,12},{12,8},{9,1... | collective-permute-start | bytes 3145736 | tf_op jit(solution)/shard_map/ppermute | solution.py:199
  89.5 2.3 %collective-permute-done.5.refs_5_ = f32[2048,128]{1,0:T(8,128)S(1)} collective-permute-done((f32[2048,128]{1,0:T(8,128)S(1)}, f32[2048,128]{1,0:T(8,128)S(1)}, u32[]{:S(2)}, u32[]{:S(2)}) %collective-permute-start.5) | collective-permute-done | bytes 1048608 | tf_op jit(solution)/shard_map/ppermute | solution.py:199
  91.8 1.8 %shard_map.72 = (bf16[128,2048]{1,0:T(8,128)(2,1)}, bf16[128,2048]{1,0:T(8,128)(2,1)}, bf16[128,2048]{1,0:T(8,128)(2,1)}) custom-call(s32[1]{0:T(128)} %bitcast.places, bf16[128,2048]{1,0:T(8,128)(2,1)S(1)} %copy-done, bf16[128,2048]{1,0:T(8,128)(2,1)S(1)} %copy-done.1, bf16[128,2048]{1,0:T(8,128)(2,1)S(1)} %copy-done.2, bf16[128,2048]{1,0:T(8,128)(2,1)S(1)} %copy-done.3, ...), custom_call_target="tpu_custom_call" | custom-call | flops 201326592 | bytes 9961472 | tf_op jit(solution)/shard_map/pallas_call | solution.py:200
Async XLA Ops:
  2.9 5.6 %collective-permute-start = (f32[2048,128]{1,0:T(8,128)S(1)}, f32[2048,128]{1,0:T(8,128)S(1)}, u32[]{:S(2)}, u32[]{:S(2)}) collective-permute-start(f32[2048,128]{1,0:T(8,128)S(1)} %get-tuple-element.22), channel_id=1, source_target_pairs={{0,4},{4,0},{1,5},{5,1},{2,6},{6,2},{3,7},{7,3},{8,12},{12,8},{9,1... | collective-permute-start | bytes 3145736 | tf_op jit(solution)/shard_map/ppermute | solution.py:165
  8.7 43.0 %copy-start.2 = (bf16[128,2048]{1,0:T(8,128)(2,1)S(1)}, bf16[128,2048]{1,0:T(8,128)(2,1)}, u32[]{:S(2)}) copy-start(bf16[128,2048]{1,0:T(8,128)(2,1)} %value.3) | copy-start | bytes 1572868
  8.7 43.0 %copy-start.3 = (bf16[128,2048]{1,0:T(8,128)(2,1)S(1)}, bf16[128,2048]{1,0:T(8,128)(2,1)}, u32[]{:S(2)}) copy-start(bf16[128,2048]{1,0:T(8,128)(2,1)} %gradient.3) | copy-start | bytes 1572868
  43.3 8.3 %copy-start = (bf16[128,2048]{1,0:T(8,128)(2,1)S(1)}, bf16[128,2048]{1,0:T(8,128)(2,1)}, u32[]{:S(2)}) copy-start(bf16[128,2048]{1,0:T(8,128)(2,1)} %query.3) | copy-start | bytes 1572868
  43.3 8.4 %copy-start.1 = (bf16[128,2048]{1,0:T(8,128)(2,1)S(1)}, bf16[128,2048]{1,0:T(8,128)(2,1)}, u32[]{:S(2)}) copy-start(bf16[128,2048]{1,0:T(8,128)(2,1)} %key.3) | copy-start | bytes 1572868
  43.3 12.0 %collective-permute-start.4 = (f32[2048,128]{1,0:T(8,128)S(1)}, f32[2048,128]{1,0:T(8,128)S(1)}, u32[]{:S(2)}, u32[]{:S(2)}) collective-permute-start(f32[2048,128]{1,0:T(8,128)S(1)} %get-tuple-element.28.keep), channel_id=1, source_target_pairs={{0,4},{4,0},{1,5},{5,1},{2,6},{6,2},{3,7},{7,3},{8,12},{12,8},{9,1... | collective-permute-start | bytes 3145736 | tf_op jit(solution)/shard_map/ppermute | solution.py:180
  47.7 7.6 %collective-permute-start.3 = (f32[64,128]{1,0:T(8,128)S(1)}, f32[64,128]{1,0:T(8,128)S(1)}, u32[]{:S(2)}, u32[]{:S(2)}) collective-permute-start(f32[64,128]{1,0:T(8,128)S(1)} %shard_map.69), channel_id=1, source_target_pairs={{0,3},{7,4},{8,11},{15,12},{16,19},{23,20},{24,27},{31,28},{32,35}... | collective-permute-start | bytes 98312 | tf_op jit(solution)/shard_map/ppermute | solution.py:136
  49.0 6.3 %collective-permute-start.2 = (f32[64,128]{1,0:T(8,128)S(1)}, f32[64,128]{1,0:T(8,128)S(1)}, u32[]{:S(2)}, u32[]{:S(2)}) collective-permute-start(f32[64,128]{1,0:T(8,128)S(1)} %shard_map.69), channel_id=1, source_target_pairs={{0,2},{1,3},{6,4},{7,5},{8,10},{9,11},{14,12},{15,13},{16,18},{17,... | collective-permute-start | bytes 98312 | tf_op jit(solution)/shard_map/ppermute | solution.py:136
  50.3 5.0 %collective-permute-start.1 = (f32[64,128]{1,0:T(8,128)S(1)}, f32[64,128]{1,0:T(8,128)S(1)}, u32[]{:S(2)}, u32[]{:S(2)}) collective-permute-start(f32[64,128]{1,0:T(8,128)S(1)} %shard_map.69), channel_id=1, source_target_pairs={{0,1},{1,2},{2,3},{5,4},{6,5},{7,6},{8,9},{9,10},{10,11},{13,12},{... | collective-permute-start | bytes 98312 | tf_op jit(solution)/shard_map/ppermute | solution.py:136
  79.3 12.5 %collective-permute-start.5 = (f32[2048,128]{1,0:T(8,128)S(1)}, f32[2048,128]{1,0:T(8,128)S(1)}, u32[]{:S(2)}, u32[]{:S(2)}) collective-permute-start(f32[2048,128]{1,0:T(8,128)S(1)} %bitcast.3), channel_id=1, source_target_pairs={{0,4},{4,0},{1,5},{5,1},{2,6},{6,2},{3,7},{7,3},{8,12},{12,8},{9,1... | collective-permute-start | bytes 3145736 | tf_op jit(solution)/shard_map/ppermute | solution.py:199

commit v6 on v5

v6 whole, which is shorter than its diff:
```python
import functools

import jax
import jax.numpy as jnp
from jax import lax
from jax.experimental import pallas as pl
from jax.experimental.pallas import tpu as pltpu
from jax.sharding import Mesh
from jax.sharding import PartitionSpec as P

HEAD = 128
LOADS = 4
EARLY = 10
ROWS = ("x", "y", "z", "c")
SMEM = pl.BlockSpec(memory_space=pltpu.SMEM)
VMEM = pl.BlockSpec(memory_space=pltpu.VMEM)
HBM = pl.BlockSpec(memory_space=pltpu.HBM)
VMEM_LIMIT = 24 * 1024 * 1024
F32, BF16 = jnp.float32, jnp.bfloat16


def contract(lhs, rhs, lhs_dim, rhs_dim):
    return lax.dot_general(
        lhs, rhs, (((lhs_dim,), (rhs_dim,)), ((), ())), preferred_element_type=F32
    )


def states_kernel(places, query, key, value, gradient, q, k, v, g, keep, send, sems):
    first = places[0] == 0
    loads = sems.shape[1]
    part = query.shape[1] // loads
    pairs = ((key, k), (value, v), (query, q), (gradient, g))
    copies = []
    for n in range(loads):
        lanes = pl.ds(n * part, part)
        for t, (source, target) in enumerate(pairs):
            copy = pltpu.make_async_copy(source.at[:, lanes], target.at[:, lanes], sems.at[t, n])
            copy.start()
            copies.append(copy)
    for n in range(loads):
        for copy in copies[4 * n : 4 * n + 4]:
            copy.wait()
        for h in range(part // HEAD):
            rows = pl.ds(n * part + h * HEAD, HEAD)
            kv = contract(k[:, rows], v[:, rows], 0, 0)
            qo = contract(q[:, rows], g[:, rows], 0, 0)
            keep[rows, :] = jnp.where(first, kv, qo)
            send[rows, :] = jnp.where(first, qo, kv)


def inner_kernel(base, query, key, value, gradient, gq, gk, gv):
    count = query.shape[0]
    causal = lax.broadcasted_iota(jnp.int32, (count, count), 0) >= lax.broadcasted_iota(
        jnp.int32, (count, count), 1
    )
    for h in range(gq.shape[1] // HEAD):
        lanes = pl.ds(base + h * HEAD, HEAD)
        q, k, v, g = query[:, lanes], key[:, lanes], value[:, lanes], gradient[:, lanes]
        dv = jnp.where(causal, contract(g, v, 1, 1), 0.0).astype(BF16)
        qk = jnp.where(causal, contract(q, k, 1, 1), 0.0).astype(BF16)
        lanes = pl.ds(h * HEAD, HEAD)
        gq[:, lanes] = contract(dv, k, 1, 0)
        gk[:, lanes] = contract(dv, q, 0, 0)
        gv[:, lanes] = contract(qk, g, 0, 0)


def merge_kernel(keep, received, out):
    out[...] = keep[...] + received[...]


def total_kernel(parts, out):
    total = parts[0]
    for n in range(1, parts.shape[0]):
        total = total + parts[n]
    out[...] = total


def scan_kernel(places, parts, *refs):
    first = places[0] == 0
    count = parts.shape[0]
    out = refs[-1]
    total = refs[0][...]
    for plane in refs[1:-1]:
        total = total + plane[...]
    for n in range(count):
        place = jnp.where(first, n, count - 1 - n)
        out[place] = total
        total = total + parts[place]


def outputs_kernel(scale, whose, places, query, key, value, gradient, *refs):
    inner = (refs[:3], refs[3:6])
    states = refs[6:-5]
    outs = refs[-5:-2]
    held, sems = refs[-2:]
    loads = sems.shape[1]
    part = query.shape[1] // loads
    cut = inner[0][0].shape[1]

    def state(rows):
        total = states[0][rows, :]
        if whose:
            total = total + states[1][rows, :]
        return total.astype(BF16)

    def produce(tensors):
        copies = []
        for n in range(loads):
            for h in range(part // HEAD):
                at = n * part + h * HEAD
                lanes = pl.ds(at, HEAD)
                group, lane = (0, at) if at < cut else (1, at - cut)
                summed = state(lanes)
                for t in tensors:
                    source, dim = ((gradient, 1), (value, 1), (key, 0))[t]
                    result = contract(source[:, lanes], summed, 1, dim)
                    result = result + inner[group][t][:, pl.ds(lane, HEAD)]
                    held[t, n, :, pl.ds(h * HEAD, HEAD)] = (scale * result).astype(BF16)
            for t in tensors:
                copy = pltpu.make_async_copy(
                    held.at[t, n], outs[t].at[:, pl.ds(n * part, part)], sems.at[t, n]
                )
                copy.start()
                copies.append(copy)
        for copy in copies:
            copy.wait()

    @pl.when(places[0] == whose)
    def _():
        produce((0,))

    @pl.when(places[0] != whose)
    def _():
        produce((1, 2))


def call(kernel, in_specs, out_specs, out_shape, flops, moved, scratch=(), aliases=None):
    return pl.pallas_call(
        kernel,
        in_specs=in_specs,
        out_specs=out_specs,
        out_shape=out_shape,
        scratch_shapes=scratch,
        input_output_aliases=aliases or {},
        cost_estimate=pl.CostEstimate(flops=flops, bytes_accessed=moved, transcendentals=0),
        compiler_params=pltpu.CompilerParams(vmem_limit_bytes=VMEM_LIMIT),
    )


def onward(array, axis, count, step):
    pairs = [(i, i + step) for i in range(count - step)]
    pairs += [(count + i, count + i - step) for i in range(step, count)]
    return lax.ppermute(array, ("c", axis), pairs)


def per_device(sizes, scale, queries, key_row_matrix, value_row_matrix, output_gradient):
    tokens, width = queries.shape
    members = sizes["y"] * sizes["z"]
    places = lax.axis_index("c").astype(jnp.int32).reshape(1)
    swap = [(0, 1), (1, 0)]
    product = 2 * width * tokens * HEAD
    token_bytes = 2 * tokens * width
    state_bytes = 4 * width * HEAD
    token_shape = jax.ShapeDtypeStruct((tokens, width), BF16)
    state_shape = jax.ShapeDtypeStruct((width, HEAD), F32)
    parts_shape = jax.ShapeDtypeStruct((members, width // members, HEAD), F32)
    inputs = (queries, key_row_matrix, value_row_matrix, output_gradient)

    *inputs, keep, send = call(
        states_kernel,
        [SMEM] + [HBM] * 4,
        [VMEM] * 6,
        [token_shape] * 4 + [state_shape] * 2,
        2 * product,
        8 * token_bytes + 2 * state_bytes,
        [pltpu.SemaphoreType.DMA((4, LOADS))],
    )(places, *(pltpu.with_memory_space_constraint(a, pltpu.HBM) for a in inputs))

    def inner(base, span):
        return call(
            functools.partial(inner_kernel, base),
            [VMEM] * 4,
            [VMEM] * 3,
            [jax.ShapeDtypeStruct((tokens, span), F32)] * 3,
            5 * product * span // width,
            10 * token_bytes * span // width,
        )(*inputs)

    received = lax.ppermute(send, "c", swap)
    early = inner(0, EARLY * HEAD)
    received, early = lax.optimization_barrier((received, early))
    chip = call(
        merge_kernel, [VMEM] * 2, VMEM, state_shape, width * HEAD, 3 * state_bytes
    )(keep, received)
    parts = lax.all_to_all(chip.reshape(parts_shape.shape), ("y", "z"), 0, 0, tiled=True)
    parts, keep, inputs = lax.optimization_barrier((parts, keep, inputs))
    plane = call(
        total_kernel,
        [VMEM],
        VMEM,
        jax.ShapeDtypeStruct(parts_shape.shape[1:], F32),
        width * HEAD,
        state_bytes,
    )(parts)
    planes = [onward(plane, "x", sizes["x"], k) for k in range(1, sizes["x"])]
    other = lax.ppermute(keep, "c", swap)
    late = inner(EARLY * HEAD, width - EARLY * HEAD)
    planes, other, late = lax.optimization_barrier((planes, other, late))
    prefixes = call(
        scan_kernel,
        [SMEM] + [VMEM] * (1 + len(planes)),
        VMEM,
        parts_shape,
        width * HEAD,
        2 * state_bytes,
    )(places, parts, *planes)
    own = lax.all_to_all(prefixes, ("y", "z"), 0, 0, tiled=True).reshape(width, HEAD)
    theirs = lax.ppermute(own, "c", swap)

    def outputs(whose, states, results):
        return call(
            functools.partial(outputs_kernel, scale, whose),
            [SMEM] + [VMEM] * (10 + len(states)) + [HBM] * len(results),
            [HBM] * 3,
            [token_shape] * 3,
            3 * product // 2,
            7 * token_bytes + 2 * state_bytes,
            [
                pltpu.VMEM((3, LOADS, tokens, width // LOADS), BF16),
                pltpu.SemaphoreType.DMA((3, LOADS)),
            ],
            {11 + len(states) + n: n for n in range(len(results))},
        )(places, *inputs, *early, *late, *states, *results)

    results = outputs(0, (own,), ())
    return tuple(outputs(1, (theirs, other), tuple(results)))


def solution(mesh):
    sizes = {"y": 4, "z": 8, "c": 2, "x": 4}
    fine = Mesh(mesh.devices.reshape(tuple(sizes.values())), tuple(sizes))

    def program(queries, key_row_matrix, value_row_matrix, output_gradient):
        scale = float(HEAD * queries.shape[0]) ** -0.5
        spec = P(ROWS, None)
        return jax.shard_map(
            functools.partial(per_device, sizes, scale),
            mesh=fine,
            in_specs=(spec,) * 4,
            out_specs=(spec,) * 3,
            check_vma=False,
        )(queries, key_row_matrix, value_row_matrix, output_gradient)

    return program
```

time: 94.6 us -> 93.2 us (0.985)
  blocking collectives: 58.5 us -> 61.1 us
  starting transfers between devices: 21.8 us -> 19.2 us
  waiting for transfers between devices: 4.58 us -> 3.02 us
  Pallas kernels: 7.97 us -> 8.95 us
    all_to_all x1, blocking collectives: 23.9 us -> 26.6 us  [per_device(): lax.all_to_all(prefixes, ('y', 'z'), 0, 0, tiled=True).reshape(width, HEAD)]
    ppermute x1, starting transfers between devices: 10.2 us -> 7.66 us  [per_device(): theirs = lax.ppermute(own, 'c', swap)]
    ppermute x1, waiting for transfers between devices: 2.29 us -> 0.01 us  [per_device(): received = lax.ppermute(send, 'c', swap)]
    ppermute x3, waiting for transfers between devices: 0.01 us -> 2.12 us  [onward(): return lax.ppermute(array, ('c', axis), pairs)]
    ppermute x1, waiting for transfers between devices: 2.29 us -> 0.9 us  [per_device(): theirs = lax.ppermute(own, 'c', swap)]
    pallas_call x3 -> x5, Pallas kernels: 7.71 us -> 8.7 us  [the longest x2 3.76 us: inner(): call(functools.partial(inner_kernel, base), [VMEM] * 4, [VMEM] * 3, [jax....]
  transfers between devices with their start and end apart: 6 -> 6, of which waited for: 2 -> 3; matrix products, arithmetic and copies ran while one was open for 0% -> 0% of each run, Pallas kernels for 4% -> 6%
where the time goes in v6:
time: 93.2 us; the launch traced here: 93 us
  blocking collectives  61.1 us (66%)
  starting transfers between devices  19.2 us (21%)
  Pallas kernels  8.95 us (10%)
  waiting for transfers between devices  3.02 us (3%)
    all_to_all x1, blocking collectives, per_device(): lax.all_to_all(chip.reshape(parts_shape.shape), ('y', 'z'), 0, 0, tiled=T...  34.5 us
    all_to_all x1, blocking collectives, per_device(): lax.all_to_all(prefixes, ('y', 'z'), 0, 0, tiled=True).reshape(width, HEAD)  26.6 us
    ppermute x1, starting transfers between devices, per_device(): theirs = lax.ppermute(own, 'c', swap)  7.66 us
    ppermute x1, starting transfers between devices, per_device(): other = lax.ppermute(keep, 'c', swap)  4.36 us
    ppermute x3, starting transfers between devices, onward(): return lax.ppermute(array, ('c', axis), pairs)  3.88 us
    pallas_call x2, Pallas kernels, inner(): call(functools.partial(inner_kernel, base), [VMEM] * 4, [VMEM] * 3, [jax....  3.76 us
    ppermute x1, starting transfers between devices, per_device(): received = lax.ppermute(send, 'c', swap)  3.33 us
    pallas_call x2, Pallas kernels, outputs(): call(functools.partial(outputs_kernel, scale, whose), [SMEM] + [VMEM] * (...  2.63 us
  transfers between devices with their start and end apart: 6, of which 3 were waited for; matrix products, arithmetic and copies ran while one was open for 0% of the time, Pallas kernels for 6%

profile of v6, /device:TPU:1, one launch (start us, length us, event | category | flops | bytes accessed | tf_op | source)
XLA Modules:
  0.0 93.0 jit_solution(13016893580207467531)
XLA Ops:
  0.6 2.3 %shard_map.67 = (bf16[128,2048]{1,0:T(8,128)(2,1)S(1)}, bf16[128,2048]{1,0:T(8,128)(2,1)S(1)}, bf16[128,2048]{1,0:T(8,128)(2,1)S(1)}, bf16[128,2048]{1,0:T(8,128...) custom-call(s32[1]{0:T(128)} %bitcast.places, bf16[128,2048]{1,0:T(8,128)(2,1)} %query.1, ...), custom_call_target="tpu_custom_call" | custom-call | flops 134217728 | bytes 6291456 | tf_op jit(solution)/shard_map/pallas_call | solution.py:169
  3.0 3.3 %collective-permute-start = (f32[2048,128]{1,0:T(8,128)S(1)}, f32[2048,128]{1,0:T(8,128)S(1)}, u32[]{:S(2)}, u32[]{:S(2)}) collective-permute-start(f32[2048,128]{1,0:T(8,128)S(1)} %get-tuple-element.36), channel_id=1, source_target_pairs={{0,4},{4,0},{1,5},{5,1},{2,6},{6,2},{3,7},{7,3},{8,12},{12,8},{9,1... | collective-permute-start | bytes 3145736 | tf_op jit(solution)/shard_map/ppermute | solution.py:189
  6.3 2.3 %shard_map.68 = (f32[128,1280]{1,0:T(8,128)S(1)}, f32[128,1280]{1,0:T(8,128)S(1)}, f32[128,1280]{1,0:T(8,128)S(1)}) custom-call(bf16[128,2048]{1,0:T(8,128)(2,1)S(1)} %get-tuple-element.45.query, bf16[128,2048]{1,0:T(8,128)(2,1)S(1)} %get-tuple-element.46.key, bf16[128,2048]{1,0:T(8,128)(2,1)S(1)} %get-tuple-element.47.value, ...), custom_call_target="tpu_custom_call" | custom-call | flops 209715200 | bytes 3276800 | tf_op jit(solution)/shard_map/pallas_call | solution.py:180
  8.6 0.0 collective-permute-done.received
  8.6 0.1 shard_map.69
  8.7 34.5 %all_to_all.10.parts = f32[32,64,128]{2,1,0:T(8,128)S(1)} all-to-all(f32[32,64,128]{2,1,0:T(8,128)S(1)} %bitcast.5), channel_id=1, replica_groups=mesh['y'=4,'z'=8,'c'=2,'x'=4] {'y','z'}, dimensions={0} | all-to-all | bytes 2097152 | tf_op jit(solution)/shard_map/all_to_all | solution.py:195
  43.2 4.4 %collective-permute-start.4 = (f32[2048,128]{1,0:T(8,128)S(1)}, f32[2048,128]{1,0:T(8,128)S(1)}, u32[]{:S(2)}, u32[]{:S(2)}) collective-permute-start(f32[2048,128]{1,0:T(8,128)S(1)} %get-tuple-element.53.keep), channel_id=1, source_target_pairs={{0,4},{4,0},{1,5},{5,1},{2,6},{6,2},{3,7},{7,3},{8,12},{12,8},{9,1... | collective-permute-start | bytes 3145736 | tf_op jit(solution)/shard_map/ppermute | solution.py:206
  47.5 0.1 shard_map.70
  47.6 1.3 %collective-permute-start.3 = (f32[64,128]{1,0:T(8,128)S(1)}, f32[64,128]{1,0:T(8,128)S(1)}, u32[]{:S(2)}, u32[]{:S(2)}) collective-permute-start(f32[64,128]{1,0:T(8,128)S(1)} %shard_map.70), channel_id=1, source_target_pairs={{0,3},{7,4},{8,11},{15,12},{16,19},{23,20},{24,27},{31,28},{32,35}... | collective-permute-start | bytes 98312 | tf_op jit(solution)/shard_map/ppermute | solution.py:153
  48.9 1.3 %collective-permute-start.2 = (f32[64,128]{1,0:T(8,128)S(1)}, f32[64,128]{1,0:T(8,128)S(1)}, u32[]{:S(2)}, u32[]{:S(2)}) collective-permute-start(f32[64,128]{1,0:T(8,128)S(1)} %shard_map.70), channel_id=1, source_target_pairs={{0,2},{1,3},{6,4},{7,5},{8,10},{9,11},{14,12},{15,13},{16,18},{17,... | collective-permute-start | bytes 98312 | tf_op jit(solution)/shard_map/ppermute | solution.py:153
  50.2 1.3 %collective-permute-start.1 = (f32[64,128]{1,0:T(8,128)S(1)}, f32[64,128]{1,0:T(8,128)S(1)}, u32[]{:S(2)}, u32[]{:S(2)}) collective-permute-start(f32[64,128]{1,0:T(8,128)S(1)} %shard_map.70), channel_id=1, source_target_pairs={{0,1},{1,2},{2,3},{5,4},{6,5},{7,6},{8,9},{9,10},{10,11},{13,12},{... | collective-permute-start | bytes 98312 | tf_op jit(solution)/shard_map/ppermute | solution.py:153
  51.5 1.4 %shard_map.71 = (f32[128,768]{1,0:T(8,128)S(1)}, f32[128,768]{1,0:T(8,128)S(1)}, f32[128,768]{1,0:T(8,128)S(1)}) custom-call(bf16[128,2048]{1,0:T(8,128)(2,1)S(1)} %get-tuple-element.45.query, bf16[128,2048]{1,0:T(8,128)(2,1)S(1)} %get-tuple-element.46.key, bf16[128,2048]{1,0:T(8,128)(2,1)S(1)} %get-tuple-element.47.value, ...), custom_call_target="tpu_custom_call" | custom-call | flops 125829120 | bytes 1966080 | tf_op jit(solution)/shard_map/pallas_call | solution.py:180
  53.0 0.5 collective-permute-done.3.refs_2_
  53.5 1.6 %collective-permute-done.2.refs_1_ = f32[64,128]{1,0:T(8,128)S(1)} collective-permute-done((f32[64,128]{1,0:T(8,128)S(1)}, f32[64,128]{1,0:T(8,128)S(1)}, u32[]{:S(2)}, u32[]{:S(2)}) %collective-permute-start.2) | collective-permute-done | bytes 32800 | tf_op jit(solution)/shard_map/ppermute | solution.py:153
  55.1 0.0 collective-permute-done.1.refs_0_
  55.1 0.0 collective-permute-done.4.refs_7_
  55.1 0.1 shard_map.72
  55.2 26.6 %all_to_all.11 = f32[32,64,128]{2,1,0:T(8,128)S(1)} all-to-all(f32[32,64,128]{2,1,0:T(8,128)S(1)} %shard_map.72), channel_id=1, replica_groups=mesh['y'=4,'z'=8,'c'=2,'x'=4] {'y','z'}, dimensions={0} | all-to-all | bytes 2097152 | tf_op jit(solution)/shard_map/all_to_all | solution.py:217
  81.8 7.7 %collective-permute-start.5 = (f32[2048,128]{1,0:T(8,128)S(1)}, f32[2048,128]{1,0:T(8,128)S(1)}, u32[]{:S(2)}, u32[]{:S(2)}) collective-permute-start(f32[2048,128]{1,0:T(8,128)S(1)} %bitcast.3), channel_id=1, source_target_pairs={{0,4},{4,0},{1,5},{5,1},{2,6},{6,2},{3,7},{7,3},{8,12},{12,8},{9,1... | collective-permute-start | bytes 3145736 | tf_op jit(solution)/shard_map/ppermute | solution.py:218
  89.4 1.4 %shard_map.73 = (bf16[128,2048]{1,0:T(8,128)(2,1)}, bf16[128,2048]{1,0:T(8,128)(2,1)}, bf16[128,2048]{1,0:T(8,128)(2,1)}) custom-call(s32[1]{0:T(128)} %bitcast.places, bf16[128,2048]{1,0:T(8,128)(2,1)S(1)} %get-tuple-element.45.query, bf16[128,2048]{1,0:T(8,128)(2,1)S(1)} %get-tuple-element.46.key, bf16[128,2048]{1,0:T(8,128)(2,1)S(1)} %get-tuple-element.47.value, ...), custom_call_target="tpu_custom_call" | custom-call | flops 100663296 | bytes 5767168 | tf_op jit(solution)/shard_map/pallas_call | solution.py:221
  90.8 0.9 collective-permute-done.5.refs_6_
  91.7 1.2 %shard_map.74 = (bf16[128,2048]{1,0:T(8,128)(2,1)}, bf16[128,2048]{1,0:T(8,128)(2,1)}, bf16[128,2048]{1,0:T(8,128)(2,1)}) custom-call(s32[1]{0:T(128)} %bitcast.places, bf16[128,2048]{1,0:T(8,128)(2,1)S(1)} %get-tuple-element.45.query, bf16[128,2048]{1,0:T(8,128)(2,1)S(1)} %get-tuple-element.46.key, ...), custom_call_target="tpu_custom_call", output_to_operand_aliasing={{0}: (13, {}), {1}: (14, {}), {2}: (15, {})} | custom-call | flops 100663296 | bytes 5767168 | tf_op jit(solution)/shard_map/pallas_call | solution.py:221
Async XLA Ops:
  3.0 5.6 %collective-permute-start = (f32[2048,128]{1,0:T(8,128)S(1)}, f32[2048,128]{1,0:T(8,128)S(1)}, u32[]{:S(2)}, u32[]{:S(2)}) collective-permute-start(f32[2048,128]{1,0:T(8,128)S(1)} %get-tuple-element.36), channel_id=1, source_target_pairs={{0,4},{4,0},{1,5},{5,1},{2,6},{6,2},{3,7},{7,3},{8,12},{12,8},{9,1... | collective-permute-start | bytes 3145736 | tf_op jit(solution)/shard_map/ppermute | solution.py:189
  43.2 11.9 %collective-permute-start.4 = (f32[2048,128]{1,0:T(8,128)S(1)}, f32[2048,128]{1,0:T(8,128)S(1)}, u32[]{:S(2)}, u32[]{:S(2)}) collective-permute-start(f32[2048,128]{1,0:T(8,128)S(1)} %get-tuple-element.53.keep), channel_id=1, source_target_pairs={{0,4},{4,0},{1,5},{5,1},{2,6},{6,2},{3,7},{7,3},{8,12},{12,8},{9,1... | collective-permute-start | bytes 3145736 | tf_op jit(solution)/shard_map/ppermute | solution.py:206
  47.6 5.9 %collective-permute-start.3 = (f32[64,128]{1,0:T(8,128)S(1)}, f32[64,128]{1,0:T(8,128)S(1)}, u32[]{:S(2)}, u32[]{:S(2)}) collective-permute-start(f32[64,128]{1,0:T(8,128)S(1)} %shard_map.70), channel_id=1, source_target_pairs={{0,3},{7,4},{8,11},{15,12},{16,19},{23,20},{24,27},{31,28},{32,35}... | collective-permute-start | bytes 98312 | tf_op jit(solution)/shard_map/ppermute | solution.py:153
  48.9 6.2 %collective-permute-start.2 = (f32[64,128]{1,0:T(8,128)S(1)}, f32[64,128]{1,0:T(8,128)S(1)}, u32[]{:S(2)}, u32[]{:S(2)}) collective-permute-start(f32[64,128]{1,0:T(8,128)S(1)} %shard_map.70), channel_id=1, source_target_pairs={{0,2},{1,3},{6,4},{7,5},{8,10},{9,11},{14,12},{15,13},{16,18},{17,... | collective-permute-start | bytes 98312 | tf_op jit(solution)/shard_map/ppermute | solution.py:153
  50.2 4.9 %collective-permute-start.1 = (f32[64,128]{1,0:T(8,128)S(1)}, f32[64,128]{1,0:T(8,128)S(1)}, u32[]{:S(2)}, u32[]{:S(2)}) collective-permute-start(f32[64,128]{1,0:T(8,128)S(1)} %shard_map.70), channel_id=1, source_target_pairs={{0,1},{1,2},{2,3},{5,4},{6,5},{7,6},{8,9},{9,10},{10,11},{13,12},{... | collective-permute-start | bytes 98312 | tf_op jit(solution)/shard_map/ppermute | solution.py:153
  81.8 9.9 %collective-permute-start.5 = (f32[2048,128]{1,0:T(8,128)S(1)}, f32[2048,128]{1,0:T(8,128)S(1)}, u32[]{:S(2)}, u32[]{:S(2)}) collective-permute-start(f32[2048,128]{1,0:T(8,128)S(1)} %bitcast.3), channel_id=1, source_target_pairs={{0,4},{4,0},{1,5},{5,1},{2,6},{6,2},{3,7},{7,3},{8,12},{12,8},{9,1... | collective-permute-start | bytes 3145736 | tf_op jit(solution)/shard_map/ppermute | solution.py:218

commit v7 on v6

--- a/solution.py
+++ b/solution.py
@@ -75,7 +75,7 @@
     out[...] = total
 
 
-def scan_kernel(places, parts, *refs):
+def scan_kernel(order, places, parts, *refs):
     first = places[0] == 0
     count = parts.shape[0]
     out = refs[-1]
@@ -83,7 +83,7 @@
     for plane in refs[1:-1]:
         total = total + plane[...]
     for n in range(count):
-        place = jnp.where(first, n, count - 1 - n)
+        place = jnp.where(first, order[n], order[count - 1 - n])
         out[place] = total
         total = total + parts[place]
 
@@ -98,10 +98,7 @@
     cut = inner[0][0].shape[1]
 
     def state(rows):
-        total = states[0][rows, :]
-        if whose:
-            total = total + states[1][rows, :]
-        return total.astype(BF16)
+        return states[0][rows, :].astype(BF16)
 
     def produce(tensors):
         copies = []
@@ -147,6 +144,25 @@
     )
 
 
+def order_of(sizes):
+    rows, depths = sizes["y"], sizes["z"]
+    last = rows * depths - 1
+    return [last - (n % depths * rows + n // depths) for n in range(last + 1)]
+
+
+def exchange(sizes, array):
+    order = order_of(sizes)
+    members = sorted(range(len(order)), key=lambda n: order[n])
+    groups = [
+        [(n * sizes["c"] + c) * sizes["x"] + x for n in members]
+        for c in range(sizes["c"])
+        for x in range(sizes["x"])
+    ]
+    return lax.all_to_all(
+        array, tuple(sizes), 0, 0, tiled=True, axis_index_groups=groups
+    )
+
+
 def onward(array, axis, count, step):
     pairs = [(i, i + step) for i in range(count - step)]
     pairs += [(count + i, count + i - step) for i in range(step, count)]
@@ -192,8 +208,8 @@
     chip = call(
         merge_kernel, [VMEM] * 2, VMEM, state_shape, width * HEAD, 3 * state_bytes
     )(keep, received)
-    parts = lax.all_to_all(chip.reshape(parts_shape.shape), ("y", "z"), 0, 0, tiled=True)
-    parts, keep, inputs = lax.optimization_barrier((parts, keep, inputs))
+    parts = exchange(sizes, chip.reshape(parts_shape.shape))
+    parts, inputs = lax.optimization_barrier((parts, inputs))
     plane = call(
         total_kernel,
         [VMEM],
@@ -203,19 +219,21 @@
         state_bytes,
     )(parts)
     planes = [onward(plane, "x", sizes["x"], k) for k in range(1, sizes["x"])]
-    other = lax.ppermute(keep, "c", swap)
     late = inner(EARLY * HEAD, width - EARLY * HEAD)
-    planes, other, late = lax.optimization_barrier((planes, other, late))
+    planes, late = lax.optimization_barrier((planes, late))
     prefixes = call(
-        scan_kernel,
+        functools.partial(scan_kernel, order_of(sizes)),
         [SMEM] + [VMEM] * (1 + len(planes)),
         VMEM,
         parts_shape,
         width * HEAD,
         2 * state_bytes,
     )(places, parts, *planes)
-    own = lax.all_to_all(prefixes, ("y", "z"), 0, 0, tiled=True).reshape(width, HEAD)
-    theirs = lax.ppermute(own, "c", swap)
+    own = exchange(sizes, prefixes).reshape(width, HEAD)
+    onto = call(
+        merge_kernel, [VMEM] * 2, VMEM, state_shape, width * HEAD, 3 * state_bytes
+    )(own, keep)
+    theirs = lax.ppermute(onto, "c", swap)
 
     def outputs(whose, states, results):
         return call(
@@ -233,7 +251,7 @@
         )(places, *inputs, *early, *late, *states, *results)
 
     results = outputs(0, (own,), ())
-    return tuple(outputs(1, (theirs, other), tuple(results)))
+    return tuple(outputs(1, (theirs,), tuple(results)))
 
 
 def solution(mesh):

time: 93.2 us -> 88.6 us (0.951)
  starting transfers between devices: 19.2 us -> 14.9 us
    ppermute x2 -> x1, starting transfers between devices: 12 us -> 7.74 us  [per_device(): theirs = lax.ppermute(onto, 'c', swap)]
  transfers between devices with their start and end apart: 6 -> 5, of which waited for: 3 -> 3; matrix products, arithmetic and copies ran while one was open for 0% -> 0% of each run, Pallas kernels for 6% -> 6%
where the time goes in v7:
time: 88.6 us; the launch traced here: 88.3 us
  blocking collectives  60.6 us (68%)
  starting transfers between devices  14.9 us (17%)
  Pallas kernels  9.05 us (10%)
  waiting for transfers between devices  3.02 us (3%)
    all_to_all x2, blocking collectives, exchange(): lax.all_to_all(array, tuple(sizes), 0, 0, tiled=True, axis_index_groups=g...  60.6 us
    ppermute x1, starting transfers between devices, per_device(): theirs = lax.ppermute(onto, 'c', swap)  7.74 us
    ppermute x3, starting transfers between devices, onward(): return lax.ppermute(array, ('c', axis), pairs)  3.88 us
    pallas_call x2, Pallas kernels, inner(): call(functools.partial(inner_kernel, base), [VMEM] * 4, [VMEM] * 3, [jax....  3.76 us
    ppermute x1, starting transfers between devices, per_device(): received = lax.ppermute(send, 'c', swap)  3.33 us
    pallas_call x2, Pallas kernels, outputs(): call(functools.partial(outputs_kernel, scale, whose), [SMEM] + [VMEM] * (...  2.62 us
    pallas_call x1, Pallas kernels, per_device(): call(states_kernel, [SMEM] + [HBM] * 4, [VMEM] * 6, [token_shape] * 4 + [...  2.31 us
    ppermute x3, waiting for transfers between devices, onward(): return lax.ppermute(array, ('c', axis), pairs)  2.12 us
  transfers between devices with their start and end apart: 5, of which 3 were waited for; matrix products, arithmetic and copies ran while one was open for 0% of the time, Pallas kernels for 6%

profile of v7, /device:TPU:1, one launch (start us, length us, event | category | flops | bytes accessed | tf_op | source)
XLA Modules:
  0.0 88.3 jit_solution(2490475148238421567)
XLA Ops:
  0.6 2.3 %shard_map.67 = (bf16[128,2048]{1,0:T(8,128)(2,1)S(1)}, bf16[128,2048]{1,0:T(8,128)(2,1)S(1)}, bf16[128,2048]{1,0:T(8,128)(2,1)S(1)}, bf16[128,2048]{1,0:T(8,128...) custom-call(s32[1]{0:T(128)} %bitcast.places, bf16[128,2048]{1,0:T(8,128)(2,1)} %query.1, ...), custom_call_target="tpu_custom_call" | custom-call | flops 134217728 | bytes 6291456 | tf_op jit(solution)/shard_map/pallas_call | solution.py:185
  3.0 3.3 %collective-permute-start = (f32[2048,128]{1,0:T(8,128)S(1)}, f32[2048,128]{1,0:T(8,128)S(1)}, u32[]{:S(2)}, u32[]{:S(2)}) collective-permute-start(f32[2048,128]{1,0:T(8,128)S(1)} %get-tuple-element.34), channel_id=1, source_target_pairs={{0,4},{4,0},{1,5},{5,1},{2,6},{6,2},{3,7},{7,3},{8,12},{12,8},{9,1... | collective-permute-start | bytes 3145736 | tf_op jit(solution)/shard_map/ppermute | solution.py:205
  6.3 2.3 %shard_map.68 = (f32[128,1280]{1,0:T(8,128)S(1)}, f32[128,1280]{1,0:T(8,128)S(1)}, f32[128,1280]{1,0:T(8,128)S(1)}) custom-call(bf16[128,2048]{1,0:T(8,128)(2,1)S(1)} %get-tuple-element.43.query, bf16[128,2048]{1,0:T(8,128)(2,1)S(1)} %get-tuple-element.44.key, bf16[128,2048]{1,0:T(8,128)(2,1)S(1)} %get-tuple-element.45.value, ...), custom_call_target="tpu_custom_call" | custom-call | flops 209715200 | bytes 3276800 | tf_op jit(solution)/shard_map/pallas_call | solution.py:196
  8.6 0.0 collective-permute-done.received
  8.6 0.1 shard_map.69
  8.7 33.0 %all_to_all.10.parts = f32[32,64,128]{2,1,0:T(8,128)S(1)} all-to-all(f32[32,64,128]{2,1,0:T(8,128)S(1)} %bitcast.5), channel_id=1, replica_groups={{248,184,120,56,240,176,112,48,232,168,104,40,224,160,96,32,216,152,88,..., dimensions={0} | all-to-all | bytes 2097152 | tf_op jit(solution)/shard_map/all_to_all | solution.py:161
  41.7 0.1 shard_map.70
  41.8 1.3 %collective-permute-start.3 = (f32[64,128]{1,0:T(8,128)S(1)}, f32[64,128]{1,0:T(8,128)S(1)}, u32[]{:S(2)}, u32[]{:S(2)}) collective-permute-start(f32[64,128]{1,0:T(8,128)S(1)} %shard_map.70), channel_id=1, source_target_pairs={{0,3},{7,4},{8,11},{15,12},{16,19},{23,20},{24,27},{31,28},{32,35}... | collective-permute-start | bytes 98312 | tf_op jit(solution)/shard_map/ppermute | solution.py:169
  43.1 1.3 %collective-permute-start.2 = (f32[64,128]{1,0:T(8,128)S(1)}, f32[64,128]{1,0:T(8,128)S(1)}, u32[]{:S(2)}, u32[]{:S(2)}) collective-permute-start(f32[64,128]{1,0:T(8,128)S(1)} %shard_map.70), channel_id=1, source_target_pairs={{0,2},{1,3},{6,4},{7,5},{8,10},{9,11},{14,12},{15,13},{16,18},{17,... | collective-permute-start | bytes 98312 | tf_op jit(solution)/shard_map/ppermute | solution.py:169
  44.4 1.3 %collective-permute-start.1 = (f32[64,128]{1,0:T(8,128)S(1)}, f32[64,128]{1,0:T(8,128)S(1)}, u32[]{:S(2)}, u32[]{:S(2)}) collective-permute-start(f32[64,128]{1,0:T(8,128)S(1)} %shard_map.70), channel_id=1, source_target_pairs={{0,1},{1,2},{2,3},{5,4},{6,5},{7,6},{8,9},{9,10},{10,11},{13,12},{... | collective-permute-start | bytes 98312 | tf_op jit(solution)/shard_map/ppermute | solution.py:169
  45.7 1.4 %shard_map.71 = (f32[128,768]{1,0:T(8,128)S(1)}, f32[128,768]{1,0:T(8,128)S(1)}, f32[128,768]{1,0:T(8,128)S(1)}) custom-call(bf16[128,2048]{1,0:T(8,128)(2,1)S(1)} %get-tuple-element.43.query, bf16[128,2048]{1,0:T(8,128)(2,1)S(1)} %get-tuple-element.44.key, bf16[128,2048]{1,0:T(8,128)(2,1)S(1)} %get-tuple-element.45.value, ...), custom_call_target="tpu_custom_call" | custom-call | flops 125829120 | bytes 1966080 | tf_op jit(solution)/shard_map/pallas_call | solution.py:196
  47.2 0.5 collective-permute-done.3.refs_2_
  47.7 1.6 %collective-permute-done.2.refs_1_ = f32[64,128]{1,0:T(8,128)S(1)} collective-permute-done((f32[64,128]{1,0:T(8,128)S(1)}, f32[64,128]{1,0:T(8,128)S(1)}, u32[]{:S(2)}, u32[]{:S(2)}) %collective-permute-start.2) | collective-permute-done | bytes 32800 | tf_op jit(solution)/shard_map/ppermute | solution.py:169
  49.3 0.0 collective-permute-done.1.refs_0_
  49.3 0.1 shard_map.72
  49.4 27.6 %all_to_all.11 = f32[32,64,128]{2,1,0:T(8,128)S(1)} all-to-all(f32[32,64,128]{2,1,0:T(8,128)S(1)} %shard_map.72), channel_id=1, replica_groups={{248,184,120,56,240,176,112,48,232,168,104,40,224,160,96,32,216,152,88,..., dimensions={0} | all-to-all | bytes 2097152 | tf_op jit(solution)/shard_map/all_to_all | solution.py:161
  77.0 0.1 shard_map.73
  77.1 7.7 %collective-permute-start.4 = (f32[2048,128]{1,0:T(8,128)S(1)}, f32[2048,128]{1,0:T(8,128)S(1)}, u32[]{:S(2)}, u32[]{:S(2)}) collective-permute-start(f32[2048,128]{1,0:T(8,128)S(1)} %shard_map.73), channel_id=1, source_target_pairs={{0,4},{4,0},{1,5},{5,1},{2,6},{6,2},{3,7},{7,3},{8,12},{12,8},{9,1... | collective-permute-start | bytes 3145736 | tf_op jit(solution)/shard_map/ppermute | solution.py:236
  84.8 1.4 %shard_map.74 = (bf16[128,2048]{1,0:T(8,128)(2,1)}, bf16[128,2048]{1,0:T(8,128)(2,1)}, bf16[128,2048]{1,0:T(8,128)(2,1)}) custom-call(s32[1]{0:T(128)} %bitcast.places, bf16[128,2048]{1,0:T(8,128)(2,1)S(1)} %get-tuple-element.43.query, bf16[128,2048]{1,0:T(8,128)(2,1)S(1)} %get-tuple-element.44.key, bf16[128,2048]{1,0:T(8,128)(2,1)S(1)} %get-tuple-element.45.value, ...), custom_call_target="tpu_custom_call" | custom-call | flops 100663296 | bytes 5767168 | tf_op jit(solution)/shard_map/pallas_call | solution.py:239
  86.2 0.9 %collective-permute-done.4.refs_6_ = f32[2048,128]{1,0:T(8,128)S(1)} collective-permute-done((f32[2048,128]{1,0:T(8,128)S(1)}, f32[2048,128]{1,0:T(8,128)S(1)}, u32[]{:S(2)}, u32[]{:S(2)}) %collective-permute-start.4) | collective-permute-done | bytes 1048608 | tf_op jit(solution)/shard_map/ppermute | solution.py:236
  87.1 1.2 %shard_map.75 = (bf16[128,2048]{1,0:T(8,128)(2,1)}, bf16[128,2048]{1,0:T(8,128)(2,1)}, bf16[128,2048]{1,0:T(8,128)(2,1)}) custom-call(s32[1]{0:T(128)} %bitcast.places, bf16[128,2048]{1,0:T(8,128)(2,1)S(1)} %get-tuple-element.43.query, bf16[128,2048]{1,0:T(8,128)(2,1)S(1)} %get-tuple-element.44.key, ...), custom_call_target="tpu_custom_call", output_to_operand_aliasing={{0}: (12, {}), {1}: (13, {}), {2}: (14, {})} | custom-call | flops 100663296 | bytes 5767168 | tf_op jit(solution)/shard_map/pallas_call | solution.py:239
Async XLA Ops:
  3.0 5.6 %collective-permute-start = (f32[2048,128]{1,0:T(8,128)S(1)}, f32[2048,128]{1,0:T(8,128)S(1)}, u32[]{:S(2)}, u32[]{:S(2)}) collective-permute-start(f32[2048,128]{1,0:T(8,128)S(1)} %get-tuple-element.34), channel_id=1, source_target_pairs={{0,4},{4,0},{1,5},{5,1},{2,6},{6,2},{3,7},{7,3},{8,12},{12,8},{9,1... | collective-permute-start | bytes 3145736 | tf_op jit(solution)/shard_map/ppermute | solution.py:205
  41.8 5.9 %collective-permute-start.3 = (f32[64,128]{1,0:T(8,128)S(1)}, f32[64,128]{1,0:T(8,128)S(1)}, u32[]{:S(2)}, u32[]{:S(2)}) collective-permute-start(f32[64,128]{1,0:T(8,128)S(1)} %shard_map.70), channel_id=1, source_target_pairs={{0,3},{7,4},{8,11},{15,12},{16,19},{23,20},{24,27},{31,28},{32,35}... | collective-permute-start | bytes 98312 | tf_op jit(solution)/shard_map/ppermute | solution.py:169
  43.1 6.2 %collective-permute-start.2 = (f32[64,128]{1,0:T(8,128)S(1)}, f32[64,128]{1,0:T(8,128)S(1)}, u32[]{:S(2)}, u32[]{:S(2)}) collective-permute-start(f32[64,128]{1,0:T(8,128)S(1)} %shard_map.70), channel_id=1, source_target_pairs={{0,2},{1,3},{6,4},{7,5},{8,10},{9,11},{14,12},{15,13},{16,18},{17,... | collective-permute-start | bytes 98312 | tf_op jit(solution)/shard_map/ppermute | solution.py:169
  44.4 4.9 %collective-permute-start.1 = (f32[64,128]{1,0:T(8,128)S(1)}, f32[64,128]{1,0:T(8,128)S(1)}, u32[]{:S(2)}, u32[]{:S(2)}) collective-permute-start(f32[64,128]{1,0:T(8,128)S(1)} %shard_map.70), channel_id=1, source_target_pairs={{0,1},{1,2},{2,3},{5,4},{6,5},{7,6},{8,9},{9,10},{10,11},{13,12},{... | collective-permute-start | bytes 98312 | tf_op jit(solution)/shard_map/ppermute | solution.py:169
  77.1 10.0 %collective-permute-start.4 = (f32[2048,128]{1,0:T(8,128)S(1)}, f32[2048,128]{1,0:T(8,128)S(1)}, u32[]{:S(2)}, u32[]{:S(2)}) collective-permute-start(f32[2048,128]{1,0:T(8,128)S(1)} %shard_map.73), channel_id=1, source_target_pairs={{0,4},{4,0},{1,5},{5,1},{2,6},{6,2},{3,7},{7,3},{8,12},{12,8},{9,1... | collective-permute-start | bytes 3145736 | tf_op jit(solution)/shard_map/ppermute | solution.py:236

commit v8 on v7

--- a/solution.py
+++ b/solution.py
@@ -10,7 +10,6 @@
 
 HEAD = 128
 LOADS = 4
-EARLY = 10
 ROWS = ("x", "y", "z", "c")
 SMEM = pl.BlockSpec(memory_space=pltpu.SMEM)
 VMEM = pl.BlockSpec(memory_space=pltpu.VMEM)
@@ -25,47 +24,87 @@
     )
 
 
-def states_kernel(places, query, key, value, gradient, q, k, v, g, keep, send, sems):
-    first = places[0] == 0
+def load(pairs, sems):
     loads = sems.shape[1]
-    part = query.shape[1] // loads
-    pairs = ((key, k), (value, v), (query, q), (gradient, g))
+    width = pairs[0][0].shape[1] // loads
     copies = []
     for n in range(loads):
-        lanes = pl.ds(n * part, part)
+        lanes = pl.ds(n * width, width)
         for t, (source, target) in enumerate(pairs):
             copy = pltpu.make_async_copy(source.at[:, lanes], target.at[:, lanes], sems.at[t, n])
             copy.start()
             copies.append(copy)
+    return copies
+
+
+def states(pairs, sems, out):
+    copies = load(pairs, sems)
+    lhs, rhs = (target for _, target in pairs)
+    loads = sems.shape[1]
+    span = lhs.shape[1] // loads
     for n in range(loads):
-        for copy in copies[4 * n : 4 * n + 4]:
+        for copy in copies[2 * n : 2 * n + 2]:
             copy.wait()
-        for h in range(part // HEAD):
-            rows = pl.ds(n * part + h * HEAD, HEAD)
-            kv = contract(k[:, rows], v[:, rows], 0, 0)
-            qo = contract(q[:, rows], g[:, rows], 0, 0)
-            keep[rows, :] = jnp.where(first, kv, qo)
-            send[rows, :] = jnp.where(first, qo, kv)
-
-
-def inner_kernel(base, query, key, value, gradient, gq, gk, gv):
+        for h in range(span // HEAD):
+            rows = pl.ds(n * span + h * HEAD, HEAD)
+            out[rows, :] = contract(lhs[:, rows], rhs[:, rows], 0, 0)
+
+
+def send_kernel(core, query, key, value, gradient, send, left, right, sems):
+    @pl.when(core[0] == 0)
+    def _():
+        states(((query, left), (gradient, right)), sems, send)
+
+    @pl.when(core[0] != 0)
+    def _():
+        states(((key, left), (value, right)), sems, send)
+
+
+def keep_kernel(core, query, key, value, gradient, keep, q, k, v, g, sems, more):
+    @pl.when(core[0] == 0)
+    def _():
+        rest = load(((query, q), (gradient, g)), more)
+        states(((key, k), (value, v)), sems, keep)
+        for copy in rest:
+            copy.wait()
+
+    @pl.when(core[0] != 0)
+    def _():
+        rest = load(((key, k), (value, v)), more)
+        states(((query, q), (gradient, g)), sems, keep)
+        for copy in rest:
+            copy.wait()
+
+
+def inner_products(query, key, value, gradient, gq, gk, gv):
     count = query.shape[0]
     causal = lax.broadcasted_iota(jnp.int32, (count, count), 0) >= lax.broadcasted_iota(
         jnp.int32, (count, count), 1
     )
-    for h in range(gq.shape[1] // HEAD):
-        lanes = pl.ds(base + h * HEAD, HEAD)
+    for h in range(query.shape[1] // HEAD):
+        lanes = pl.ds(h * HEAD, HEAD)
         q, k, v, g = query[:, lanes], key[:, lanes], value[:, lanes], gradient[:, lanes]
         dv = jnp.where(causal, contract(g, v, 1, 1), 0.0).astype(BF16)
         qk = jnp.where(causal, contract(q, k, 1, 1), 0.0).astype(BF16)
-        lanes = pl.ds(h * HEAD, HEAD)
         gq[:, lanes] = contract(dv, k, 1, 0)
         gk[:, lanes] = contract(dv, q, 0, 0)
         gv[:, lanes] = contract(qk, g, 0, 0)
 
 
-def merge_kernel(keep, received, out):
-    out[...] = keep[...] + received[...]
+def merge_kernel(core, keep, received, *refs):
+    @pl.when(core[0] == 0)
+    def _():
+        inner_products(*refs[:4], *refs[5:])
+
+    refs[4][...] = keep[...] + received[...]
+
+
+def onto_kernel(core, own, keep, *refs):
+    @pl.when(core[0] != 0)
+    def _():
+        inner_products(*refs[:4], *refs[8:])
+
+    refs[7][...] = own[...] + keep[...]
 
 
 def total_kernel(parts, out):
@@ -89,16 +128,15 @@
 
 
 def outputs_kernel(scale, whose, places, query, key, value, gradient, *refs):
-    inner = (refs[:3], refs[3:6])
-    states = refs[6:-5]
+    inner = refs[:3]
+    sums = refs[3:-5]
     outs = refs[-5:-2]
     held, sems = refs[-2:]
     loads = sems.shape[1]
     part = query.shape[1] // loads
-    cut = inner[0][0].shape[1]
 
     def state(rows):
-        return states[0][rows, :].astype(BF16)
+        return sums[0][rows, :].astype(BF16)
 
     def produce(tensors):
         copies = []
@@ -106,12 +144,11 @@
             for h in range(part // HEAD):
                 at = n * part + h * HEAD
                 lanes = pl.ds(at, HEAD)
-                group, lane = (0, at) if at < cut else (1, at - cut)
                 summed = state(lanes)
                 for t in tensors:
                     source, dim = ((gradient, 1), (value, 1), (key, 0))[t]
                     result = contract(source[:, lanes], summed, 1, dim)
-                    result = result + inner[group][t][:, pl.ds(lane, HEAD)]
+                    result = result + inner[t][:, lanes]
                     held[t, n, :, pl.ds(h * HEAD, HEAD)] = (scale * result).astype(BF16)
             for t in tensors:
                 copy = pltpu.make_async_copy(
@@ -182,34 +219,37 @@
     parts_shape = jax.ShapeDtypeStruct((members, width // members, HEAD), F32)
     inputs = (queries, key_row_matrix, value_row_matrix, output_gradient)
 
-    *inputs, keep, send = call(
-        states_kernel,
+    inner_shape = jax.ShapeDtypeStruct((tokens, width), F32)
+    resting = [pltpu.with_memory_space_constraint(a, pltpu.HBM) for a in inputs]
+    send = call(
+        send_kernel,
         [SMEM] + [HBM] * 4,
-        [VMEM] * 6,
-        [token_shape] * 4 + [state_shape] * 2,
-        2 * product,
-        8 * token_bytes + 2 * state_bytes,
-        [pltpu.SemaphoreType.DMA((4, LOADS))],
-    )(places, *(pltpu.with_memory_space_constraint(a, pltpu.HBM) for a in inputs))
-
-    def inner(base, span):
-        return call(
-            functools.partial(inner_kernel, base),
-            [VMEM] * 4,
-            [VMEM] * 3,
-            [jax.ShapeDtypeStruct((tokens, span), F32)] * 3,
-            5 * product * span // width,
-            10 * token_bytes * span // width,
-        )(*inputs)
-
+        VMEM,
+        state_shape,
+        product,
+        2 * token_bytes + state_bytes,
+        [pltpu.VMEM((tokens, width), BF16)] * 2 + [pltpu.SemaphoreType.DMA((2, LOADS))],
+    )(places, *resting)
     received = lax.ppermute(send, "c", swap)
-    early = inner(0, EARLY * HEAD)
-    received, early = lax.optimization_barrier((received, early))
-    chip = call(
-        merge_kernel, [VMEM] * 2, VMEM, state_shape, width * HEAD, 3 * state_bytes
-    )(keep, received)
+    keep, *inputs = call(
+        keep_kernel,
+        [SMEM] + [HBM] * 4,
+        [VMEM] * 5,
+        [state_shape] + [token_shape] * 4,
+        product,
+        8 * token_bytes + state_bytes,
+        [pltpu.SemaphoreType.DMA((2, LOADS))] * 2,
+    )(places, *resting)
+    received, keep = lax.optimization_barrier((received, keep))
+    chip, *inner = call(
+        merge_kernel,
+        [SMEM] + [VMEM] * 6,
+        [VMEM] * 4,
+        [state_shape] + [inner_shape] * 3,
+        5 * product,
+        10 * token_bytes + 3 * state_bytes,
+    )(places, keep, received, *inputs)
     parts = exchange(sizes, chip.reshape(parts_shape.shape))
-    parts, inputs = lax.optimization_barrier((parts, inputs))
     plane = call(
         total_kernel,
         [VMEM],
@@ -219,8 +259,6 @@
         state_bytes,
     )(parts)
     planes = [onward(plane, "x", sizes["x"], k) for k in range(1, sizes["x"])]
-    late = inner(EARLY * HEAD, width - EARLY * HEAD)
-    planes, late = lax.optimization_barrier((planes, late))
     prefixes = call(
         functools.partial(scan_kernel, order_of(sizes)),
         [SMEM] + [VMEM] * (1 + len(planes)),
@@ -230,15 +268,21 @@
         2 * state_bytes,
     )(places, parts, *planes)
     own = exchange(sizes, prefixes).reshape(width, HEAD)
-    onto = call(
-        merge_kernel, [VMEM] * 2, VMEM, state_shape, width * HEAD, 3 * state_bytes
-    )(own, keep)
+    onto, *inner = call(
+        onto_kernel,
+        [SMEM] + [VMEM] * 9,
+        [VMEM] * 4,
+        [state_shape] + [inner_shape] * 3,
+        5 * product,
+        10 * token_bytes + 3 * state_bytes,
+        aliases={7 + n: 1 + n for n in range(3)},
+    )(places, own, keep, *inputs, *inner)
     theirs = lax.ppermute(onto, "c", swap)
 
     def outputs(whose, states, results):
         return call(
             functools.partial(outputs_kernel, scale, whose),
-            [SMEM] + [VMEM] * (10 + len(states)) + [HBM] * len(results),
+            [SMEM] + [VMEM] * (7 + len(states)) + [HBM] * len(results),
             [HBM] * 3,
             [token_shape] * 3,
             3 * product // 2,
@@ -247,8 +291,8 @@
                 pltpu.VMEM((3, LOADS, tokens, width // LOADS), BF16),
                 pltpu.SemaphoreType.DMA((3, LOADS)),
             ],
-            {11 + len(states) + n: n for n in range(len(results))},
-        )(places, *inputs, *early, *late, *states, *results)
+            {8 + len(states) + n: n for n in range(len(results))},
+        )(places, *inputs, *inner, *states, *results)
 
     results = outputs(0, (own,), ())
     return tuple(outputs(1, (theirs,), tuple(results)))

time: 88.6 us -> 85.3 us (0.963)
  blocking collectives: 60.6 us -> 55.7 us
  waiting for transfers between devices: 3.02 us -> 4.63 us
  Pallas kernels: 9.05 us -> 10.6 us
  starting transfers between devices: 14.9 us -> 13.4 us
    all_to_all x2, blocking collectives: 60.6 us -> 55.7 us  [exchange(): lax.all_to_all(array, tuple(sizes), 0, 0, tiled=True, axis_index_groups=g...]
    pallas_call x5 -> x4, Pallas kernels: 6.29 us -> 7.87 us  [the longest x1 3.73 us: per_device(): call(onto_kernel, [SMEM] + [VMEM] * 9, [VMEM] * 4, [state_shape] + [inner...]
    ppermute x1, starting transfers between devices: 7.74 us -> 6.21 us  [per_device(): theirs = lax.ppermute(onto, 'c', swap)]
    ppermute x3, waiting for transfers between devices: 2.12 us -> 3.57 us  [onward(): return lax.ppermute(array, ('c', axis), pairs)]
  transfers between devices with their start and end apart: 5 -> 5, of which waited for: 3 -> 4; matrix products, arithmetic and copies ran while one was open for 0% -> 0% of each run, Pallas kernels for 6% -> 4%
where the time goes in v8:
time: 85.3 us; the launch traced here: 85 us
  blocking collectives  55.7 us (65%)
  starting transfers between devices  13.4 us (16%)
  Pallas kernels  10.6 us (12%)
  waiting for transfers between devices  4.63 us (5%)
    all_to_all x2, blocking collectives, exchange(): lax.all_to_all(array, tuple(sizes), 0, 0, tiled=True, axis_index_groups=g...  55.7 us
    ppermute x1, starting transfers between devices, per_device(): theirs = lax.ppermute(onto, 'c', swap)  6.21 us
    ppermute x3, starting transfers between devices, onward(): return lax.ppermute(array, ('c', axis), pairs)  3.88 us
    pallas_call x1, Pallas kernels, per_device(): call(onto_kernel, [SMEM] + [VMEM] * 9, [VMEM] * 4, [state_shape] + [inner...  3.73 us
    ppermute x3, waiting for transfers between devices, onward(): return lax.ppermute(array, ('c', axis), pairs)  3.57 us
    ppermute x1, starting transfers between devices, per_device(): received = lax.ppermute(send, 'c', swap)  3.32 us
    pallas_call x2, Pallas kernels, outputs(): call(functools.partial(outputs_kernel, scale, whose), [SMEM] + [VMEM] * (...  2.62 us
    pallas_call x1, Pallas kernels, per_device(): call(keep_kernel, [SMEM] + [HBM] * 4, [VMEM] * 5, [state_shape] + [token_...  2.11 us
  transfers between devices with their start and end apart: 5, of which 4 were waited for; matrix products, arithmetic and copies ran while one was open for 0% of the time, Pallas kernels for 4%

profile of v8, /device:TPU:1, one launch (start us, length us, event | category | flops | bytes accessed | tf_op | source)
XLA Modules:
  0.0 85.0 jit_solution(15631067502727345629)
XLA Ops:
  0.6 1.9 %shard_map.68 = f32[2048,128]{1,0:T(8,128)S(1)} custom-call(s32[1]{0:T(128)} %bitcast.core.places, bf16[128,2048]{1,0:T(8,128)(2,1)} %query.3, bf16[128,2048]{1,0:T(8,128)(2,1)} %key.3, bf16[128,2048]{1,0:T(8,128)(2,1)} %value.3, bf16[128,2048]{1,0:T(8,128)(2,1)} %gradient.3), custom_call_target="tpu_custom_call" | custom-call | flops 67108864 | bytes 2097152 | tf_op jit(solution)/shard_map/pallas_call | solution.py:224
  2.6 3.3 %collective-permute-start = (f32[2048,128]{1,0:T(8,128)S(1)}, f32[2048,128]{1,0:T(8,128)S(1)}, u32[]{:S(2)}, u32[]{:S(2)}) collective-permute-start(f32[2048,128]{1,0:T(8,128)S(1)} %shard_map.68), channel_id=1, source_target_pairs={{0,4},{4,0},{1,5},{5,1},{2,6},{6,2},{3,7},{7,3},{8,12},{12,8},{9,1... | collective-permute-start | bytes 3145736 | tf_op jit(solution)/shard_map/ppermute | solution.py:233
  5.9 2.1 %shard_map.67 = (f32[2048,128]{1,0:T(8,128)S(1)}, bf16[128,2048]{1,0:T(8,128)(2,1)S(1)}, bf16[128,2048]{1,0:T(8,128)(2,1)S(1)}, bf16[128,2048]{1,0:T(8,128)(2,1)S(1)}, bf16[128,2048]{1,0:T(8,128)(2,1)S(1)}) custom-call(s32[1]{0:T(128)} %bitcast.core.places, bf16[128,2048]{1,0:T(8,128)(2,1)} %query.3, bf16[128,2048]{1,0:T(8,128)(2,1)} %key.3, ...), custom_call_target="tpu_custom_call" | custom-call | flops 67108864 | bytes 5242880 | tf_op jit(solution)/shard_map/pallas_call | solution.py:234
  8.0 0.2 collective-permute-done.received
  8.2 0.1 shard_map.69
  8.3 28.3 %all_to_all.10.parts = f32[32,64,128]{2,1,0:T(8,128)S(1)} all-to-all(f32[32,64,128]{2,1,0:T(8,128)S(1)} %bitcast.5), channel_id=1, replica_groups={{248,184,120,56,240,176,112,48,232,168,104,40,224,160,96,32,216,152,88,..., dimensions={0} | all-to-all | bytes 2097152 | tf_op jit(solution)/shard_map/all_to_all | solution.py:198
  36.6 0.1 shard_map.70
  36.6 1.3 %collective-permute-start.3 = (f32[64,128]{1,0:T(8,128)S(1)}, f32[64,128]{1,0:T(8,128)S(1)}, u32[]{:S(2)}, u32[]{:S(2)}) collective-permute-start(f32[64,128]{1,0:T(8,128)S(1)} %shard_map.70), channel_id=1, source_target_pairs={{0,3},{7,4},{8,11},{15,12},{16,19},{23,20},{24,27},{31,28},{32,35}... | collective-permute-start | bytes 98312 | tf_op jit(solution)/shard_map/ppermute | solution.py:206
  37.9 1.3 %collective-permute-start.2 = (f32[64,128]{1,0:T(8,128)S(1)}, f32[64,128]{1,0:T(8,128)S(1)}, u32[]{:S(2)}, u32[]{:S(2)}) collective-permute-start(f32[64,128]{1,0:T(8,128)S(1)} %shard_map.70), channel_id=1, source_target_pairs={{0,2},{1,3},{6,4},{7,5},{8,10},{9,11},{14,12},{15,13},{16,18},{17,... | collective-permute-start | bytes 98312 | tf_op jit(solution)/shard_map/ppermute | solution.py:206
  39.2 1.3 %collective-permute-start.1 = (f32[64,128]{1,0:T(8,128)S(1)}, f32[64,128]{1,0:T(8,128)S(1)}, u32[]{:S(2)}, u32[]{:S(2)}) collective-permute-start(f32[64,128]{1,0:T(8,128)S(1)} %shard_map.70), channel_id=1, source_target_pairs={{0,1},{1,2},{2,3},{5,4},{6,5},{7,6},{8,9},{9,10},{10,11},{13,12},{... | collective-permute-start | bytes 98312 | tf_op jit(solution)/shard_map/ppermute | solution.py:206
  40.5 2.3 %collective-permute-done.3.refs_2_ = f32[64,128]{1,0:T(8,128)S(1)} collective-permute-done((f32[64,128]{1,0:T(8,128)S(1)}, f32[64,128]{1,0:T(8,128)S(1)}, u32[]{:S(2)}, u32[]{:S(2)}) %collective-permute-start.3) | collective-permute-done | bytes 32800 | tf_op jit(solution)/shard_map/ppermute | solution.py:206
  42.8 1.3 %collective-permute-done.2.refs_1_ = f32[64,128]{1,0:T(8,128)S(1)} collective-permute-done((f32[64,128]{1,0:T(8,128)S(1)}, f32[64,128]{1,0:T(8,128)S(1)}, u32[]{:S(2)}, u32[]{:S(2)}) %collective-permute-start.2) | collective-permute-done | bytes 32800 | tf_op jit(solution)/shard_map/ppermute | solution.py:206
  44.1 0.0 collective-permute-done.1.refs_0_
  44.1 0.1 shard_map.71
  44.2 27.4 %all_to_all.11 = f32[32,64,128]{2,1,0:T(8,128)S(1)} all-to-all(f32[32,64,128]{2,1,0:T(8,128)S(1)} %shard_map.71), channel_id=1, replica_groups={{248,184,120,56,240,176,112,48,232,168,104,40,224,160,96,32,216,152,88,..., dimensions={0} | all-to-all | bytes 2097152 | tf_op jit(solution)/shard_map/all_to_all | solution.py:198
  71.6 3.7 %shard_map.72 = (f32[2048,128]{1,0:T(8,128)S(1)}, f32[128,2048]{1,0:T(8,128)S(1)}, f32[128,2048]{1,0:T(8,128)S(1)}, f32[128,2048]{1,0:T(8,128)S(1)}) custom-call(s32[1]{0:T(128)} %bitcast.core.places, f32[2048,128]{1,0:T(8,128)S(1)} %bitcast.3, f32[2048,128]{1,0:T(8,128)S(1)} %get-tuple-element.26.keep, ...), custom_call_target="tpu_custom_call", output_to_operand_aliasing={{1}: (7, {}), {2}: (8, {}), {3}: (9, {})} | custom-call | flops 335544320 | bytes 8388608 | tf_op jit(solution)/shard_map/pallas_call | solution.py:271
  75.3 6.2 %collective-permute-start.4 = (f32[2048,128]{1,0:T(8,128)S(1)}, f32[2048,128]{1,0:T(8,128)S(1)}, u32[]{:S(2)}, u32[]{:S(2)}) collective-permute-start(f32[2048,128]{1,0:T(8,128)S(1)} %get-tuple-element.35), channel_id=1, source_target_pairs={{0,4},{4,0},{1,5},{5,1},{2,6},{6,2},{3,7},{7,3},{8,12},{12,8},{9,1... | collective-permute-start | bytes 3145736 | tf_op jit(solution)/shard_map/ppermute | solution.py:280
  81.5 1.4 %shard_map.73 = (bf16[128,2048]{1,0:T(8,128)(2,1)}, bf16[128,2048]{1,0:T(8,128)(2,1)}, bf16[128,2048]{1,0:T(8,128)(2,1)}) custom-call(s32[1]{0:T(128)} %bitcast.core.places, bf16[128,2048]{1,0:T(8,128)(2,1)S(1)} %get-tuple-element.21.refs_0_.query, bf16[128,2048]{1,0:T(8,128)(2,1)S(1)} %get-tuple-element.22.refs_1_.key, ...), custom_call_target="tpu_custom_call" | custom-call | flops 100663296 | bytes 5767168 | tf_op jit(solution)/shard_map/pallas_call | solution.py:283
  82.9 0.9 %collective-permute-done.4.refs_3_ = f32[2048,128]{1,0:T(8,128)S(1)} collective-permute-done((f32[2048,128]{1,0:T(8,128)S(1)}, f32[2048,128]{1,0:T(8,128)S(1)}, u32[]{:S(2)}, u32[]{:S(2)}) %collective-permute-start.4) | collective-permute-done | bytes 1048608 | tf_op jit(solution)/shard_map/ppermute | solution.py:280
  83.8 1.2 %shard_map.74 = (bf16[128,2048]{1,0:T(8,128)(2,1)}, bf16[128,2048]{1,0:T(8,128)(2,1)}, bf16[128,2048]{1,0:T(8,128)(2,1)}) custom-call(s32[1]{0:T(128)} %bitcast.core.places, bf16[128,2048]{1,0:T(8,128)(2,1)S(1)} %get-tuple-element.21.refs_0_.query, ...), custom_call_target="tpu_custom_call", output_to_operand_aliasing={{0}: (9, {}), {1}: (10, {}), {2}: (11, {})} | custom-call | flops 100663296 | bytes 5767168 | tf_op jit(solution)/shard_map/pallas_call | solution.py:283
Async XLA Ops:
  2.6 5.6 %collective-permute-start = (f32[2048,128]{1,0:T(8,128)S(1)}, f32[2048,128]{1,0:T(8,128)S(1)}, u32[]{:S(2)}, u32[]{:S(2)}) collective-permute-start(f32[2048,128]{1,0:T(8,128)S(1)} %shard_map.68), channel_id=1, source_target_pairs={{0,4},{4,0},{1,5},{5,1},{2,6},{6,2},{3,7},{7,3},{8,12},{12,8},{9,1... | collective-permute-start | bytes 3145736 | tf_op jit(solution)/shard_map/ppermute | solution.py:233
  36.6 6.2 %collective-permute-start.3 = (f32[64,128]{1,0:T(8,128)S(1)}, f32[64,128]{1,0:T(8,128)S(1)}, u32[]{:S(2)}, u32[]{:S(2)}) collective-permute-start(f32[64,128]{1,0:T(8,128)S(1)} %shard_map.70), channel_id=1, source_target_pairs={{0,3},{7,4},{8,11},{15,12},{16,19},{23,20},{24,27},{31,28},{32,35}... | collective-permute-start | bytes 98312 | tf_op jit(solution)/shard_map/ppermute | solution.py:206
  37.9 6.2 %collective-permute-start.2 = (f32[64,128]{1,0:T(8,128)S(1)}, f32[64,128]{1,0:T(8,128)S(1)}, u32[]{:S(2)}, u32[]{:S(2)}) collective-permute-start(f32[64,128]{1,0:T(8,128)S(1)} %shard_map.70), channel_id=1, source_target_pairs={{0,2},{1,3},{6,4},{7,5},{8,10},{9,11},{14,12},{15,13},{16,18},{17,... | collective-permute-start | bytes 98312 | tf_op jit(solution)/shard_map/ppermute | solution.py:206
  39.2 4.9 %collective-permute-start.1 = (f32[64,128]{1,0:T(8,128)S(1)}, f32[64,128]{1,0:T(8,128)S(1)}, u32[]{:S(2)}, u32[]{:S(2)}) collective-permute-start(f32[64,128]{1,0:T(8,128)S(1)} %shard_map.70), channel_id=1, source_target_pairs={{0,1},{1,2},{2,3},{5,4},{6,5},{7,6},{8,9},{9,10},{10,11},{13,12},{... | collective-permute-start | bytes 98312 | tf_op jit(solution)/shard_map/ppermute | solution.py:206
  75.3 8.5 %collective-permute-start.4 = (f32[2048,128]{1,0:T(8,128)S(1)}, f32[2048,128]{1,0:T(8,128)S(1)}, u32[]{:S(2)}, u32[]{:S(2)}) collective-permute-start(f32[2048,128]{1,0:T(8,128)S(1)} %get-tuple-element.35), channel_id=1, source_target_pairs={{0,4},{4,0},{1,5},{5,1},{2,6},{6,2},{3,7},{7,3},{8,12},{12,8},{9,1... | collective-permute-start | bytes 3145736 | tf_op jit(solution)/shard_map/ppermute | solution.py:280

commit v9 on v8

--- a/solution.py
+++ b/solution.py
@@ -9,7 +9,7 @@
 from jax.sharding import PartitionSpec as P
 
 HEAD = 128
-LOADS = 4
+LOADS = 2
 ROWS = ("x", "y", "z", "c")
 SMEM = pl.BlockSpec(memory_space=pltpu.SMEM)
 VMEM = pl.BlockSpec(memory_space=pltpu.VMEM)
@@ -51,24 +51,24 @@
 
 
 def send_kernel(core, query, key, value, gradient, send, left, right, sems):
-    @pl.when(core[0] == 0)
+    @pl.when(lax.rem(core[0], 2) == 0)
     def _():
         states(((query, left), (gradient, right)), sems, send)
 
-    @pl.when(core[0] != 0)
+    @pl.when(lax.rem(core[0], 2) != 0)
     def _():
         states(((key, left), (value, right)), sems, send)
 
 
 def keep_kernel(core, query, key, value, gradient, keep, q, k, v, g, sems, more):
-    @pl.when(core[0] == 0)
+    @pl.when(lax.rem(core[0], 2) == 0)
     def _():
         rest = load(((query, q), (gradient, g)), more)
         states(((key, k), (value, v)), sems, keep)
         for copy in rest:
             copy.wait()
 
-    @pl.when(core[0] != 0)
+    @pl.when(lax.rem(core[0], 2) != 0)
     def _():
         rest = load(((key, k), (value, v)), more)
         states(((query, q), (gradient, g)), sems, keep)
@@ -92,7 +92,7 @@
 
 
 def merge_kernel(core, keep, received, *refs):
-    @pl.when(core[0] == 0)
+    @pl.when(lax.rem(core[0], 2) == 0)
     def _():
         inner_products(*refs[:4], *refs[5:])
 
@@ -100,7 +100,7 @@
 
 
 def onto_kernel(core, own, keep, *refs):
-    @pl.when(core[0] != 0)
+    @pl.when(lax.rem(core[0], 2) != 0)
     def _():
         inner_products(*refs[:4], *refs[8:])
 
@@ -115,12 +115,14 @@
 
 
 def scan_kernel(order, places, parts, *refs):
-    first = places[0] == 0
+    first = lax.rem(places[0], 2) == 0
     count = parts.shape[0]
     out = refs[-1]
-    total = refs[0][...]
-    for plane in refs[1:-1]:
-        total = total + plane[...]
+    spot = lax.div(places[0], 2)
+    spot = jnp.where(first, spot, len(refs) - 1 - spot)
+    total = jnp.zeros(out.shape[1:], F32)
+    for step, plane in enumerate(refs[:-1], 1):
+        total = total + jnp.where(spot >= step, plane[...], 0.0)
     for n in range(count):
         place = jnp.where(first, order[n], order[count - 1 - n])
         out[place] = total
@@ -159,11 +161,11 @@
         for copy in copies:
             copy.wait()
 
-    @pl.when(places[0] == whose)
+    @pl.when(lax.rem(places[0], 2) == whose)
     def _():
         produce((0,))
 
-    @pl.when(places[0] != whose)
+    @pl.when(lax.rem(places[0], 2) != whose)
     def _():
         produce((1, 2))
 
@@ -184,7 +186,7 @@
 def order_of(sizes):
     rows, depths = sizes["y"], sizes["z"]
     last = rows * depths - 1
-    return [last - (n % depths * rows + n // depths) for n in range(last + 1)]
+    return [17 * (last - (n % depths * rows + n // depths)) % (last + 1) for n in range(last + 1)]
 
 
 def exchange(sizes, array):
@@ -201,15 +203,16 @@
 
 
 def onward(array, axis, count, step):
-    pairs = [(i, i + step) for i in range(count - step)]
-    pairs += [(count + i, count + i - step) for i in range(step, count)]
+    pairs = [(i, (i + step) % count) for i in range(count)]
+    pairs += [(count + i, count + (i - step) % count) for i in range(count)]
     return lax.ppermute(array, ("c", axis), pairs)
 
 
 def per_device(sizes, scale, queries, key_row_matrix, value_row_matrix, output_gradient):
     tokens, width = queries.shape
     members = sizes["y"] * sizes["z"]
-    places = lax.axis_index("c").astype(jnp.int32).reshape(1)
+    places = lax.axis_index("c") + 2 * lax.axis_index("x")
+    places = places.astype(jnp.int32).reshape(1)
     swap = [(0, 1), (1, 0)]
     product = 2 * width * tokens * HEAD
     token_bytes = 2 * tokens * width

time: 85.3 us -> 83.2 us (0.975)
  waiting for transfers between devices: 4.63 us -> 2.9 us
    ppermute x3, waiting for transfers between devices: 3.57 us -> 1.61 us  [onward(): return lax.ppermute(array, ('c', axis), pairs)]
    ppermute x3, starting transfers between devices: 3.88 us -> 4.9 us  [onward(): return lax.ppermute(array, ('c', axis), pairs)]
where the time goes in v9:
time: 83.2 us; the launch traced here: 83 us
  blocking collectives  55.4 us (67%)
  starting transfers between devices  13.9 us (17%)
  Pallas kernels  10.1 us (12%)
  waiting for transfers between devices  2.9 us (3%)
    all_to_all x2, blocking collectives, exchange(): lax.all_to_all(array, tuple(sizes), 0, 0, tiled=True, axis_index_groups=g...  55.4 us
    ppermute x1, starting transfers between devices, per_device(): theirs = lax.ppermute(onto, 'c', swap)  5.72 us
    ppermute x3, starting transfers between devices, onward(): return lax.ppermute(array, ('c', axis), pairs)  4.9 us
    pallas_call x1, Pallas kernels, per_device(): call(onto_kernel, [SMEM] + [VMEM] * 9, [VMEM] * 4, [state_shape] + [inner...  3.73 us
    ppermute x1, starting transfers between devices, per_device(): received = lax.ppermute(send, 'c', swap)  3.32 us
    pallas_call x2, Pallas kernels, outputs(): call(functools.partial(outputs_kernel, scale, whose), [SMEM] + [VMEM] * (...  2.66 us
    pallas_call x1, Pallas kernels, per_device(): call(keep_kernel, [SMEM] + [HBM] * 4, [VMEM] * 5, [state_shape] + [token_...  1.84 us
  transfers between devices with their start and end apart: 5, of which 4 were waited for; matrix products, arithmetic and copies ran while one was open for 0% of the time, Pallas kernels for 4%

profile of v9, /device:TPU:1, one launch (start us, length us, event | category | flops | bytes accessed | tf_op | source)
XLA Modules:
  0.0 83.0 jit_solution(6784023142752388419)
XLA Ops:
  0.6 1.6 %shard_map.68 = f32[2048,128]{1,0:T(8,128)S(1)} custom-call(s32[1]{0:T(128)} %bitcast.core.places, bf16[128,2048]{1,0:T(8,128)(2,1)} %query.3, bf16[128,2048]{1,0:T(8,128)(2,1)} %key.3, bf16[128,2048]{1,0:T(8,128)(2,1)} %value.3, bf16[128,2048]{1,0:T(8,128)(2,1)} %gradient.3), custom_call_target="tpu_custom_call" | custom-call | flops 67108864 | bytes 2097152 | tf_op jit(solution)/shard_map/pallas_call | solution.py:227
  2.3 3.3 %collective-permute-start = (f32[2048,128]{1,0:T(8,128)S(1)}, f32[2048,128]{1,0:T(8,128)S(1)}, u32[]{:S(2)}, u32[]{:S(2)}) collective-permute-start(f32[2048,128]{1,0:T(8,128)S(1)} %shard_map.68), channel_id=1, source_target_pairs={{0,4},{4,0},{1,5},{5,1},{2,6},{6,2},{3,7},{7,3},{8,12},{12,8},{9,1... | collective-permute-start | bytes 3145736 | tf_op jit(solution)/shard_map/ppermute | solution.py:236
  5.6 1.8 %shard_map.67 = (f32[2048,128]{1,0:T(8,128)S(1)}, bf16[128,2048]{1,0:T(8,128)(2,1)S(1)}, bf16[128,2048]{1,0:T(8,128)(2,1)S(1)}, bf16[128,2048]{1,0:T(8,128)(2,1)S(1)}, bf16[128,2048]{1,0:T(8,128)(2,1)S(1)}) custom-call(s32[1]{0:T(128)} %bitcast.core.places, bf16[128,2048]{1,0:T(8,128)(2,1)} %query.3, bf16[128,2048]{1,0:T(8,128)(2,1)} %key.3, ...), custom_call_target="tpu_custom_call" | custom-call | flops 67108864 | bytes 5242880 | tf_op jit(solution)/shard_map/pallas_call | solution.py:237
  7.4 0.4 collective-permute-done.received
  7.9 0.1 shard_map.69
  8.0 28.6 %all_to_all.10.parts = f32[32,64,128]{2,1,0:T(8,128)S(1)} all-to-all(f32[32,64,128]{2,1,0:T(8,128)S(1)} %bitcast.5), channel_id=1, replica_groups={{248,152,120,24,240,144,112,16,232,136,104,8,224,128,96,0,216,184,88,56..., dimensions={0} | all-to-all | bytes 2097152 | tf_op jit(solution)/shard_map/all_to_all | solution.py:200
  36.6 0.1 shard_map.70
  36.6 1.3 %collective-permute-start.3 = (f32[64,128]{1,0:T(8,128)S(1)}, f32[64,128]{1,0:T(8,128)S(1)}, u32[]{:S(2)}, u32[]{:S(2)}) collective-permute-start(f32[64,128]{1,0:T(8,128)S(1)} %shard_map.70), channel_id=1, source_target_pairs={{0,3},{1,0},{2,1},{3,2},{4,5},{5,6},{6,7},{7,4},{8,11},{9,8},{10,9... | collective-permute-start | bytes 98312 | tf_op jit(solution)/shard_map/ppermute | solution.py:208
  37.9 2.5 %collective-permute-start.2 = (f32[64,128]{1,0:T(8,128)S(1)}, f32[64,128]{1,0:T(8,128)S(1)}, u32[]{:S(2)}, u32[]{:S(2)}) collective-permute-start(f32[64,128]{1,0:T(8,128)S(1)} %shard_map.70), channel_id=1, source_target_pairs={{0,2},{1,3},{2,0},{3,1},{4,6},{5,7},{6,4},{7,5},{8,10},{9,11},{10,... | collective-permute-start | bytes 98312 | tf_op jit(solution)/shard_map/ppermute | solution.py:208
  40.4 1.2 %collective-permute-start.1 = (f32[64,128]{1,0:T(8,128)S(1)}, f32[64,128]{1,0:T(8,128)S(1)}, u32[]{:S(2)}, u32[]{:S(2)}) collective-permute-start(f32[64,128]{1,0:T(8,128)S(1)} %shard_map.70), channel_id=1, source_target_pairs={{0,1},{1,2},{2,3},{3,0},{4,7},{5,4},{6,5},{7,6},{8,9},{9,10},{10,1... | collective-permute-start | bytes 98312 | tf_op jit(solution)/shard_map/ppermute | solution.py:208
  41.5 0.0 collective-permute-done.3.refs_2_
  41.5 0.8 collective-permute-done.2.refs_1_
  42.3 0.8 %collective-permute-done.1.refs_0_ = f32[64,128]{1,0:T(8,128)S(1)} collective-permute-done((f32[64,128]{1,0:T(8,128)S(1)}, f32[64,128]{1,0:T(8,128)S(1)}, u32[]{:S(2)}, u32[]{:S(2)}) %collective-permute-start.1) | collective-permute-done | bytes 32800 | tf_op jit(solution)/shard_map/ppermute | solution.py:208
  43.1 0.1 shard_map.71
  43.2 26.8 %all_to_all.11 = f32[32,64,128]{2,1,0:T(8,128)S(1)} all-to-all(f32[32,64,128]{2,1,0:T(8,128)S(1)} %shard_map.71), channel_id=1, replica_groups={{248,152,120,24,240,144,112,16,232,136,104,8,224,128,96,0,216,184,88,56..., dimensions={0} | all-to-all | bytes 2097152 | tf_op jit(solution)/shard_map/all_to_all | solution.py:200
  70.0 3.7 %shard_map.72 = (f32[2048,128]{1,0:T(8,128)S(1)}, f32[128,2048]{1,0:T(8,128)S(1)}, f32[128,2048]{1,0:T(8,128)S(1)}, f32[128,2048]{1,0:T(8,128)S(1)}) custom-call(s32[1]{0:T(128)} %bitcast.core.places, f32[2048,128]{1,0:T(8,128)S(1)} %bitcast.3, f32[2048,128]{1,0:T(8,128)S(1)} %get-tuple-element.26.keep, ...), custom_call_target="tpu_custom_call", output_to_operand_aliasing={{1}: (7, {}), {2}: (8, {}), {3}: (9, {})} | custom-call | flops 335544320 | bytes 8388608 | tf_op jit(solution)/shard_map/pallas_call | solution.py:274
  73.8 5.7 %collective-permute-start.4 = (f32[2048,128]{1,0:T(8,128)S(1)}, f32[2048,128]{1,0:T(8,128)S(1)}, u32[]{:S(2)}, u32[]{:S(2)}) collective-permute-start(f32[2048,128]{1,0:T(8,128)S(1)} %get-tuple-element.35), channel_id=1, source_target_pairs={{0,4},{4,0},{1,5},{5,1},{2,6},{6,2},{3,7},{7,3},{8,12},{12,8},{9,1... | collective-permute-start | bytes 3145736 | tf_op jit(solution)/shard_map/ppermute | solution.py:283
  79.5 1.4 %shard_map.73 = (bf16[128,2048]{1,0:T(8,128)(2,1)}, bf16[128,2048]{1,0:T(8,128)(2,1)}, bf16[128,2048]{1,0:T(8,128)(2,1)}) custom-call(s32[1]{0:T(128)} %bitcast.core.places, bf16[128,2048]{1,0:T(8,128)(2,1)S(1)} %get-tuple-element.21.refs_0_.query, bf16[128,2048]{1,0:T(8,128)(2,1)S(1)} %get-tuple-element.22.refs_1_.key, ...), custom_call_target="tpu_custom_call" | custom-call | flops 100663296 | bytes 5767168 | tf_op jit(solution)/shard_map/pallas_call | solution.py:286
  80.9 0.9 %collective-permute-done.4.refs_3_ = f32[2048,128]{1,0:T(8,128)S(1)} collective-permute-done((f32[2048,128]{1,0:T(8,128)S(1)}, f32[2048,128]{1,0:T(8,128)S(1)}, u32[]{:S(2)}, u32[]{:S(2)}) %collective-permute-start.4) | collective-permute-done | bytes 1048608 | tf_op jit(solution)/shard_map/ppermute | solution.py:283
  81.8 1.2 %shard_map.74 = (bf16[128,2048]{1,0:T(8,128)(2,1)}, bf16[128,2048]{1,0:T(8,128)(2,1)}, bf16[128,2048]{1,0:T(8,128)(2,1)}) custom-call(s32[1]{0:T(128)} %bitcast.core.places, bf16[128,2048]{1,0:T(8,128)(2,1)S(1)} %get-tuple-element.21.refs_0_.query, ...), custom_call_target="tpu_custom_call", output_to_operand_aliasing={{0}: (9, {}), {1}: (10, {}), {2}: (11, {})} | custom-call | flops 100663296 | bytes 5767168 | tf_op jit(solution)/shard_map/pallas_call | solution.py:286
Async XLA Ops:
  2.3 5.6 %collective-permute-start = (f32[2048,128]{1,0:T(8,128)S(1)}, f32[2048,128]{1,0:T(8,128)S(1)}, u32[]{:S(2)}, u32[]{:S(2)}) collective-permute-start(f32[2048,128]{1,0:T(8,128)S(1)} %shard_map.68), channel_id=1, source_target_pairs={{0,4},{4,0},{1,5},{5,1},{2,6},{6,2},{3,7},{7,3},{8,12},{12,8},{9,1... | collective-permute-start | bytes 3145736 | tf_op jit(solution)/shard_map/ppermute | solution.py:236
  36.6 4.9 %collective-permute-start.3 = (f32[64,128]{1,0:T(8,128)S(1)}, f32[64,128]{1,0:T(8,128)S(1)}, u32[]{:S(2)}, u32[]{:S(2)}) collective-permute-start(f32[64,128]{1,0:T(8,128)S(1)} %shard_map.70), channel_id=1, source_target_pairs={{0,3},{1,0},{2,1},{3,2},{4,5},{5,6},{6,7},{7,4},{8,11},{9,8},{10,9... | collective-permute-start | bytes 98312 | tf_op jit(solution)/shard_map/ppermute | solution.py:208
  37.9 4.4 %collective-permute-start.2 = (f32[64,128]{1,0:T(8,128)S(1)}, f32[64,128]{1,0:T(8,128)S(1)}, u32[]{:S(2)}, u32[]{:S(2)}) collective-permute-start(f32[64,128]{1,0:T(8,128)S(1)} %shard_map.70), channel_id=1, source_target_pairs={{0,2},{1,3},{2,0},{3,1},{4,6},{5,7},{6,4},{7,5},{8,10},{9,11},{10,... | collective-permute-start | bytes 98312 | tf_op jit(solution)/shard_map/ppermute | solution.py:208
  40.4 2.8 %collective-permute-start.1 = (f32[64,128]{1,0:T(8,128)S(1)}, f32[64,128]{1,0:T(8,128)S(1)}, u32[]{:S(2)}, u32[]{:S(2)}) collective-permute-start(f32[64,128]{1,0:T(8,128)S(1)} %shard_map.70), channel_id=1, source_target_pairs={{0,1},{1,2},{2,3},{3,0},{4,7},{5,4},{6,5},{7,6},{8,9},{9,10},{10,1... | collective-permute-start | bytes 98312 | tf_op jit(solution)/shard_map/ppermute | solution.py:208
  73.8 8.0 %collective-permute-start.4 = (f32[2048,128]{1,0:T(8,128)S(1)}, f32[2048,128]{1,0:T(8,128)S(1)}, u32[]{:S(2)}, u32[]{:S(2)}) collective-permute-start(f32[2048,128]{1,0:T(8,128)S(1)} %get-tuple-element.35), channel_id=1, source_target_pairs={{0,4},{4,0},{1,5},{5,1},{2,6},{6,2},{3,7},{7,3},{8,12},{12,8},{9,1... | collective-permute-start | bytes 3145736 | tf_op jit(solution)/shard_map/ppermute | solution.py:283

commit v10 on v9

--- a/solution.py
+++ b/solution.py
@@ -61,13 +61,6 @@
 
 
 def keep_kernel(core, query, key, value, gradient, keep, q, k, v, g, sems, more):
-    @pl.when(lax.rem(core[0], 2) == 0)
-    def _():
-        rest = load(((query, q), (gradient, g)), more)
-        states(((key, k), (value, v)), sems, keep)
-        for copy in rest:
-            copy.wait()
-
     @pl.when(lax.rem(core[0], 2) != 0)
     def _():
         rest = load(((key, k), (value, v)), more)
@@ -91,12 +84,22 @@
         gv[:, lanes] = contract(qk, g, 0, 0)
 
 
-def merge_kernel(core, keep, received, *refs):
+def merge_kernel(core, query, key, value, gradient, received, *refs):
+    keep, q, k, v, g, chip = refs[5:11]
+    inner, sems, more = refs[11:14], refs[14], refs[15]
+
     @pl.when(lax.rem(core[0], 2) == 0)
     def _():
-        inner_products(*refs[:4], *refs[5:])
-
-    refs[4][...] = keep[...] + received[...]
+        rest = load(((query, q), (gradient, g)), more)
+        states(((key, k), (value, v)), sems, keep)
+        for copy in rest:
+            copy.wait()
+        inner_products(q, k, v, g, *inner)
+        chip[...] = keep[...] + received[...]
+
+    @pl.when(lax.rem(core[0], 2) != 0)
+    def _():
+        chip[...] = refs[0][...] + received[...]
 
 
 def onto_kernel(core, own, keep, *refs):
@@ -244,14 +247,17 @@
         [pltpu.SemaphoreType.DMA((2, LOADS))] * 2,
     )(places, *resting)
     received, keep = lax.optimization_barrier((received, keep))
-    chip, *inner = call(
+    keep, *rest = call(
         merge_kernel,
-        [SMEM] + [VMEM] * 6,
-        [VMEM] * 4,
-        [state_shape] + [inner_shape] * 3,
-        5 * product,
-        10 * token_bytes + 3 * state_bytes,
-    )(places, keep, received, *inputs)
+        [SMEM] + [HBM] * 4 + [VMEM] * 6,
+        [VMEM] * 9,
+        [state_shape] + [token_shape] * 4 + [state_shape] + [inner_shape] * 3,
+        6 * product,
+        14 * token_bytes + 3 * state_bytes,
+        [pltpu.SemaphoreType.DMA((2, LOADS))] * 2,
+        {6 + n: n for n in range(5)},
+    )(places, *resting, received, keep, *inputs)
+    inputs, chip, inner = rest[:4], rest[4], rest[5:]
     parts = exchange(sizes, chip.reshape(parts_shape.shape))
     plane = call(
         total_kernel,

time: 83.2 us -> 81.4 us (0.978)
  blocking collectives: 55.4 us -> 51.6 us
  starting transfers between devices: 13.9 us -> 15.5 us
    all_to_all x2, blocking collectives: 55.4 us -> 51.6 us  [exchange(): lax.all_to_all(array, tuple(sizes), 0, 0, tiled=True, axis_index_groups=g...]
    ppermute x1, starting transfers between devices: 5.72 us -> 7.33 us  [per_device(): theirs = lax.ppermute(onto, 'c', swap)]
where the time goes in v10:
time: 81.4 us; the launch traced here: 81.2 us
  blocking collectives  51.6 us (63%)
  starting transfers between devices  15.5 us (19%)
  Pallas kernels  10.2 us (13%)
  waiting for transfers between devices  3.19 us (4%)
    all_to_all x2, blocking collectives, exchange(): lax.all_to_all(array, tuple(sizes), 0, 0, tiled=True, axis_index_groups=g...  51.6 us
    ppermute x1, starting transfers between devices, per_device(): theirs = lax.ppermute(onto, 'c', swap)  7.33 us
    ppermute x3, starting transfers between devices, onward(): return lax.ppermute(array, ('c', axis), pairs)  4.9 us
    pallas_call x1, Pallas kernels, per_device(): call(onto_kernel, [SMEM] + [VMEM] * 9, [VMEM] * 4, [state_shape] + [inner...  3.73 us
    ppermute x1, starting transfers between devices, per_device(): received = lax.ppermute(send, 'c', swap)  3.32 us
    pallas_call x2, Pallas kernels, outputs(): call(functools.partial(outputs_kernel, scale, whose), [SMEM] + [VMEM] * (...  2.66 us
    ppermute x3, waiting for transfers between devices, onward(): return lax.ppermute(array, ('c', axis), pairs)  1.9 us
    pallas_call x1, Pallas kernels, per_device(): call(keep_kernel, [SMEM] + [HBM] * 4, [VMEM] * 5, [state_shape] + [token_...  1.84 us
  transfers between devices with their start and end apart: 5, of which 4 were waited for; matrix products, arithmetic and copies ran while one was open for 0% of the time, Pallas kernels for 4%

profile of v10, /device:TPU:1, one launch (start us, length us, event | category | flops | bytes accessed | tf_op | source)
XLA Modules:
  0.0 81.2 jit_solution(9272192694626858948)
XLA Ops:
  0.6 1.6 %shard_map.67 = f32[2048,128]{1,0:T(8,128)S(1)} custom-call(s32[1]{0:T(128)} %bitcast.core.places, bf16[128,2048]{1,0:T(8,128)(2,1)} %query.5, bf16[128,2048]{1,0:T(8,128)(2,1)} %key.5, bf16[128,2048]{1,0:T(8,128)(2,1)} %value.5, bf16[128,2048]{1,0:T(8,128)(2,1)} %gradient.5), custom_call_target="tpu_custom_call" | custom-call | flops 67108864 | bytes 2097152 | tf_op jit(solution)/shard_map/pallas_call | solution.py:230
  2.3 3.3 %collective-permute-start = (f32[2048,128]{1,0:T(8,128)S(1)}, f32[2048,128]{1,0:T(8,128)S(1)}, u32[]{:S(2)}, u32[]{:S(2)}) collective-permute-start(f32[2048,128]{1,0:T(8,128)S(1)} %shard_map.67), channel_id=1, source_target_pairs={{0,4},{4,0},{1,5},{5,1},{2,6},{6,2},{3,7},{7,3},{8,12},{12,8},{9,1... | collective-permute-start | bytes 3145736 | tf_op jit(solution)/shard_map/ppermute | solution.py:239
  5.6 1.8 %shard_map.68 = (f32[2048,128]{1,0:T(8,128)S(1)}, bf16[128,2048]{1,0:T(8,128)(2,1)S(1)}, bf16[128,2048]{1,0:T(8,128)(2,1)S(1)}, bf16[128,2048]{1,0:T(8,128)(2,1)S(1)}, bf16[128,2048]{1,0:T(8,128)(2,1)S(1)}) custom-call(s32[1]{0:T(128)} %bitcast.core.places, bf16[128,2048]{1,0:T(8,128)(2,1)} %query.5, bf16[128,2048]{1,0:T(8,128)(2,1)} %key.5, ...), custom_call_target="tpu_custom_call" | custom-call | flops 67108864 | bytes 5242880 | tf_op jit(solution)/shard_map/pallas_call | solution.py:240
  7.4 0.4 collective-permute-done.received
  7.9 0.2 shard_map.69
  8.0 26.9 %all_to_all.10.parts = f32[32,64,128]{2,1,0:T(8,128)S(1)} all-to-all(f32[32,64,128]{2,1,0:T(8,128)S(1)} %bitcast.5), channel_id=1, replica_groups={{248,152,120,24,240,144,112,16,232,136,104,8,224,128,96,0,216,184,88,56..., dimensions={0} | all-to-all | bytes 2097152 | tf_op jit(solution)/shard_map/all_to_all | solution.py:203
  34.9 0.1 shard_map.70
  35.0 1.3 %collective-permute-start.3 = (f32[64,128]{1,0:T(8,128)S(1)}, f32[64,128]{1,0:T(8,128)S(1)}, u32[]{:S(2)}, u32[]{:S(2)}) collective-permute-start(f32[64,128]{1,0:T(8,128)S(1)} %shard_map.70), channel_id=1, source_target_pairs={{0,3},{1,0},{2,1},{3,2},{4,5},{5,6},{6,7},{7,4},{8,11},{9,8},{10,9... | collective-permute-start | bytes 98312 | tf_op jit(solution)/shard_map/ppermute | solution.py:211
  36.3 2.5 %collective-permute-start.2 = (f32[64,128]{1,0:T(8,128)S(1)}, f32[64,128]{1,0:T(8,128)S(1)}, u32[]{:S(2)}, u32[]{:S(2)}) collective-permute-start(f32[64,128]{1,0:T(8,128)S(1)} %shard_map.70), channel_id=1, source_target_pairs={{0,2},{1,3},{2,0},{3,1},{4,6},{5,7},{6,4},{7,5},{8,10},{9,11},{10,... | collective-permute-start | bytes 98312 | tf_op jit(solution)/shard_map/ppermute | solution.py:211
  38.7 1.2 %collective-permute-start.1 = (f32[64,128]{1,0:T(8,128)S(1)}, f32[64,128]{1,0:T(8,128)S(1)}, u32[]{:S(2)}, u32[]{:S(2)}) collective-permute-start(f32[64,128]{1,0:T(8,128)S(1)} %shard_map.70), channel_id=1, source_target_pairs={{0,1},{1,2},{2,3},{3,0},{4,7},{5,4},{6,5},{7,6},{8,9},{9,10},{10,1... | collective-permute-start | bytes 98312 | tf_op jit(solution)/shard_map/ppermute | solution.py:211
  39.9 0.0 collective-permute-done.3.refs_2_
  39.9 0.9 %collective-permute-done.2.refs_1_ = f32[64,128]{1,0:T(8,128)S(1)} collective-permute-done((f32[64,128]{1,0:T(8,128)S(1)}, f32[64,128]{1,0:T(8,128)S(1)}, u32[]{:S(2)}, u32[]{:S(2)}) %collective-permute-start.2) | collective-permute-done | bytes 32800 | tf_op jit(solution)/shard_map/ppermute | solution.py:211
  40.8 0.9 %collective-permute-done.1.refs_0_ = f32[64,128]{1,0:T(8,128)S(1)} collective-permute-done((f32[64,128]{1,0:T(8,128)S(1)}, f32[64,128]{1,0:T(8,128)S(1)}, u32[]{:S(2)}, u32[]{:S(2)}) %collective-permute-start.1) | collective-permute-done | bytes 32800 | tf_op jit(solution)/shard_map/ppermute | solution.py:211
  41.8 0.1 shard_map.71
  41.9 24.7 %all_to_all.11 = f32[32,64,128]{2,1,0:T(8,128)S(1)} all-to-all(f32[32,64,128]{2,1,0:T(8,128)S(1)} %shard_map.71), channel_id=1, replica_groups={{248,152,120,24,240,144,112,16,232,136,104,8,224,128,96,0,216,184,88,56..., dimensions={0} | all-to-all | bytes 2097152 | tf_op jit(solution)/shard_map/all_to_all | solution.py:203
  66.6 3.7 %shard_map.72 = (f32[2048,128]{1,0:T(8,128)S(1)}, f32[128,2048]{1,0:T(8,128)S(1)}, f32[128,2048]{1,0:T(8,128)S(1)}, f32[128,2048]{1,0:T(8,128)S(1)}) custom-call(s32[1]{0:T(128)} %bitcast.core.places, f32[2048,128]{1,0:T(8,128)S(1)} %bitcast.3, f32[2048,128]{1,0:T(8,128)S(1)} %get-tuple-element.38.keep, ...), custom_call_target="tpu_custom_call", output_to_operand_aliasing={{1}: (7, {}), {2}: (8, {}), {3}: (9, {})} | custom-call | flops 335544320 | bytes 8388608 | tf_op jit(solution)/shard_map/pallas_call | solution.py:280
  70.3 7.3 %collective-permute-start.4 = (f32[2048,128]{1,0:T(8,128)S(1)}, f32[2048,128]{1,0:T(8,128)S(1)}, u32[]{:S(2)}, u32[]{:S(2)}) collective-permute-start(f32[2048,128]{1,0:T(8,128)S(1)} %get-tuple-element.45), channel_id=1, source_target_pairs={{0,4},{4,0},{1,5},{5,1},{2,6},{6,2},{3,7},{7,3},{8,12},{12,8},{9,1... | collective-permute-start | bytes 3145736 | tf_op jit(solution)/shard_map/ppermute | solution.py:289
  77.6 1.4 %shard_map.73 = (bf16[128,2048]{1,0:T(8,128)(2,1)}, bf16[128,2048]{1,0:T(8,128)(2,1)}, bf16[128,2048]{1,0:T(8,128)(2,1)}) custom-call(s32[1]{0:T(128)} %bitcast.core.places, bf16[128,2048]{1,0:T(8,128)(2,1)S(1)} %get-tuple-element.33.refs_0_.query, bf16[128,2048]{1,0:T(8,128)(2,1)S(1)} %get-tuple-element.34.refs_1_.key, ...), custom_call_target="tpu_custom_call" | custom-call | flops 100663296 | bytes 5767168 | tf_op jit(solution)/shard_map/pallas_call | solution.py:292
  79.1 0.9 %collective-permute-done.4.refs_3_ = f32[2048,128]{1,0:T(8,128)S(1)} collective-permute-done((f32[2048,128]{1,0:T(8,128)S(1)}, f32[2048,128]{1,0:T(8,128)S(1)}, u32[]{:S(2)}, u32[]{:S(2)}) %collective-permute-start.4) | collective-permute-done | bytes 1048608 | tf_op jit(solution)/shard_map/ppermute | solution.py:289
  79.9 1.2 %shard_map.74 = (bf16[128,2048]{1,0:T(8,128)(2,1)}, bf16[128,2048]{1,0:T(8,128)(2,1)}, bf16[128,2048]{1,0:T(8,128)(2,1)}) custom-call(s32[1]{0:T(128)} %bitcast.core.places, bf16[128,2048]{1,0:T(8,128)(2,1)S(1)} %get-tuple-element.33.refs_0_.query, ...), custom_call_target="tpu_custom_call", output_to_operand_aliasing={{0}: (9, {}), {1}: (10, {}), {2}: (11, {})} | custom-call | flops 100663296 | bytes 5767168 | tf_op jit(solution)/shard_map/pallas_call | solution.py:292
Async XLA Ops:
  2.3 5.6 %collective-permute-start = (f32[2048,128]{1,0:T(8,128)S(1)}, f32[2048,128]{1,0:T(8,128)S(1)}, u32[]{:S(2)}, u32[]{:S(2)}) collective-permute-start(f32[2048,128]{1,0:T(8,128)S(1)} %shard_map.67), channel_id=1, source_target_pairs={{0,4},{4,0},{1,5},{5,1},{2,6},{6,2},{3,7},{7,3},{8,12},{12,8},{9,1... | collective-permute-start | bytes 3145736 | tf_op jit(solution)/shard_map/ppermute | solution.py:239
  35.0 4.9 %collective-permute-start.3 = (f32[64,128]{1,0:T(8,128)S(1)}, f32[64,128]{1,0:T(8,128)S(1)}, u32[]{:S(2)}, u32[]{:S(2)}) collective-permute-start(f32[64,128]{1,0:T(8,128)S(1)} %shard_map.70), channel_id=1, source_target_pairs={{0,3},{1,0},{2,1},{3,2},{4,5},{5,6},{6,7},{7,4},{8,11},{9,8},{10,9... | collective-permute-start | bytes 98312 | tf_op jit(solution)/shard_map/ppermute | solution.py:211
  36.3 4.6 %collective-permute-start.2 = (f32[64,128]{1,0:T(8,128)S(1)}, f32[64,128]{1,0:T(8,128)S(1)}, u32[]{:S(2)}, u32[]{:S(2)}) collective-permute-start(f32[64,128]{1,0:T(8,128)S(1)} %shard_map.70), channel_id=1, source_target_pairs={{0,2},{1,3},{2,0},{3,1},{4,6},{5,7},{6,4},{7,5},{8,10},{9,11},{10,... | collective-permute-start | bytes 98312 | tf_op jit(solution)/shard_map/ppermute | solution.py:211
  38.7 3.1 %collective-permute-start.1 = (f32[64,128]{1,0:T(8,128)S(1)}, f32[64,128]{1,0:T(8,128)S(1)}, u32[]{:S(2)}, u32[]{:S(2)}) collective-permute-start(f32[64,128]{1,0:T(8,128)S(1)} %shard_map.70), channel_id=1, source_target_pairs={{0,1},{1,2},{2,3},{3,0},{4,7},{5,4},{6,5},{7,6},{8,9},{9,10},{10,1... | collective-permute-start | bytes 98312 | tf_op jit(solution)/shard_map/ppermute | solution.py:211
  70.3 9.6 %collective-permute-start.4 = (f32[2048,128]{1,0:T(8,128)S(1)}, f32[2048,128]{1,0:T(8,128)S(1)}, u32[]{:S(2)}, u32[]{:S(2)}) collective-permute-start(f32[2048,128]{1,0:T(8,128)S(1)} %get-tuple-element.45), channel_id=1, source_target_pairs={{0,4},{4,0},{1,5},{5,1},{2,6},{6,2},{3,7},{7,3},{8,12},{12,8},{9,1... | collective-permute-start | bytes 3145736 | tf_op jit(solution)/shard_map/ppermute | solution.py:289

commit v11 on v10

--- a/solution.py
+++ b/solution.py
@@ -10,6 +10,7 @@
 
 HEAD = 128
 LOADS = 2
+STORES = 4
 ROWS = ("x", "y", "z", "c")
 SMEM = pl.BlockSpec(memory_space=pltpu.SMEM)
 VMEM = pl.BlockSpec(memory_space=pltpu.VMEM)
@@ -57,7 +58,7 @@
 
     @pl.when(lax.rem(core[0], 2) != 0)
     def _():
-        states(((key, left), (value, right)), sems, send)
+        states(((value, left), (key, right)), sems, send)
 
 
 def keep_kernel(core, query, key, value, gradient, keep, q, k, v, g, sems, more):
@@ -91,7 +92,7 @@
     @pl.when(lax.rem(core[0], 2) == 0)
     def _():
         rest = load(((query, q), (gradient, g)), more)
-        states(((key, k), (value, v)), sems, keep)
+        states(((value, v), (key, k)), sems, keep)
         for copy in rest:
             copy.wait()
         inner_products(q, k, v, g, *inner)
@@ -151,7 +152,7 @@
                 lanes = pl.ds(at, HEAD)
                 summed = state(lanes)
                 for t in tensors:
-                    source, dim = ((gradient, 1), (value, 1), (key, 0))[t]
+                    source, dim = ((gradient, 0), (value, 1), (key, 0))[t]
                     result = contract(source[:, lanes], summed, 1, dim)
                     result = result + inner[t][:, lanes]
                     held[t, n, :, pl.ds(h * HEAD, HEAD)] = (scale * result).astype(BF16)
@@ -297,8 +298,8 @@
             3 * product // 2,
             7 * token_bytes + 2 * state_bytes,
             [
-                pltpu.VMEM((3, LOADS, tokens, width // LOADS), BF16),
-                pltpu.SemaphoreType.DMA((3, LOADS)),
+                pltpu.VMEM((3, STORES, tokens, width // STORES), BF16),
+                pltpu.SemaphoreType.DMA((3, STORES)),
             ],
             {8 + len(states) + n: n for n in range(len(results))},
         )(places, *inputs, *inner, *states, *results)

time: 81.4 us -> 81.2 us (level)
  no operation moved by 1% of the time
where the time goes in v11:
time: 81.2 us; the launch traced here: 81 us
  blocking collectives  51.6 us (64%)
  starting transfers between devices  15.5 us (19%)
  Pallas kernels  9.96 us (12%)
  waiting for transfers between devices  3.24 us (4%)
    all_to_all x2, blocking collectives, exchange(): lax.all_to_all(array, tuple(sizes), 0, 0, tiled=True, axis_index_groups=g...  51.6 us
    ppermute x1, starting transfers between devices, per_device(): theirs = lax.ppermute(onto, 'c', swap)  7.33 us
    ppermute x3, starting transfers between devices, onward(): return lax.ppermute(array, ('c', axis), pairs)  4.9 us
    pallas_call x1, Pallas kernels, per_device(): call(onto_kernel, [SMEM] + [VMEM] * 9, [VMEM] * 4, [state_shape] + [inner...  3.73 us
    ppermute x1, starting transfers between devices, per_device(): received = lax.ppermute(send, 'c', swap)  3.32 us
    pallas_call x2, Pallas kernels, outputs(): call(functools.partial(outputs_kernel, scale, whose), [SMEM] + [VMEM] * (...  2.46 us
    ppermute x3, waiting for transfers between devices, onward(): return lax.ppermute(array, ('c', axis), pairs)  1.9 us
    pallas_call x1, Pallas kernels, per_device(): call(keep_kernel, [SMEM] + [HBM] * 4, [VMEM] * 5, [state_shape] + [token_...  1.84 us
  transfers between devices with their start and end apart: 5, of which 4 were waited for; matrix products, arithmetic and copies ran while one was open for 0% of the time, Pallas kernels for 4%

profile of v11, /device:TPU:1, one launch (start us, length us, event | category | flops | bytes accessed | tf_op | source)
XLA Modules:
  0.0 81.0 jit_solution(1321535607619937923)
XLA Ops:
  0.6 1.6 %shard_map.67 = f32[2048,128]{1,0:T(8,128)S(1)} custom-call(s32[1]{0:T(128)} %bitcast.core.places, bf16[128,2048]{1,0:T(8,128)(2,1)} %query.5, bf16[128,2048]{1,0:T(8,128)(2,1)} %key.5, bf16[128,2048]{1,0:T(8,128)(2,1)} %value.5, bf16[128,2048]{1,0:T(8,128)(2,1)} %gradient.5), custom_call_target="tpu_custom_call" | custom-call | flops 67108864 | bytes 2097152 | tf_op jit(solution)/shard_map/pallas_call | solution.py:231
  2.3 3.3 %collective-permute-start = (f32[2048,128]{1,0:T(8,128)S(1)}, f32[2048,128]{1,0:T(8,128)S(1)}, u32[]{:S(2)}, u32[]{:S(2)}) collective-permute-start(f32[2048,128]{1,0:T(8,128)S(1)} %shard_map.67), channel_id=1, source_target_pairs={{0,4},{4,0},{1,5},{5,1},{2,6},{6,2},{3,7},{7,3},{8,12},{12,8},{9,1... | collective-permute-start | bytes 3145736 | tf_op jit(solution)/shard_map/ppermute | solution.py:240
  5.6 1.8 %shard_map.68 = (f32[2048,128]{1,0:T(8,128)S(1)}, bf16[128,2048]{1,0:T(8,128)(2,1)S(1)}, bf16[128,2048]{1,0:T(8,128)(2,1)S(1)}, bf16[128,2048]{1,0:T(8,128)(2,1)S(1)}, bf16[128,2048]{1,0:T(8,128)(2,1)S(1)}) custom-call(s32[1]{0:T(128)} %bitcast.core.places, bf16[128,2048]{1,0:T(8,128)(2,1)} %query.5, bf16[128,2048]{1,0:T(8,128)(2,1)} %key.5, ...), custom_call_target="tpu_custom_call" | custom-call | flops 67108864 | bytes 5242880 | tf_op jit(solution)/shard_map/pallas_call | solution.py:241
  7.4 0.4 collective-permute-done.received
  7.9 0.2 shard_map.69
  8.0 26.9 %all_to_all.10.parts = f32[32,64,128]{2,1,0:T(8,128)S(1)} all-to-all(f32[32,64,128]{2,1,0:T(8,128)S(1)} %bitcast.5), channel_id=1, replica_groups={{248,152,120,24,240,144,112,16,232,136,104,8,224,128,96,0,216,184,88,56..., dimensions={0} | all-to-all | bytes 2097152 | tf_op jit(solution)/shard_map/all_to_all | solution.py:204
  34.9 0.1 shard_map.70
  35.0 1.3 %collective-permute-start.3 = (f32[64,128]{1,0:T(8,128)S(1)}, f32[64,128]{1,0:T(8,128)S(1)}, u32[]{:S(2)}, u32[]{:S(2)}) collective-permute-start(f32[64,128]{1,0:T(8,128)S(1)} %shard_map.70), channel_id=1, source_target_pairs={{0,3},{1,0},{2,1},{3,2},{4,5},{5,6},{6,7},{7,4},{8,11},{9,8},{10,9... | collective-permute-start | bytes 98312 | tf_op jit(solution)/shard_map/ppermute | solution.py:212
  36.3 2.5 %collective-permute-start.2 = (f32[64,128]{1,0:T(8,128)S(1)}, f32[64,128]{1,0:T(8,128)S(1)}, u32[]{:S(2)}, u32[]{:S(2)}) collective-permute-start(f32[64,128]{1,0:T(8,128)S(1)} %shard_map.70), channel_id=1, source_target_pairs={{0,2},{1,3},{2,0},{3,1},{4,6},{5,7},{6,4},{7,5},{8,10},{9,11},{10,... | collective-permute-start | bytes 98312 | tf_op jit(solution)/shard_map/ppermute | solution.py:212
  38.7 1.2 %collective-permute-start.1 = (f32[64,128]{1,0:T(8,128)S(1)}, f32[64,128]{1,0:T(8,128)S(1)}, u32[]{:S(2)}, u32[]{:S(2)}) collective-permute-start(f32[64,128]{1,0:T(8,128)S(1)} %shard_map.70), channel_id=1, source_target_pairs={{0,1},{1,2},{2,3},{3,0},{4,7},{5,4},{6,5},{7,6},{8,9},{9,10},{10,1... | collective-permute-start | bytes 98312 | tf_op jit(solution)/shard_map/ppermute | solution.py:212
  39.9 0.0 collective-permute-done.3.refs_2_
  39.9 0.9 %collective-permute-done.2.refs_1_ = f32[64,128]{1,0:T(8,128)S(1)} collective-permute-done((f32[64,128]{1,0:T(8,128)S(1)}, f32[64,128]{1,0:T(8,128)S(1)}, u32[]{:S(2)}, u32[]{:S(2)}) %collective-permute-start.2) | collective-permute-done | bytes 32800 | tf_op jit(solution)/shard_map/ppermute | solution.py:212
  40.8 0.9 %collective-permute-done.1.refs_0_ = f32[64,128]{1,0:T(8,128)S(1)} collective-permute-done((f32[64,128]{1,0:T(8,128)S(1)}, f32[64,128]{1,0:T(8,128)S(1)}, u32[]{:S(2)}, u32[]{:S(2)}) %collective-permute-start.1) | collective-permute-done | bytes 32800 | tf_op jit(solution)/shard_map/ppermute | solution.py:212
  41.8 0.1 shard_map.71
  41.9 24.7 %all_to_all.11 = f32[32,64,128]{2,1,0:T(8,128)S(1)} all-to-all(f32[32,64,128]{2,1,0:T(8,128)S(1)} %shard_map.71), channel_id=1, replica_groups={{248,152,120,24,240,144,112,16,232,136,104,8,224,128,96,0,216,184,88,56..., dimensions={0} | all-to-all | bytes 2097152 | tf_op jit(solution)/shard_map/all_to_all | solution.py:204
  66.6 3.7 %shard_map.72 = (f32[2048,128]{1,0:T(8,128)S(1)}, f32[128,2048]{1,0:T(8,128)S(1)}, f32[128,2048]{1,0:T(8,128)S(1)}, f32[128,2048]{1,0:T(8,128)S(1)}) custom-call(s32[1]{0:T(128)} %bitcast.core.places, f32[2048,128]{1,0:T(8,128)S(1)} %bitcast.3, f32[2048,128]{1,0:T(8,128)S(1)} %get-tuple-element.38.keep, ...), custom_call_target="tpu_custom_call", output_to_operand_aliasing={{1}: (7, {}), {2}: (8, {}), {3}: (9, {})} | custom-call | flops 335544320 | bytes 8388608 | tf_op jit(solution)/shard_map/pallas_call | solution.py:281
  70.3 7.3 %collective-permute-start.4 = (f32[2048,128]{1,0:T(8,128)S(1)}, f32[2048,128]{1,0:T(8,128)S(1)}, u32[]{:S(2)}, u32[]{:S(2)}) collective-permute-start(f32[2048,128]{1,0:T(8,128)S(1)} %get-tuple-element.45), channel_id=1, source_target_pairs={{0,4},{4,0},{1,5},{5,1},{2,6},{6,2},{3,7},{7,3},{8,12},{12,8},{9,1... | collective-permute-start | bytes 3145736 | tf_op jit(solution)/shard_map/ppermute | solution.py:290
  77.6 1.4 %shard_map.73 = (bf16[128,2048]{1,0:T(8,128)(2,1)}, bf16[128,2048]{1,0:T(8,128)(2,1)}, bf16[128,2048]{1,0:T(8,128)(2,1)}) custom-call(s32[1]{0:T(128)} %bitcast.core.places, bf16[128,2048]{1,0:T(8,128)(2,1)S(1)} %get-tuple-element.33.refs_0_.query, bf16[128,2048]{1,0:T(8,128)(2,1)S(1)} %get-tuple-element.34.refs_1_.key, ...), custom_call_target="tpu_custom_call" | custom-call | flops 100663296 | bytes 5767168 | tf_op jit(solution)/shard_map/pallas_call | solution.py:293
  79.0 0.9 %collective-permute-done.4.refs_3_ = f32[2048,128]{1,0:T(8,128)S(1)} collective-permute-done((f32[2048,128]{1,0:T(8,128)S(1)}, f32[2048,128]{1,0:T(8,128)S(1)}, u32[]{:S(2)}, u32[]{:S(2)}) %collective-permute-start.4) | collective-permute-done | bytes 1048608 | tf_op jit(solution)/shard_map/ppermute | solution.py:290
  79.9 1.1 %shard_map.74 = (bf16[128,2048]{1,0:T(8,128)(2,1)}, bf16[128,2048]{1,0:T(8,128)(2,1)}, bf16[128,2048]{1,0:T(8,128)(2,1)}) custom-call(s32[1]{0:T(128)} %bitcast.core.places, bf16[128,2048]{1,0:T(8,128)(2,1)S(1)} %get-tuple-element.33.refs_0_.query, ...), custom_call_target="tpu_custom_call", output_to_operand_aliasing={{0}: (9, {}), {1}: (10, {}), {2}: (11, {})} | custom-call | flops 100663296 | bytes 5767168 | tf_op jit(solution)/shard_map/pallas_call | solution.py:293
Async XLA Ops:
  2.3 5.6 %collective-permute-start = (f32[2048,128]{1,0:T(8,128)S(1)}, f32[2048,128]{1,0:T(8,128)S(1)}, u32[]{:S(2)}, u32[]{:S(2)}) collective-permute-start(f32[2048,128]{1,0:T(8,128)S(1)} %shard_map.67), channel_id=1, source_target_pairs={{0,4},{4,0},{1,5},{5,1},{2,6},{6,2},{3,7},{7,3},{8,12},{12,8},{9,1... | collective-permute-start | bytes 3145736 | tf_op jit(solution)/shard_map/ppermute | solution.py:240
  35.0 4.9 %collective-permute-start.3 = (f32[64,128]{1,0:T(8,128)S(1)}, f32[64,128]{1,0:T(8,128)S(1)}, u32[]{:S(2)}, u32[]{:S(2)}) collective-permute-start(f32[64,128]{1,0:T(8,128)S(1)} %shard_map.70), channel_id=1, source_target_pairs={{0,3},{1,0},{2,1},{3,2},{4,5},{5,6},{6,7},{7,4},{8,11},{9,8},{10,9... | collective-permute-start | bytes 98312 | tf_op jit(solution)/shard_map/ppermute | solution.py:212
  36.3 4.6 %collective-permute-start.2 = (f32[64,128]{1,0:T(8,128)S(1)}, f32[64,128]{1,0:T(8,128)S(1)}, u32[]{:S(2)}, u32[]{:S(2)}) collective-permute-start(f32[64,128]{1,0:T(8,128)S(1)} %shard_map.70), channel_id=1, source_target_pairs={{0,2},{1,3},{2,0},{3,1},{4,6},{5,7},{6,4},{7,5},{8,10},{9,11},{10,... | collective-permute-start | bytes 98312 | tf_op jit(solution)/shard_map/ppermute | solution.py:212
  38.7 3.1 %collective-permute-start.1 = (f32[64,128]{1,0:T(8,128)S(1)}, f32[64,128]{1,0:T(8,128)S(1)}, u32[]{:S(2)}, u32[]{:S(2)}) collective-permute-start(f32[64,128]{1,0:T(8,128)S(1)} %shard_map.70), channel_id=1, source_target_pairs={{0,1},{1,2},{2,3},{3,0},{4,7},{5,4},{6,5},{7,6},{8,9},{9,10},{10,1... | collective-permute-start | bytes 98312 | tf_op jit(solution)/shard_map/ppermute | solution.py:212
  70.3 9.6 %collective-permute-start.4 = (f32[2048,128]{1,0:T(8,128)S(1)}, f32[2048,128]{1,0:T(8,128)S(1)}, u32[]{:S(2)}, u32[]{:S(2)}) collective-permute-start(f32[2048,128]{1,0:T(8,128)S(1)} %get-tuple-element.45), channel_id=1, source_target_pairs={{0,4},{4,0},{1,5},{5,1},{2,6},{6,2},{3,7},{7,3},{8,12},{12,8},{9,1... | collective-permute-start | bytes 3145736 | tf_op jit(solution)/shard_map/ppermute | solution.py:290

commit v12 on v11

--- a/solution.py
+++ b/solution.py
@@ -9,7 +9,7 @@
 from jax.sharding import PartitionSpec as P
 
 HEAD = 128
-LOADS = 2
+LOADS = 1
 STORES = 4
 ROWS = ("x", "y", "z", "c")
 SMEM = pl.BlockSpec(memory_space=pltpu.SMEM)

time: 81.2 us -> 81 us (level)
  no operation moved by 1% of the time
where the time goes in v12:
time: 81 us; the launch traced here: 80.8 us
  blocking collectives  51 us (63%)
  starting transfers between devices  16 us (20%)
  Pallas kernels  9.96 us (12%)
  waiting for transfers between devices  3.16 us (4%)
    all_to_all x2, blocking collectives, exchange(): lax.all_to_all(array, tuple(sizes), 0, 0, tiled=True, axis_index_groups=g...  51 us
    ppermute x1, starting transfers between devices, per_device(): theirs = lax.ppermute(onto, 'c', swap)  7.75 us
    ppermute x3, starting transfers between devices, onward(): return lax.ppermute(array, ('c', axis), pairs)  4.92 us
    pallas_call x1, Pallas kernels, per_device(): call(onto_kernel, [SMEM] + [VMEM] * 9, [VMEM] * 4, [state_shape] + [inner...  3.73 us
    ppermute x1, starting transfers between devices, per_device(): received = lax.ppermute(send, 'c', swap)  3.32 us
    pallas_call x2, Pallas kernels, outputs(): call(functools.partial(outputs_kernel, scale, whose), [SMEM] + [VMEM] * (...  2.46 us
    pallas_call x1, Pallas kernels, per_device(): call(keep_kernel, [SMEM] + [HBM] * 4, [VMEM] * 5, [state_shape] + [token_...  1.9 us
    ppermute x3, waiting for transfers between devices, onward(): return lax.ppermute(array, ('c', axis), pairs)  1.88 us
  transfers between devices with their start and end apart: 5, of which 4 were waited for; matrix products, arithmetic and copies ran while one was open for 0% of the time, Pallas kernels for 4%

profile of v12, /device:TPU:1, one launch (start us, length us, event | category | flops | bytes accessed | tf_op | source)
XLA Modules:
  0.0 80.8 jit_solution(922539834649165216)
XLA Ops:
  0.6 1.6 %shard_map.67 = f32[2048,128]{1,0:T(8,128)S(1)} custom-call(s32[1]{0:T(128)} %bitcast.core.places, bf16[128,2048]{1,0:T(8,128)(2,1)} %query.5, bf16[128,2048]{1,0:T(8,128)(2,1)} %key.5, bf16[128,2048]{1,0:T(8,128)(2,1)} %value.5, bf16[128,2048]{1,0:T(8,128)(2,1)} %gradient.5), custom_call_target="tpu_custom_call" | custom-call | flops 67108864 | bytes 2097152 | tf_op jit(solution)/shard_map/pallas_call | solution.py:231
  2.2 3.3 %collective-permute-start = (f32[2048,128]{1,0:T(8,128)S(1)}, f32[2048,128]{1,0:T(8,128)S(1)}, u32[]{:S(2)}, u32[]{:S(2)}) collective-permute-start(f32[2048,128]{1,0:T(8,128)S(1)} %shard_map.67), channel_id=1, source_target_pairs={{0,4},{4,0},{1,5},{5,1},{2,6},{6,2},{3,7},{7,3},{8,12},{12,8},{9,1... | collective-permute-start | bytes 3145736 | tf_op jit(solution)/shard_map/ppermute | solution.py:240
  5.5 1.9 %shard_map.68 = (f32[2048,128]{1,0:T(8,128)S(1)}, bf16[128,2048]{1,0:T(8,128)(2,1)S(1)}, bf16[128,2048]{1,0:T(8,128)(2,1)S(1)}, bf16[128,2048]{1,0:T(8,128)(2,1)S(1)}, bf16[128,2048]{1,0:T(8,128)(2,1)S(1)}) custom-call(s32[1]{0:T(128)} %bitcast.core.places, bf16[128,2048]{1,0:T(8,128)(2,1)} %query.5, bf16[128,2048]{1,0:T(8,128)(2,1)} %key.5, ...), custom_call_target="tpu_custom_call" | custom-call | flops 67108864 | bytes 5242880 | tf_op jit(solution)/shard_map/pallas_call | solution.py:241
  7.4 0.4 collective-permute-done.received
  7.8 0.1 shard_map.69
  8.0 26.8 %all_to_all.10.parts = f32[32,64,128]{2,1,0:T(8,128)S(1)} all-to-all(f32[32,64,128]{2,1,0:T(8,128)S(1)} %bitcast.5), channel_id=1, replica_groups={{248,152,120,24,240,144,112,16,232,136,104,8,224,128,96,0,216,184,88,56..., dimensions={0} | all-to-all | bytes 2097152 | tf_op jit(solution)/shard_map/all_to_all | solution.py:204
  34.8 0.1 shard_map.70
  34.8 1.3 %collective-permute-start.3 = (f32[64,128]{1,0:T(8,128)S(1)}, f32[64,128]{1,0:T(8,128)S(1)}, u32[]{:S(2)}, u32[]{:S(2)}) collective-permute-start(f32[64,128]{1,0:T(8,128)S(1)} %shard_map.70), channel_id=1, source_target_pairs={{0,3},{1,0},{2,1},{3,2},{4,5},{5,6},{6,7},{7,4},{8,11},{9,8},{10,9... | collective-permute-start | bytes 98312 | tf_op jit(solution)/shard_map/ppermute | solution.py:212
  36.1 2.4 %collective-permute-start.2 = (f32[64,128]{1,0:T(8,128)S(1)}, f32[64,128]{1,0:T(8,128)S(1)}, u32[]{:S(2)}, u32[]{:S(2)}) collective-permute-start(f32[64,128]{1,0:T(8,128)S(1)} %shard_map.70), channel_id=1, source_target_pairs={{0,2},{1,3},{2,0},{3,1},{4,6},{5,7},{6,4},{7,5},{8,10},{9,11},{10,... | collective-permute-start | bytes 98312 | tf_op jit(solution)/shard_map/ppermute | solution.py:212
  38.6 1.2 %collective-permute-start.1 = (f32[64,128]{1,0:T(8,128)S(1)}, f32[64,128]{1,0:T(8,128)S(1)}, u32[]{:S(2)}, u32[]{:S(2)}) collective-permute-start(f32[64,128]{1,0:T(8,128)S(1)} %shard_map.70), channel_id=1, source_target_pairs={{0,1},{1,2},{2,3},{3,0},{4,7},{5,4},{6,5},{7,6},{8,9},{9,10},{10,1... | collective-permute-start | bytes 98312 | tf_op jit(solution)/shard_map/ppermute | solution.py:212
  39.7 0.0 collective-permute-done.3.refs_2_
  39.7 1.0 %collective-permute-done.2.refs_1_ = f32[64,128]{1,0:T(8,128)S(1)} collective-permute-done((f32[64,128]{1,0:T(8,128)S(1)}, f32[64,128]{1,0:T(8,128)S(1)}, u32[]{:S(2)}, u32[]{:S(2)}) %collective-permute-start.2) | collective-permute-done | bytes 32800 | tf_op jit(solution)/shard_map/ppermute | solution.py:212
  40.7 0.9 %collective-permute-done.1.refs_0_ = f32[64,128]{1,0:T(8,128)S(1)} collective-permute-done((f32[64,128]{1,0:T(8,128)S(1)}, f32[64,128]{1,0:T(8,128)S(1)}, u32[]{:S(2)}, u32[]{:S(2)}) %collective-permute-start.1) | collective-permute-done | bytes 32800 | tf_op jit(solution)/shard_map/ppermute | solution.py:212
  41.6 0.1 shard_map.71
  41.7 24.2 %all_to_all.11 = f32[32,64,128]{2,1,0:T(8,128)S(1)} all-to-all(f32[32,64,128]{2,1,0:T(8,128)S(1)} %shard_map.71), channel_id=1, replica_groups={{248,152,120,24,240,144,112,16,232,136,104,8,224,128,96,0,216,184,88,56..., dimensions={0} | all-to-all | bytes 2097152 | tf_op jit(solution)/shard_map/all_to_all | solution.py:204
  65.9 3.7 %shard_map.72 = (f32[2048,128]{1,0:T(8,128)S(1)}, f32[128,2048]{1,0:T(8,128)S(1)}, f32[128,2048]{1,0:T(8,128)S(1)}, f32[128,2048]{1,0:T(8,128)S(1)}) custom-call(s32[1]{0:T(128)} %bitcast.core.places, f32[2048,128]{1,0:T(8,128)S(1)} %bitcast.3, f32[2048,128]{1,0:T(8,128)S(1)} %get-tuple-element.38.keep, ...), custom_call_target="tpu_custom_call", output_to_operand_aliasing={{1}: (7, {}), {2}: (8, {}), {3}: (9, {})} | custom-call | flops 335544320 | bytes 8388608 | tf_op jit(solution)/shard_map/pallas_call | solution.py:281
  69.7 7.7 %collective-permute-start.4 = (f32[2048,128]{1,0:T(8,128)S(1)}, f32[2048,128]{1,0:T(8,128)S(1)}, u32[]{:S(2)}, u32[]{:S(2)}) collective-permute-start(f32[2048,128]{1,0:T(8,128)S(1)} %get-tuple-element.45), channel_id=1, source_target_pairs={{0,4},{4,0},{1,5},{5,1},{2,6},{6,2},{3,7},{7,3},{8,12},{12,8},{9,1... | collective-permute-start | bytes 3145736 | tf_op jit(solution)/shard_map/ppermute | solution.py:290
  77.4 1.4 %shard_map.73 = (bf16[128,2048]{1,0:T(8,128)(2,1)}, bf16[128,2048]{1,0:T(8,128)(2,1)}, bf16[128,2048]{1,0:T(8,128)(2,1)}) custom-call(s32[1]{0:T(128)} %bitcast.core.places, bf16[128,2048]{1,0:T(8,128)(2,1)S(1)} %get-tuple-element.33.refs_0_.query, bf16[128,2048]{1,0:T(8,128)(2,1)S(1)} %get-tuple-element.34.refs_1_.key, ...), custom_call_target="tpu_custom_call" | custom-call | flops 100663296 | bytes 5767168 | tf_op jit(solution)/shard_map/pallas_call | solution.py:293
  78.8 0.9 %collective-permute-done.4.refs_3_ = f32[2048,128]{1,0:T(8,128)S(1)} collective-permute-done((f32[2048,128]{1,0:T(8,128)S(1)}, f32[2048,128]{1,0:T(8,128)S(1)}, u32[]{:S(2)}, u32[]{:S(2)}) %collective-permute-start.4) | collective-permute-done | bytes 1048608 | tf_op jit(solution)/shard_map/ppermute | solution.py:290
  79.7 1.1 %shard_map.74 = (bf16[128,2048]{1,0:T(8,128)(2,1)}, bf16[128,2048]{1,0:T(8,128)(2,1)}, bf16[128,2048]{1,0:T(8,128)(2,1)}) custom-call(s32[1]{0:T(128)} %bitcast.core.places, bf16[128,2048]{1,0:T(8,128)(2,1)S(1)} %get-tuple-element.33.refs_0_.query, ...), custom_call_target="tpu_custom_call", output_to_operand_aliasing={{0}: (9, {}), {1}: (10, {}), {2}: (11, {})} | custom-call | flops 100663296 | bytes 5767168 | tf_op jit(solution)/shard_map/pallas_call | solution.py:293
Async XLA Ops:
  2.2 5.6 %collective-permute-start = (f32[2048,128]{1,0:T(8,128)S(1)}, f32[2048,128]{1,0:T(8,128)S(1)}, u32[]{:S(2)}, u32[]{:S(2)}) collective-permute-start(f32[2048,128]{1,0:T(8,128)S(1)} %shard_map.67), channel_id=1, source_target_pairs={{0,4},{4,0},{1,5},{5,1},{2,6},{6,2},{3,7},{7,3},{8,12},{12,8},{9,1... | collective-permute-start | bytes 3145736 | tf_op jit(solution)/shard_map/ppermute | solution.py:240
  34.8 4.9 %collective-permute-start.3 = (f32[64,128]{1,0:T(8,128)S(1)}, f32[64,128]{1,0:T(8,128)S(1)}, u32[]{:S(2)}, u32[]{:S(2)}) collective-permute-start(f32[64,128]{1,0:T(8,128)S(1)} %shard_map.70), channel_id=1, source_target_pairs={{0,3},{1,0},{2,1},{3,2},{4,5},{5,6},{6,7},{7,4},{8,11},{9,8},{10,9... | collective-permute-start | bytes 98312 | tf_op jit(solution)/shard_map/ppermute | solution.py:212
  36.1 4.6 %collective-permute-start.2 = (f32[64,128]{1,0:T(8,128)S(1)}, f32[64,128]{1,0:T(8,128)S(1)}, u32[]{:S(2)}, u32[]{:S(2)}) collective-permute-start(f32[64,128]{1,0:T(8,128)S(1)} %shard_map.70), channel_id=1, source_target_pairs={{0,2},{1,3},{2,0},{3,1},{4,6},{5,7},{6,4},{7,5},{8,10},{9,11},{10,... | collective-permute-start | bytes 98312 | tf_op jit(solution)/shard_map/ppermute | solution.py:212
  38.6 3.1 %collective-permute-start.1 = (f32[64,128]{1,0:T(8,128)S(1)}, f32[64,128]{1,0:T(8,128)S(1)}, u32[]{:S(2)}, u32[]{:S(2)}) collective-permute-start(f32[64,128]{1,0:T(8,128)S(1)} %shard_map.70), channel_id=1, source_target_pairs={{0,1},{1,2},{2,3},{3,0},{4,7},{5,4},{6,5},{7,6},{8,9},{9,10},{10,1... | collective-permute-start | bytes 98312 | tf_op jit(solution)/shard_map/ppermute | solution.py:212
  69.7 10.0 %collective-permute-start.4 = (f32[2048,128]{1,0:T(8,128)S(1)}, f32[2048,128]{1,0:T(8,128)S(1)}, u32[]{:S(2)}, u32[]{:S(2)}) collective-permute-start(f32[2048,128]{1,0:T(8,128)S(1)} %get-tuple-element.45), channel_id=1, source_target_pairs={{0,4},{4,0},{1,5},{5,1},{2,6},{6,2},{3,7},{7,3},{8,12},{12,8},{9,1... | collective-permute-start | bytes 3145736 | tf_op jit(solution)/shard_map/ppermute | solution.py:290
